TPU v7x, 512 devices: a whole 4x8x8 slice. The times are simulated.
512 devices in a mesh: seq: 64 (over z, x, core), head: 8 (over y).
Axes of the slice: x: 4, y: 8, z: 8, core: 2. Of those that a mesh axis runs over, the one named last changes fastest.
Arguments:
- queries: bfloat16 [2, 8192, 1024], P(None, 'seq', 'head'), may hold values from -13 to 13
- key_vectors: bfloat16 [2, 8192, 1024], P(None, 'seq', 'head'), may hold values from -13 to 13
- value_vectors: bfloat16 [2, 8192, 1024], P(None, 'seq', 'head'), may hold values from -6 to 6
- conv_taps: float32 [33, 16], P(None, 'head'), may hold values from -1 to 1
- out_weight: bfloat16 [1024, 2048], P('head'), may hold values from -0.1875 to 0.1875
- out_grad: bfloat16 [2, 8192, 2048], P(None, 'seq', 'head'), may hold values from -16 to 16
Outputs:
- layer_output: bfloat16 [2, 8192, 2048], P(None, 'seq', 'head')
- query_grad: bfloat16 [2, 8192, 1024], P(None, 'seq', 'head')
- key_grad: bfloat16 [2, 8192, 1024], P(None, 'seq', 'head')
- value_grad: bfloat16 [2, 8192, 1024], P(None, 'seq', 'head')
- weight_grad: float32 [1024, 2048], P('head', 'seq')
All inputs are finite; a program needn't handle non-finite values.
Results may differ from a plain program's by a relative error of at most 0.0049.
Values may be sent and summed in bfloat16 or wider, within the bound.
No kernel may reach another device: no remote copies, remote signals or barrier semaphores. Data moves between devices by JAX's collectives and lax.ppermute only.
A program may use at most 64 MiB of HBM per device.

v0:
```python
import jax
import jax.numpy as jnp
from jax import lax
from jax.sharding import PartitionSpec as P

ITERS = 2
LM_DEV = 2


highest = lax.Precision.HIGHEST


def padded(cells, sides, width):
    for axis, dim in sides:
        count = lax.axis_size(axis)
        ends = count - 1
        head = lax.slice_in_dim(cells, 0, width, axis=dim)
        tail = lax.slice_in_dim(cells, cells.shape[dim] - width, cells.shape[dim], axis=dim)
        cells = jnp.concatenate(
            [
                lax.ppermute(tail, axis, [(i, (i + 1) % count) for i in range(ends)]),
                cells,
                lax.ppermute(head, axis, [((i + 1) % count, i) for i in range(ends)]),
            ],
            axis=dim,
        )
    return cells


def newton_inverse(matrix):
    column_peak = lax.stop_gradient(jnp.max(jnp.sum(matrix, axis=-2), axis=-1))
    approx = jnp.swapaxes(matrix, -1, -2) / column_peak[..., None, None]
    identity = jnp.eye(matrix.shape[-1], dtype=matrix.dtype)
    for iteration in range(ITERS):
        product = jnp.matmul(matrix, approx, precision=highest)
        factor = 7.0 * identity - product
        factor = 15.0 * identity - jnp.matmul(product, factor, precision=highest)
        factor = 13.0 * identity - jnp.matmul(product, factor, precision=highest)
        approx = 0.25 * jnp.matmul(approx, factor, precision=highest)
    return approx


def softmax_back(weights, upstream, score_scale):
    return weights * (upstream - jnp.sum(upstream * weights, axis=-1, keepdims=True)) * score_scale


def shards(queries, key_vectors, value_vectors, conv_taps, out_weight, out_grad):
    documents, tokens, channels = queries.shape
    heads_here = conv_taps.shape[1]
    head_size = channels // heads_here
    segment = tokens // LM_DEV
    landmarks = LM_DEV * lax.axis_size("seq")
    score_scale = head_size ** (-0.5)
    rim_width = conv_taps.shape[0] // 2
    model_width = out_weight.shape[1]
    own_width = model_width // lax.axis_size("head")
    query_flat = queries.astype(jnp.float32)
    key_flat = key_vectors.astype(jnp.float32)
    query_rows = query_flat.reshape(documents, tokens, heads_here, head_size)
    key_rows = key_flat.reshape(documents, tokens, heads_here, head_size)
    value_rows = value_vectors.astype(jnp.float32).reshape(documents, tokens, heads_here, head_size)
    local_query_means = query_flat.reshape(documents, LM_DEV, segment, channels).mean(axis=2)
    local_key_means = key_flat.reshape(documents, LM_DEV, segment, channels).mean(axis=2)
    query_means, key_means = (
        lax.all_gather(local_query_means, "seq", axis=1, tiled=True),
        lax.all_gather(local_key_means, "seq", axis=1, tiled=True),
    )
    query_marks = query_means.reshape(documents, landmarks, heads_here, head_size)
    key_marks = key_means.reshape(documents, landmarks, heads_here, head_size)
    token_weights = jax.nn.softmax(
        jnp.einsum("bnhd,bmhd->bhnm", query_rows, key_marks, precision=highest) * score_scale,
        axis=-1,
    )
    landmark_weights = jax.nn.softmax(
        jnp.einsum("bjhd,bmhd->bhjm", query_marks, key_marks, precision=highest) * score_scale,
        axis=-1,
    )
    key_scores = (
        jnp.einsum("bjhd,bnhd->bhjn", query_marks, key_rows, precision=highest) * score_scale
    )
    local_peak = jnp.max(key_scores, axis=-1)
    key_peak = lax.pmax(local_peak, "seq")
    local_exp = jnp.exp(key_scores - key_peak[..., None])
    key_total, key_summed = lax.psum(
        (
            jnp.sum(local_exp, axis=-1),
            jnp.einsum("bhjn,bnhd->bhjd", local_exp, value_rows, precision=highest),
        ),
        "seq",
    )
    key_weights = jnp.exp(key_scores - key_peak[..., None]) / key_total[..., None]
    mixed_values = key_summed / key_total[..., None]
    inverse, inverse_pullback = jax.vjp(newton_inverse, landmark_weights)
    landmark_mix = jnp.matmul(inverse, mixed_values, precision=highest)
    wide_taps = jnp.repeat(conv_taps, head_size, axis=1)
    padded_values = padded(value_vectors, (("seq", 1),), rim_width).astype(jnp.float32)
    conv_part = wide_taps[0] * padded_values[:, 0:tokens]
    for offset in range(1, wide_taps.shape[0]):
        conv_part = conv_part + wide_taps[offset] * padded_values[:, offset : offset + tokens]
    attended = jnp.einsum("bhnm,bhmd->bnhd", token_weights, landmark_mix, precision=highest)
    context_b = (attended.reshape(documents, tokens, channels) + conv_part).astype(jnp.bfloat16)
    flat_context = context_b.reshape(documents * tokens, channels)
    weight_block = out_weight
    projected = lax.psum_scatter(
        lax.dot_general(
            weight_block, flat_context, (((0,), (1,)), ((), ())), preferred_element_type=jnp.float32
        ),
        "head",
        scatter_dimension=0,
        tiled=True,
    )
    layer_output = projected.T.astype(jnp.bfloat16).reshape(documents, tokens, own_width)
    shard_piece = lax.all_gather(out_grad, "head", axis=2, tiled=True)
    amount = shard_piece.shape[2]
    flat_piece = shard_piece.reshape(-1, amount)
    weight_block = out_weight
    context_part = lax.dot_general(
        flat_piece, weight_block, (((1,), (1,)), ((), ())), preferred_element_type=jnp.float32
    )
    weight_piece = lax.dot_general(
        flat_context, flat_piece, (((0,), (0,)), ((), ())), preferred_element_type=jnp.float32
    )
    context_grad = context_part
    weight_grad = lax.psum_scatter(weight_piece, "seq", scatter_dimension=1, tiled=True)
    context_grad = context_grad.reshape(documents, tokens, channels)
    padded_grad = padded(context_grad, (("seq", 1),), rim_width)
    value_conv = wide_taps[0] * padded_grad[:, 2 * rim_width : 2 * rim_width + tokens]
    for offset in range(1, wide_taps.shape[0]):
        start_row = 2 * rim_width - offset
        value_conv = value_conv + wide_taps[offset] * padded_grad[:, start_row : start_row + tokens]
    grad_heads = context_grad.reshape(documents, tokens, heads_here, head_size)
    token_upstream = jnp.einsum("bnhd,bhmd->bhnm", grad_heads, landmark_mix, precision=highest)
    token_scores_grad = softmax_back(token_weights, token_upstream, score_scale)
    query_direct = jnp.einsum("bhnm,bmhd->bnhd", token_scores_grad, key_marks, precision=highest)
    key_mean_terms = jnp.einsum("bhnm,bnhd->bmhd", token_scores_grad, query_rows, precision=highest)
    mix_terms = jnp.einsum("bhnm,bnhd->bhmd", token_weights, grad_heads, precision=highest)
    position = lax.axis_index("seq") * LM_DEV
    mix_grad = lax.psum(mix_terms, "seq")
    inverse_grad = jnp.einsum("bhmd,bhjd->bhmj", mix_grad, mixed_values, precision=highest)
    mixed_grad = jnp.einsum("bhmj,bhmd->bhjd", inverse, mix_grad, precision=highest)
    landmark_grad = inverse_pullback(inverse_grad)[0]
    landmark_scores_grad = softmax_back(landmark_weights, landmark_grad, score_scale)
    query_mean_direct = jnp.einsum(
        "bhjm,bmhd->bjhd", landmark_scores_grad, key_marks, precision=highest
    )
    key_mean_direct = jnp.einsum(
        "bhjm,bjhd->bmhd", landmark_scores_grad, query_marks, precision=highest
    )
    mixed_dot = jnp.sum(mixed_grad * mixed_values, axis=-1)
    weight_upstream = jnp.einsum("bhjd,bnhd->bhjn", mixed_grad, value_rows, precision=highest)
    key_scores_grad = key_weights * (weight_upstream - mixed_dot[..., None]) * score_scale
    query_mean_terms = jnp.einsum("bhjn,bnhd->bjhd", key_scores_grad, key_rows, precision=highest)
    key_direct = jnp.einsum("bhjn,bjhd->bnhd", key_scores_grad, query_marks, precision=highest)
    value_direct = jnp.einsum("bhjn,bhjd->bnhd", key_weights, mixed_grad, precision=highest)
    query_terms_flat = query_mean_terms.reshape(documents, landmarks, channels)
    query_mean_grad, key_mean_grad = (
        lax.psum_scatter(query_terms_flat, "seq", scatter_dimension=1, tiled=True),
        lax.psum_scatter(
            key_mean_terms.reshape(documents, landmarks, channels),
            "seq",
            scatter_dimension=1,
            tiled=True,
        ),
    )
    query_mean_grad = query_mean_grad + lax.dynamic_slice_in_dim(
        query_mean_direct.reshape(documents, landmarks, channels), position, LM_DEV, 1
    )
    key_mean_grad = key_mean_grad + lax.dynamic_slice_in_dim(
        key_mean_direct.reshape(documents, landmarks, channels), position, LM_DEV, 1
    )
    query_grad = query_direct.reshape(documents, tokens, channels) + jnp.repeat(
        query_mean_grad / segment, segment, axis=1
    )
    key_grad = key_direct.reshape(documents, tokens, channels) + jnp.repeat(
        key_mean_grad / segment, segment, axis=1
    )
    value_grad = value_direct.reshape(documents, tokens, channels) + value_conv
    return (
        layer_output,
        query_grad.astype(jnp.bfloat16),
        key_grad.astype(jnp.bfloat16),
        value_grad.astype(jnp.bfloat16),
        weight_grad,
    )


def solution(mesh):
    in_specs = (
        P(None, "seq", "head"),
        P(None, "seq", "head"),
        P(None, "seq", "head"),
        P(None, "head"),
        P("head", None),
        P(None, "seq", "head"),
    )
    out_specs = (
        P(None, "seq", "head"),
        P(None, "seq", "head"),
        P(None, "seq", "head"),
        P(None, "seq", "head"),
        P("head", "seq"),
    )
    return jax.shard_map(shards, mesh=mesh, in_specs=in_specs, out_specs=out_specs, check_vma=False)
```

profile of v0, /device:TPU:1, one launch (start us, length us, event | category | flops | bytes accessed | tf_op | source)
XLA Modules:
  0.0 1004.1 jit_solution(10653146830273043303)
XLA Ops:
  7.2 0.8 fusion.181
  8.0 4.5 collective-permute-start
  12.5 5.6 collective-permute-start.1
  18.1 1.7 copy.147
  19.8 0.9 convert_reduce_fusion.1
  20.7 1.0 copy.143
  21.7 0.9 convert_reduce_fusion
  22.5 1.0 copy.140
  23.5 1.0 copy.141
  24.6 54.3 %all_gather.10 = f32[2,128,128]{2,0,1:T(2,128)S(1)} all-gather(f32[2,2,128]{2,0,1:T(2,128)S(1)} %copy.133), channel_id=1, replica_groups=mesh['seq'=64,'head'=8] {'seq'}, dimensions={1}, use_global_device_ids=true | all-gather | bytes 133120 | tf_op jit(solution)/shard_map/all_gather | solution.py:66
  79.0 47.0 %all_gather.9 = f32[2,128,128]{2,0,1:T(2,128)S(1)} all-gather(f32[2,2,128]{2,0,1:T(2,128)S(1)} %copy.131), channel_id=1, replica_groups=mesh['seq'=64,'head'=8] {'seq'}, dimensions={1}, use_global_device_ids=true | all-gather | bytes 133120 | tf_op jit(solution)/shard_map/all_gather | solution.py:65
  126.5 123.6 %pmax.7 = f32[2,2,128]{2,1,0:T(2,128)S(1)} all-reduce(f32[2,2,128]{2,1,0:T(2,128)S(1)} %get-tuple-element.50), channel_id=1, replica_groups=mesh['seq'=64,'head'=8] {'seq'}, use_global_device_ids=true, to_apply=%region_7.0 | all-reduce | flops 512 | bytes 4096 | tf_op jit(solution)/shard_map/pmax | solution.py:82
  250.1 0.9 fusion.16
  252.6 0.7 fusion.170
  254.7 0.7 copy-done.13
  255.4 0.7 convolution_multiply_fusion.4
  257.5 0.7 copy-done.2
  258.2 1.1 convolution_multiply_fusion.3
  261.9 0.7 broadcast_in_dim.178
  262.6 0.7 broadcast_in_dim.176
  263.3 0.7 broadcast_in_dim.174
  268.2 0.7 broadcast_in_dim.222
  272.2 0.7 broadcast_in_dim.212
  273.6 0.7 broadcast_in_dim.208
  277.1 0.7 broadcast_in_dim.198
  279.2 0.7 broadcast_in_dim.192
  282.6 1.3 dynamic-slice
  284.5 126.7 %psum.22 = f32[2,2,128]{2,1,0:T(2,128)S(1)} all-reduce(f32[2,2,128]{2,1,0:T(2,128)S(1)} %fusion.15), channel_id=1, replica_groups=mesh['seq'=64,'head'=8] {'seq'}, use_global_device_ids=true, to_apply=%region_10.0 | all-reduce | flops 512 | bytes 4096 | tf_op jit(solution)/shard_map/psum | solution.py:84
  411.2 1.5 copy.148
  412.7 1.1 fusion.185
  413.8 1.1 reshape.303
  415.1 2.3 fusion.172
  417.4 1.4 fusion.180
  418.8 2.5 collective-permute-start.2
  421.3 3.2 collective-permute-start.3
  424.5 176.8 %all-reduce.9.cloned.1.call-done = (f32[2,2,128,64]{2,3,1,0:T(8,128)}, f32[2,2,128,64]{2,3,1,0:T(8,128)}) async-done(((f32[2,2,128,64]{2,3,1,0:T(8,128)}, f32[2,2,128,64]{2,3,1,0:T(8,128)}), (f32[2,2,128,64]{2,3,1,0:T(8,128)}, f32[2,2,128,64]{2,3,1,0:T(8,128)})) %all-reduce.9.cloned.1.call-update) | async-done | bytes 262160 | tf_op jit(solution)/shard_map/psum | solution.py:84
  601.3 1.5 fusion.169
  602.9 1.4 multiply_reduce_fusion.2
  604.3 1.6 convolution_multiply_fusion
  605.9 2.0 fusion.175
  607.9 2.9 multiply_reduce_fusion.1
  610.8 1.4 fusion.189
  612.8 0.8 copy.156
  613.6 1.0 copy.146
  614.6 2.0 fusion.154
  616.6 1.6 copy.169
  618.3 1.3 fusion.115
  620.3 1.8 convolution_bitcast_fusion
  622.1 2.4 fusion.158
  624.6 2.3 convolution_bitcast_fusion.1
  626.8 2.2 fusion.192
  629.7 0.7 fusion.187
  631.0 0.7 convolution_add_fusion.4
  632.3 0.7 fusion.188
  634.5 0.7 fusion.190
  635.8 0.7 convolution_add_fusion.2
  637.5 0.7 multiply_reduce_fusion
  639.7 1.1 fusion.155
  641.8 2.6 fusion.22
  644.4 161.6 %all-reduce.7.cloned.1.call-done = (f32[2,128,128]{2,0,1:T(2,128)}, f32[2,128,128]{2,0,1:T(2,128)}) async-done(((f32[2,128,128]{2,0,1:T(2,128)}, f32[2,128,128]{2,0,1:T(2,128)}), (f32[2,128,128]{2,0,1:T(2,128)}, f32[2,128,128]{2,0,1:T(2,128)})) %all-reduce.7.cloned.1.call-update) | async-done | bytes 262160
  805.9 0.7 constant_dynamic-slice_fusion
  808.6 37.5 %reduce-scatter.3.cloned.1.call-done = f32[256,256]{0,1:T(8,128)} async-done(((f32[2048,256]{0,1:T(8,128)}), f32[256,256]{0,1:T(8,128)}) %reduce-scatter.3.cloned.1.call-update) | async-done | bytes 262160 | tf_op jit(solution)/shard_map/reduce_scatter | solution.py:104
  846.0 1.6 convert_element_type.27
  847.7 149.9 %reduce-scatter.5.cloned.1.call-done = f32[128,32]{0,1:T(8,128)} async-done(((f32[128,2048]{0,1:T(8,128)}), f32[128,32]{0,1:T(8,128)}) %reduce-scatter.5.cloned.1.call-update) | async-done | bytes 16400 | tf_op jit(solution)/shard_map/reduce_scatter | solution.py:124
  (280 shorter events, 33.2 us)
Async XLA Ops:
  7.2 405.5 %copy-start = (bf16[128,2048]{1,0:T(8,128)(2,1)S(1)}, bf16[128,2048]{1,0:T(8,128)(2,1)}, u32[]{:S(2)}) copy-start(bf16[128,2048]{1,0:T(8,128)(2,1)} %param.10) | copy-start | bytes 1572868
  7.2 404.0 %all-gather.2.cloned.1.call-start = ((), (), s32[]{:S(2)}) async-start(), calls=%async_computation.3 | async-start | bytes 1179648 | tf_op jit(solution)/shard_map/all_gather | solution.py:113
  8.0 403.2 %collective-permute-start = (bf16[2,16,128]{2,1,0:T(8,128)(2,1)S(1)}, bf16[2,16,128]{2,1,0:T(8,128)(2,1)S(1)}, u32[]{:S(2)}, u32[]{:S(2)}) collective-permute-start(bf16[2,16,128]{2,1,0:T(8,128)(2,1)S(1)} %get-tuple-element.46), channel_id=1, source_target_pairs={{0,8},{8,16},{16,24},{24,32},{32,40},{40,48},{48,56},{56,64},{64,7... | collective-permute-start | bytes 24584 | tf_op jit(solution)/shard_map/ppermute | solution.py:21
  12.5 398.7 %collective-permute-start.1 = (bf16[2,16,128]{2,1,0:T(8,128)(2,1)S(1)}, bf16[2,16,128]{2,1,0:T(8,128)(2,1)S(1)}, u32[]{:S(2)}, u32[]{:S(2)}) collective-permute-start(bf16[2,16,128]{2,1,0:T(8,128)(2,1)S(1)} %get-tuple-element.47), channel_id=1, source_target_pairs={{8,0},{16,8},{24,16},{32,24},{40,32},{48,40},{56,48},{64,56},{72,6... | collective-permute-start | bytes 24584 | tf_op jit(solution)/shard_map/ppermute | solution.py:23
  19.8 581.6 %all-reduce.9.cloned.1.call-start = ((), (), s32[]{:S(2)}) async-start(), calls=%async_computation.6 | async-start | bytes 524288 | tf_op jit(solution)/shard_map/psum | solution.py:84
  21.6 230.4 %copy-start.25 = (bf16[2,128,128]{1,2,0:T(8,128)(2,1)}, bf16[2,128,128]{1,2,0:T(8,128)(2,1)S(1)}, u32[]{:S(2)}) copy-start(bf16[2,128,128]{1,2,0:T(8,128)(2,1)S(1)} %copy.143) | copy-start | bytes 196612
  23.5 227.6 %copy-start.21 = (bf16[2,128,128]{1,2,0:T(8,128)(2,1)}, bf16[2,128,128]{1,2,0:T(8,128)(2,1)S(1)}, u32[]{:S(2)}) copy-start(bf16[2,128,128]{1,2,0:T(8,128)(2,1)S(1)} %copy.140) | copy-start | bytes 196612
  24.5 226.6 %copy-start.26 = (bf16[2,128,128]{1,2,0:T(8,128)(2,1)}, bf16[2,128,128]{1,2,0:T(8,128)(2,1)S(1)}, u32[]{:S(2)}) copy-start(bf16[2,128,128]{1,2,0:T(8,128)(2,1)S(1)} %copy.141) | copy-start | bytes 196612
  24.5 232.2 %copy-start.7 = (f32[128,128]{1,0:T(8,128)}, f32[128,128]{1,0:T(8,128)S(1)}, u32[]{:S(2)}) copy-start(f32[128,128]{1,0:T(8,128)S(1)} %get-tuple-element.60) | copy-start | bytes 196612
  79.0 174.3 %copy-start.10 = (f32[2,128,128]{1,2,0:T(8,128)}, f32[2,128,128]{1,2,0:T(8,128)S(1)}, u32[]{:S(2)}) copy-start(f32[2,128,128]{1,2,0:T(8,128)S(1)} %copy.134) | copy-start | bytes 393220
  126.5 125.2 %copy-start.4 = (f32[2,2,128,128]{2,3,1,0:T(8,128)}, f32[2,2,128,128]{2,3,1,0:T(8,128)S(1)}, u32[]{:S(2)}) copy-start(f32[2,2,128,128]{2,3,1,0:T(8,128)S(1)} %get-tuple-element.51) | copy-start | bytes 786436
  252.6 3.5 copy-start.76
  254.3 160.8 %copy-start.34 = (f32[2,2,128]{2,1,0:T(2,128)}, f32[2,2,128]{2,1,0:T(2,128)S(1)}, u32[]{:S(2)}) copy-start(f32[2,2,128]{2,1,0:T(2,128)S(1)} %fusion.13) | copy-start | bytes 6148
  256.1 155.1 %copy-start.24 = (bf16[2,128,128]{2,1,0:T(8,128)(2,1)S(1)}, bf16[2,128,128]{2,1,0:T(8,128)(2,1)}, u32[]{:S(2)}) copy-start(bf16[2,128,128]{2,1,0:T(8,128)(2,1)} %param.8) | copy-start | bytes 196612
  413.8 187.5 %copy-start.6 = (f32[2,2,128,128]{3,2,1,0:T(8,128)S(1)}, f32[2,2,128,128]{3,2,1,0:T(8,128)}, u32[]{:S(2)}) copy-start(f32[2,2,128,128]{3,2,1,0:T(8,128)} %convolution_multiply_fusion.3) | copy-start | bytes 786436
  417.3 190.6 %copy-start.35 = (f32[2,2,128]{2,1,0:T(2,128)S(1)}, f32[2,2,128]{2,1,0:T(2,128)}, u32[]{:S(2)}) copy-start(f32[2,2,128]{2,1,0:T(2,128)} %copy-done.34) | copy-start | bytes 6148
  417.3 193.5 %copy-start.3 = (f32[2,2,128,128]{3,2,1,0:T(8,128)S(1)}, f32[2,2,128,128]{3,2,1,0:T(8,128)}, u32[]{:S(2)}) copy-start(f32[2,2,128,128]{3,2,1,0:T(8,128)} %copy-done.2) | copy-start | bytes 786436
  417.4 388.6 %all-reduce.7.cloned.1.call-start = ((), (), s32[]{:S(2)}) async-start(), calls=%async_computation.5 | async-start | bytes 524288
  418.8 222.6 %collective-permute-start.2 = (f32[2,16,128]{2,1,0:T(8,128)}, f32[2,16,128]{2,1,0:T(8,128)}, u32[]{:S(2)}, u32[]{:S(2)}) collective-permute-start(f32[2,16,128]{2,1,0:T(8,128)} %get-tuple-element.44), channel_id=1, source_target_pairs={{8,0},{16,8},{24,16},{32,24},{40,32},{48,40},{56,48},{64,56},{72,6... | collective-permute-start | bytes 49160 | tf_op jit(solution)/shard_map/ppermute | solution.py:23
  421.3 220.1 %collective-permute-start.3 = (f32[2,16,128]{2,1,0:T(8,128)}, f32[2,16,128]{2,1,0:T(8,128)}, u32[]{:S(2)}, u32[]{:S(2)}) collective-permute-start(f32[2,16,128]{2,1,0:T(8,128)} %get-tuple-element.45), channel_id=1, source_target_pairs={{0,8},{8,16},{16,24},{24,32},{32,40},{40,48},{48,56},{56,64},{64,7... | collective-permute-start | bytes 49160 | tf_op jit(solution)/shard_map/ppermute | solution.py:21
  601.3 6.6 copy-start.32
  602.9 9.4 copy-start.5
  602.9 9.3 copy-start.27
  604.3 8.3 copy-start.30
  605.9 6.7 copy-start.22
  607.9 6.7 copy-start.16
  610.8 7.5 copy-start.37
  610.8 7.5 copy-start.39
  610.8 7.5 copy-start.41
  610.8 7.5 copy-start.43
  610.8 7.5 copy-start.45
  610.8 7.5 copy-start.47
  612.6 7.1 copy-start.18
  622.1 224.0 %reduce-scatter.3.cloned.1.call-start = ((), (), s32[]{:S(2)}) async-start(), calls=%async_computation.2 | async-start | bytes 2359296 | tf_op jit(solution)/shard_map/reduce_scatter | solution.py:104
  624.5 373.1 %reduce-scatter.5.cloned.1.call-start = ((), (), s32[]{:S(2)}) async-start(), calls=%async_computation.4 | async-start | bytes 1064960 | tf_op jit(solution)/shard_map/reduce_scatter | solution.py:124
  626.8 4.2 copy-start.8
  629.7 3.3 copy-start.19
  638.7 2.8 copy-start.9
  638.7 2.8 copy-start.38
  638.7 2.8 copy-start.40
  638.7 2.8 copy-start.42
  638.7 2.8 copy-start.44
  638.7 2.8 copy-start.46
  638.7 2.8 copy-start.48
  638.7 2.8 copy-start.49
  638.7 2.8 copy-start.50
  638.8 2.8 copy-start.51
  638.8 2.8 copy-start.52
  638.8 2.8 copy-start.53
  638.8 2.8 copy-start.54
  638.8 2.8 copy-start.55
  638.8 2.8 copy-start.56
  638.8 2.8 copy-start.57
  638.8 2.8 copy-start.58
  638.8 2.8 copy-start.59
  638.8 2.8 copy-start.60
  638.9 2.8 copy-start.61
  638.9 2.8 copy-start.62
  638.9 2.8 copy-start.63
  638.9 2.8 copy-start.64
  638.9 2.8 copy-start.65
  638.9 2.8 copy-start.66
  638.9 2.8 copy-start.67
  638.9 2.8 copy-start.68
  (24 other events, 50.7 us)
Sparse Core Ops, SparseCore 0:
  19.9 37.9 all-gather.1
  417.5 183.7 all-reduce.8
  622.2 183.7 all-reduce.6
  808.6 37.3 reduce-scatter.2
  851.0 146.4 reduce-scatter.4
where the time goes:
time: 1010 us; the launch traced here: 1000 us
  waiting for transfers between devices  526 us (52%)
  blocking collectives  352 us (35%)
  matrix products  43.3 us (4%)
  local copies, waits for them, and re-layouts  42.4 us (4%)
  starting transfers between devices  16 us (2%)
  between operations  16 us (2%)
    psum x1, waiting for transfers between devices, shards(): lax.psum((jnp.sum(local_exp, axis=-1), jnp.einsum('bhjn,bnhd->bhjd', loca...  177 us
    unnamed x6, waiting for transfers between devices  162 us
    reduce_scatter x1, waiting for transfers between devices, shards(): lax.psum_scatter(weight_piece, 'seq', scatter_dimension=1, tiled=True)  150 us
    psum x1, blocking collectives, shards(): lax.psum((jnp.sum(local_exp, axis=-1), jnp.einsum('bhjn,bnhd->bhjd', loca...  127 us
    pmax x1, blocking collectives, shards(): key_peak = lax.pmax(local_peak, 'seq')  124 us
    all_gather x1, blocking collectives, shards(): lax.all_gather(local_key_means, 'seq', axis=1, tiled=True)  54.3 us
    all_gather x1, blocking collectives, shards(): lax.all_gather(local_query_means, 'seq', axis=1, tiled=True)  47 us
    reduce_scatter x1, waiting for transfers between devices, shards(): lax.psum_scatter(lax.dot_general(weight_block, flat_context, (((0,), (1,)...  37.5 us
  transfers between devices with their start and end apart: 9, of which 4 were waited for; matrix products, arithmetic and copies ran while one was open for 9% of the time, Pallas kernels for 0%

commit v1 on v0

v1 whole, which is shorter than its diff:
```python
import functools

import jax
import jax.numpy as jnp
from jax import lax
from jax.experimental import pallas as pl
from jax.experimental.pallas import tpu as pltpu
from jax.sharding import PartitionSpec as P

ITERS = 2
SEGS = 2
f32 = jnp.float32
bf16 = jnp.bfloat16
PIECES = ((0,), (2, 6), (1, 3), (7, 5), (4,))
NN = (((1,), (0,)), ((), ()))
NT = (((1,), (1,)), ((), ()))


def dot(left, right, dims=NN):
    return lax.dot_general(left, right, dims, preferred_element_type=f32)


def halves(value):
    if value.dtype == bf16:
        return (value,)
    high = value.astype(bf16)
    return high, (value - high.astype(f32)).astype(bf16)


def prod(left, right, dims=NN):
    left = left if isinstance(left, tuple) else halves(left)
    right = right if isinstance(right, tuple) else halves(right)
    total = dot(left[0], right[0], dims)
    if len(right) > 1:
        total = total + dot(left[0], right[1], dims)
    if len(left) > 1:
        total = total + dot(left[1], right[0], dims)
    return total


def block_at(shift, parts):
    core = lax.rem(lax.axis_index("seq"), 2)
    step = jnp.where(core == 0, parts - shift, parts + shift)
    return lax.rem(lax.axis_index("head") + step, parts)


def first_head(shape):
    return lax.broadcasted_iota(jnp.int32, shape, 1) < shape[1] // 2


def stack(rows):
    mask = first_head(rows.shape)
    zero = jnp.zeros_like(rows)
    return jnp.concatenate([jnp.where(mask, rows, zero), jnp.where(mask, zero, rows)], axis=0)


def own_blocks(full):
    count = full.shape[0] // 2
    mask = first_head((count, full.shape[1]))
    zero = jnp.zeros((count, full.shape[1]), full.dtype)
    return jnp.concatenate(
        [jnp.where(mask, full[:count], zero), jnp.where(mask, zero, full[count:])], axis=0
    )


def pick(full):
    count = full.shape[0] // 2
    return jnp.where(first_head((count, full.shape[1])), full[:count], full[count:])


def marks(ref, row, groups, stride):
    return jnp.concatenate(
        [ref[pl.ds(row + seg, groups, stride=stride), :] for seg in range(SEGS)], axis=0
    )


def means_kernel(q_ref, k_ref, out_ref):
    documents, tokens, _ = q_ref.shape
    segment = tokens // SEGS
    rows = []
    for ref in (q_ref, k_ref):
        for doc in range(documents):
            for seg in range(SEGS):
                part = ref[doc, seg * segment : (seg + 1) * segment, :].astype(f32)
                rows.append(jnp.sum(part, axis=0, keepdims=True) * (1.0 / segment))
    block = jnp.concatenate(rows, axis=0)
    out_ref[...] = jnp.broadcast_to(block[None], out_ref.shape)


def stats_kernel(scale, got_ref, q_ref, k_ref, v_ref, t_ref, s_ref, o_ref, log_ref, qm_ref, km_ref):
    documents = q_ref.shape[0]
    groups = got_ref.shape[0] // 8
    count = SEGS * groups
    logs = []
    for doc in range(documents):
        qm = marks(got_ref, doc * SEGS, groups, 8)
        km = marks(got_ref, 4 + doc * SEGS, groups, 8)
        qm_ref[doc] = qm
        km_ref[doc] = km
        scores = prod(q_ref[doc], stack(km), NT) * scale
        for head in range(2):
            part = scores[:, head * count : (head + 1) * count]
            part = jnp.exp(part - jnp.max(part, axis=1, keepdims=True))
            t_ref[doc, :, head * count : (head + 1) * count] = part / jnp.sum(
                part, axis=1, keepdims=True
            )
        scores = prod(k_ref[doc], stack(qm), NT) * scale
        s_ref[doc] = scores
        peak = jnp.max(scores, axis=0, keepdims=True)
        part = jnp.exp(scores - peak)
        total = jnp.sum(part, axis=0, keepdims=True)
        o_ref[doc] = pick(prod((part / total).T, v_ref[doc]))
        log = peak + jnp.log(total)
        logs += [log[:, :count], log[:, count:]]
    logs.append(jnp.zeros((8 - len(logs), count), f32))
    log_ref[...] = jnp.concatenate(logs, axis=0)


def chunk_kernel(parts, rim, *refs):
    og_refs = refs[:parts]
    w_ref, v_ref, t_ref, o_ref, log_ref = refs[parts : parts + 5]
    out_ref, cg_ref, head_ref, tail_ref = refs[parts + 5 : parts + 9]
    documents, tokens, channels = cg_ref.shape
    groups = out_ref.shape[0] // 16
    width = w_ref.shape[1] // parts

    def columns(shift):
        return pl.ds(pl.multiple_of(block_at(shift, parts) * width, width), width)

    total = None
    for shift in range(parts):
        part = dot(og_refs[shift][...], w_ref[:, columns(shift)], NT)
        total = part if total is None else total + part
    for ref, shifts in zip(refs[parts + 9 :], PIECES):
        for slot, shift in enumerate(shifts):
            ref[slot] = w_ref[:, columns(-shift)]
    for doc in range(documents):
        grad = total[doc * tokens : (doc + 1) * tokens]
        cg_ref[doc] = grad
        for ref, rows in ((head_ref, slice(0, rim)), (tail_ref, slice(tokens - rim, tokens))):
            high, low = halves(grad[rows])
            ref[doc, 0:rim, :] = v_ref[doc, rows, :]
            ref[doc, rim : 2 * rim, :] = high
            ref[doc, 2 * rim : 3 * rim, :] = low
        mix = pick(prod(t_ref[doc].T, grad))
        for seg in range(SEGS):
            row = doc * SEGS + seg
            rows = slice(seg * groups, (seg + 1) * groups)
            out_ref[pl.ds(row, groups, stride=16), :] = o_ref[doc, rows, :]
            out_ref[pl.ds(4 + row, groups, stride=16), :] = mix[rows]
    for row in range(8):
        out_ref[pl.ds(8 + row, groups, stride=16), :] = jnp.broadcast_to(
            log_ref[row : row + 1, :], (groups, channels)
        )


def newton_kernel(scale, parts, *refs):
    og_refs = refs[:parts]
    qm_ref, km_ref, ogt_ref, a_ref, z_ref, p_ref, f2_ref, f3_ref, inv_ref = refs[parts:]
    documents, count, _ = qm_ref.shape
    width = og_refs[0].shape[1]
    for shift in range(parts):
        block = block_at(shift, parts)
        ogt_ref[pl.ds(pl.multiple_of(block * width, width), width), :] = og_refs[shift][...].T
    row = lax.broadcasted_iota(jnp.int32, (count, count), 0)
    identity = (row == lax.broadcasted_iota(jnp.int32, (count, count), 1)).astype(f32)
    units = []
    for doc in range(documents):
        scores = prod(stack(qm_ref[doc]), km_ref[doc], NT) * scale
        scores = jnp.exp(scores - jnp.max(scores, axis=1, keepdims=True))
        scores = scores / jnp.sum(scores, axis=1, keepdims=True)
        units += [scores[:count], scores[count:]]
    approx = []
    for index, unit in enumerate(units):
        a_ref[index] = unit
        sums = jnp.sum(unit, axis=0, keepdims=True)
        approx.append(unit.T / jnp.max(sums, axis=1, keepdims=True))
    units = [halves(unit) for unit in units]
    every = range(len(units))
    for step in range(ITERS):
        for i in every:
            z_ref[step, i] = approx[i]
        spread = [halves(approx[i]) for i in every]
        product = [prod(units[i], spread[i]) for i in every]
        for i in every:
            p_ref[step, i] = product[i]
        factor = [7.0 * identity - product[i] for i in every]
        product = [halves(product[i]) for i in every]
        factor = [15.0 * identity - prod(product[i], factor[i]) for i in every]
        for i in every:
            f2_ref[step, i] = factor[i]
        factor = [13.0 * identity - prod(product[i], factor[i]) for i in every]
        for i in every:
            f3_ref[step, i] = factor[i]
        approx = [0.25 * prod(spread[i], factor[i]) for i in every]
    for i in every:
        inv_ref[i] = approx[i]


def combine_kernel(got_ref, out_ref, log_ref):
    groups = got_ref.shape[0] // 16
    channels = got_ref.shape[1]
    me = lax.axis_index("seq")
    lane = lax.broadcasted_iota(jnp.int32, (groups, channels), 1)
    shares, logs = [], []
    for unit in range(4):
        log = got_ref[pl.ds(8 + unit, groups, stride=16), :]
        top = jnp.max(log, axis=0, keepdims=True)
        part = jnp.exp(log - top)
        total = jnp.sum(part, axis=0, keepdims=True)
        logs.append(top + jnp.log(total))
        shares.append(part / total)
    logs.append(jnp.zeros((4, channels), f32))
    log_ref[...] = jnp.concatenate(logs, axis=0)
    mixed, mix = [], []
    for doc in range(2):
        for seg in range(SEGS):
            row = doc * SEGS + seg
            weight = [
                jnp.sum(
                    jnp.where(lane == seg * groups + me, shares[doc * 2 + head], 0.0),
                    axis=1,
                    keepdims=True,
                )
                for head in range(2)
            ]
            weight = jnp.where(lane < channels // 2, weight[0], weight[1])
            mixed.append(
                jnp.sum(weight * got_ref[pl.ds(row, groups, stride=16), :], axis=0, keepdims=True)
            )
            mix.append(jnp.sum(got_ref[pl.ds(4 + row, groups, stride=16), :], axis=0, keepdims=True))
    block = jnp.concatenate(mixed + mix, axis=0)
    out_ref[...] = jnp.broadcast_to(block[None], out_ref.shape)


def conv_kernel(taps_ref, v_ref, cg_ref, above_ref, below_ref, conv_ref, back_ref, vp, cp):
    documents, tokens, channels = v_ref.shape
    taps = taps_ref.shape[0]
    rim = taps // 2
    for doc in range(documents):
        vp[doc, rim : rim + tokens, :] = v_ref[doc].astype(f32)
        cp[doc, rim : rim + tokens, :] = cg_ref[doc]
        for ref, start in ((above_ref, 0), (below_ref, rim + tokens)):
            rows = [ref[doc, i * rim : (i + 1) * rim, :].astype(f32) for i in range(3)]
            vp[doc, start : start + rim, :] = rows[0]
            cp[doc, start : start + rim, :] = rows[1] + rows[2]
    lane = lax.broadcasted_iota(jnp.int32, (1, channels), 1)
    for doc in range(documents):
        conv = jnp.zeros((tokens, channels), f32)
        back = jnp.zeros((tokens, channels), f32)
        for tap in range(taps):
            weight = jnp.where(lane < channels // 2, taps_ref[tap, 0], taps_ref[tap, 1])
            conv = conv + weight * vp[doc, tap : tap + tokens, :]
            start = 2 * rim - tap
            back = back + weight * cp[doc, start : start + tokens, :]
        conv_ref[doc] = conv
        back_ref[doc] = back


def context_kernel(got_ref, t_ref, inv_ref, conv_ref, ctx_ref, mixed_ref, mix_ref, lm_ref):
    documents, tokens, _ = conv_ref.shape
    groups = got_ref.shape[0] // 8
    for doc in range(documents):
        mixed = marks(got_ref, doc * SEGS, groups, 8)
        mixed_ref[doc] = mixed
        mix_ref[doc] = marks(got_ref, 4 + doc * SEGS, groups, 8)
        inverse = jnp.concatenate([inv_ref[doc * 2], inv_ref[doc * 2 + 1]], axis=0)
        landmark = own_blocks(prod(inverse, mixed))
        lm_ref[doc] = landmark
        ctx = (prod(t_ref[doc], landmark) + conv_ref[doc]).astype(bf16)
        ctx_ref[doc * tokens : (doc + 1) * tokens, :] = ctx


def main_kernel(
    scale, log_ref, t_ref, s_ref, cg_ref, qm_ref, km_ref, inv_ref, q_ref, k_ref, v_ref,
    back_ref, ogt_ref, ctx_ref, mixed_ref, mix_ref, lm_ref, out_ref, qd_ref, kd_ref, vg_ref, held,
):
    documents, tokens, channels = q_ref.shape
    count = qm_ref.shape[1]
    groups = count // SEGS
    for doc in range(documents):
        mixed = mixed_ref[doc]
        weights = t_ref[doc]
        upstream = prod(cg_ref[doc], lm_ref[doc], NT)
        back = weights * upstream
        back = jnp.concatenate(
            [
                back[:, part] - weights[:, part] * jnp.sum(back[:, part], axis=1, keepdims=True)
                for part in (slice(0, count), slice(count, 2 * count))
            ],
            axis=1,
        ) * scale
        qd_ref[doc] = prod(back, stack(km_ref[doc]))
        key_terms = pick(prod(back.T, q_ref[doc]))
        turned = jnp.concatenate([inv_ref[doc * 2].T, inv_ref[doc * 2 + 1].T], axis=0)
        mixed_grad = own_blocks(prod(turned, mix_ref[doc]))
        ones = jnp.ones((8, channels), bf16)
        mixed_dot = prod(ones, mixed_grad * stack(mixed), NT)[0:1]
        mixed_grad = halves(mixed_grad)
        log = jnp.concatenate(
            [log_ref[doc * 2 : doc * 2 + 1, :], log_ref[doc * 2 + 1 : doc * 2 + 2, :]], axis=1
        )
        key_weights = jnp.exp(s_ref[doc] - log)
        key_back = key_weights * (prod(v_ref[doc], mixed_grad, NT) - mixed_dot) * scale
        query_terms = pick(prod(key_back.T, k_ref[doc]))
        kd_ref[doc] = prod(key_back, stack(qm_ref[doc]))
        vg_ref[doc] = (prod(key_weights, mixed_grad) + back_ref[doc]).astype(bf16)
        for base, terms in ((0, query_terms), (4, key_terms)):
            high = terms.astype(bf16).astype(f32)
            low = terms - high
            for seg in range(SEGS):
                row = base + doc * SEGS + seg
                rows = slice(seg * groups, (seg + 1) * groups)
                held[pl.ds(row, groups, stride=16), :] = high[rows]
                held[pl.ds(8 + row, groups, stride=16), :] = low[rows]
    out_ref[:, 0:16, :] = held[...].astype(bf16).reshape(groups, 16, channels)
    terms = dot(ogt_ref[...], ctx_ref[...]).astype(bf16)
    out_ref[:, 16:, :] = terms.reshape(groups, terms.shape[0] // groups, channels)


def newton_back_kernel(
    scale, a_ref, z_ref, p_ref, f2_ref, f3_ref, qm_ref, km_ref, mixed_ref, mix_ref, out_ref, held
):
    documents, count, channels = qm_ref.shape
    me = lax.axis_index("seq")
    groups = count // SEGS
    row = lax.broadcasted_iota(jnp.int32, (count, count), 0)
    identity = (row == lax.broadcasted_iota(jnp.int32, (count, count), 1)).astype(f32)
    every = range(documents * 2)
    down = []
    for doc in range(documents):
        full = prod(stack(mix_ref[doc]), mixed_ref[doc], NT)
        down += [full[:count], full[count:]]
    unit_t = [halves(a_ref[i].T) for i in every]
    grads = [None for i in every]
    for step in reversed(range(ITERS)):
        down = [halves(0.25 * down[i]) for i in every]
        turned = [halves(z_ref[step, i].T) for i in every]
        product = [p_ref[step, i] for i in every]
        product_t = [halves(product[i].T) for i in every]
        third = [prod(turned[i], down[i]) for i in every]
        third = [halves(third[i]) for i in every]
        carry = [prod(down[i], f3_ref[step, i].T) for i in every]
        second = [-prod(product_t[i], third[i]) for i in every]
        second = [halves(second[i]) for i in every]
        first = [-prod(product_t[i], second[i]) for i in every]
        flow = [
            -first[i]
            - prod(third[i], f2_ref[step, i].T)
            - prod(second[i], (7.0 * identity - product[i]).T)
            for i in every
        ]
        flow = [halves(flow[i]) for i in every]
        more = [prod(flow[i], turned[i]) for i in every]
        grads = [more[i] if grads[i] is None else grads[i] + more[i] for i in every]
        down = [carry[i] + prod(unit_t[i], flow[i]) for i in every]
    for doc in range(documents):
        back, turned = [], []
        for head in range(2):
            i = doc * 2 + head
            unit = a_ref[i]
            peak = jnp.max(jnp.sum(unit, axis=0, keepdims=True), axis=1, keepdims=True)
            grad = grads[i] + down[i].T / peak
            part = unit * grad
            part = (part - unit * jnp.sum(part, axis=1, keepdims=True)) * scale
            back.append(part)
            turned.append(part.T)
        held[doc] = pick(prod(jnp.concatenate(back, axis=0), km_ref[doc]))
        held[documents + doc] = pick(prod(jnp.concatenate(turned, axis=0), qm_ref[doc]))
    for kind in range(2 * documents):
        for seg in range(SEGS):
            out_row = kind * SEGS + seg
            out_ref[out_row : out_row + 1, :] = held[kind, pl.ds(seg * groups + me, 1), :]


def finish_kernel(got_ref, own_ref, qd_ref, kd_ref, qg_ref, kg_ref, wg_ref):
    documents, tokens, _ = qd_ref.shape
    segment = tokens // SEGS
    total = jnp.sum(got_ref[:, 0:16, :].astype(f32), axis=0)
    total = (total[0:8] + total[8:16] + own_ref[...]) * (1.0 / segment)
    for base, source, target in ((0, qd_ref, qg_ref), (4, kd_ref, kg_ref)):
        for doc in range(documents):
            for seg in range(SEGS):
                row = base + doc * SEGS + seg
                rows = slice(seg * segment, (seg + 1) * segment)
                target[doc, rows, :] = (source[doc, rows, :] + total[row : row + 1]).astype(bf16)
    wg_ref[...] = jnp.sum(got_ref[:, 16:, :].astype(f32), axis=0)


def output_kernel(blocks, weights, *refs):
    total = None
    tokens = refs[-1].shape[0]
    for (index, block), (source, slot) in zip(blocks, weights):
        part = dot(refs[index][block * tokens : (block + 1) * tokens, :], refs[source][slot])
        total = part if total is None else total + part
    refs[-1][...] = total.astype(bf16)


def call(kernel, outs, *operands, scratch=(), smem=(), flops=1e8, size=2e6):
    vmem = pl.BlockSpec(memory_space=pltpu.VMEM)
    scalar = pl.BlockSpec(memory_space=pltpu.SMEM)
    return pl.pallas_call(
        kernel,
        out_shape=[jax.ShapeDtypeStruct(shape, kind) for shape, kind in outs],
        in_specs=[scalar if i in smem else vmem for i in range(len(operands))],
        out_specs=[vmem for _ in outs],
        scratch_shapes=list(scratch),
        compiler_params=pltpu.CompilerParams(vmem_limit_bytes=16 * 1024 * 1024),
        cost_estimate=pl.CostEstimate(
            flops=int(flops), bytes_accessed=int(size), transcendentals=0
        ),
    )(*operands)


def exchange(blocks, axis):
    return lax.all_to_all(blocks, axis, 0, 0, tiled=True)


def shift_by(block, shift, parts):
    pairs = []
    for i in range(lax.axis_size("seq")):
        step = shift if i % 2 == 0 else parts - shift
        pairs += [(i * parts + j, i * parts + (j + step) % parts) for j in range(parts)]
    return lax.ppermute(block, ("seq", "head"), pairs)


def gathered(block, parts):
    return [block] + [shift_by(block, shift, parts) for shift in range(1, parts)]


def shards(queries, key_vectors, value_vectors, conv_taps, out_weight, out_grad):
    documents, tokens, channels = queries.shape
    heads = conv_taps.shape[1]
    groups = lax.axis_size("seq")
    parts = lax.axis_size("head")
    count = SEGS * groups
    scale = (channels // heads) ** (-0.5)
    rim = conv_taps.shape[0] // 2
    model_width = out_weight.shape[1]
    own_width = model_width // parts
    column_rows = model_width // groups
    rows_shape = (documents, tokens, channels)
    marks_shape = (documents, count, channels)
    pair_shape = (documents, tokens, 2 * count)
    units = 2 * documents
    saved = (ITERS, units, count, count)

    (sent,) = call(means_kernel, [((groups, 8, channels), f32)], queries, key_vectors)
    own_grad, sent = lax.optimization_barrier((out_grad, sent))
    got = exchange(sent, "seq").reshape(groups * 8, channels)
    og_parts = gathered(own_grad.reshape(documents * tokens, own_width), parts)

    weights, scores, local_mixed, local_log, qm, km = call(
        functools.partial(stats_kernel, scale),
        [
            (pair_shape, f32),
            (pair_shape, f32),
            (marks_shape, f32),
            ((8, count), f32),
            (marks_shape, f32),
            (marks_shape, f32),
        ],
        got, queries, key_vectors, value_vectors,
    )
    sent, context_grad, first_rows, last_rows, *pieces = call(
        functools.partial(chunk_kernel, parts, rim),
        [((groups * 16, channels), f32), (rows_shape, f32)]
        + [((documents, 3 * rim, channels), bf16)] * 2
        + [((len(shifts), channels, own_width), bf16) for shifts in PIECES],
        *og_parts, out_weight, value_vectors, weights, local_mixed, local_log,
    )
    got = exchange(sent, "seq")
    ends = groups - 1
    above = lax.ppermute(last_rows, "seq", [(i, i + 1) for i in range(ends)])
    below = lax.ppermute(first_rows, "seq", [(i + 1, i) for i in range(ends)])
    kept, stay, up, down, across = pieces
    up = shift_by(up, 1, parts)
    down = shift_by(down, parts - 1, parts)
    across = shift_by(across, 4, parts)
    og_turned, a, z, p, f2, f3, inverse = call(
        functools.partial(newton_kernel, scale, parts),
        [((model_width, documents * tokens), bf16), ((units, count, count), f32)]
        + [(saved, f32)] * 4
        + [((units, count, count), f32)],
        *og_parts, qm, km,
        flops=3e9,
    )
    got, up, down, across, above, below, inverse = lax.optimization_barrier(
        (got, up, down, across, above, below, inverse)
    )
    sent, logs = call(
        combine_kernel, [((groups, 8, channels), f32), ((8, count), f32)], got
    )
    sent, up, down, stay = lax.optimization_barrier((sent, up, down, stay))
    got = exchange(sent, "seq").reshape(groups * 8, channels)
    conv, back = call(
        conv_kernel,
        [(rows_shape, f32), (rows_shape, f32)],
        conv_taps, value_vectors, context_grad, above, below,
        scratch=[pltpu.VMEM((documents, tokens + 2 * rim, channels), f32)] * 2,
        smem=(0,),
        flops=1e9,
    )
    up_two = shift_by(jnp.concatenate([stay[0:1], up[1:2]], axis=0), 2, parts)
    down_two = shift_by(jnp.concatenate([stay[1:2], down[1:2]], axis=0), parts - 2, parts)
    got, up_two, down_two, conv, back = lax.optimization_barrier(
        (got, up_two, down_two, conv, back)
    )
    weight_parts = [kept, up, down, across, up_two, down_two]
    context_b, mixed, mix, landmark_mix = call(
        context_kernel,
        [
            ((documents * tokens, channels), bf16),
            (marks_shape, f32),
            (marks_shape, f32),
            ((documents, 2 * count, channels), f32),
        ],
        got, weights, inverse, conv,
    )
    near = [shift_by(context_b, 1, parts), shift_by(context_b, parts - 1, parts)]
    sent, query_direct, key_direct, value_grad = call(
        functools.partial(main_kernel, scale),
        [
            ((groups, 16 + column_rows, channels), bf16),
            (rows_shape, f32),
            (rows_shape, f32),
            (rows_shape, bf16),
        ],
        logs, weights, scores, context_grad, qm, km, inverse, queries, key_vectors,
        value_vectors, back, og_turned, context_b, mixed, mix, landmark_mix,
        scratch=[pltpu.VMEM((groups * 16, channels), f32)],
        flops=1e9,
    )
    sent, near, mix = lax.optimization_barrier((sent, near, mix))
    got = exchange(sent, "seq")
    far = [
        shift_by(jnp.concatenate([near[0], context_b, near[1]], axis=0), 3, parts),
        shift_by(jnp.concatenate([near[0], context_b], axis=0), parts - 3, parts),
    ]
    (own,) = call(
        functools.partial(newton_back_kernel, scale),
        [((8, channels), f32)],
        a, z, p, f2, f3, qm, km, mixed, mix,
        scratch=[pltpu.VMEM((2 * documents, count, channels), f32)],
        flops=5e9,
    )
    blocks = ((0, 0), (1, 0), (3, 2), (3, 1), (3, 0), (4, 1), (4, 0), (2, 0))
    slots = ((5, 0), (6, 0), (9, 0), (9, 1), (8, 0), (10, 1), (10, 0), (7, 0))
    (layer_output,) = call(
        functools.partial(output_kernel, blocks, slots),
        [((documents * tokens, own_width), bf16)],
        context_b, *near, *far, *weight_parts,
    )
    query_grad, key_grad, weight_grad = call(
        finish_kernel,
        [(rows_shape, bf16), (rows_shape, bf16), ((column_rows, channels), f32)],
        got, own, query_direct, key_direct,
    )
    return (
        layer_output.reshape(documents, tokens, own_width),
        query_grad,
        key_grad,
        value_grad,
        weight_grad.T,
    )


def solution(mesh):
    in_specs = (
        P(None, "seq", "head"),
        P(None, "seq", "head"),
        P(None, "seq", "head"),
        P(None, "head"),
        P("head", None),
        P(None, "seq", "head"),
    )
    out_specs = (
        P(None, "seq", "head"),
        P(None, "seq", "head"),
        P(None, "seq", "head"),
        P(None, "seq", "head"),
        P("head", "seq"),
    )
    return jax.shard_map(shards, mesh=mesh, in_specs=in_specs, out_specs=out_specs, check_vma=False)
```

time: 1010 us -> 162 us (0.16)
  waiting for transfers between devices: 526 us -> 16.2 us
  blocking collectives: 352 us -> 0 us
  starting transfers between devices: 16 us -> 114 us
  matrix products: 43.3 us -> 0 us
  local copies, waits for them, and re-layouts: 42.4 us -> 11.5 us
  Pallas kernels: 0 us -> 17.1 us
  between operations: 16 us -> 1.18 us
    reduce_scatter x2 -> x0, waiting for transfers between devices: 187 us -> none  [the longest x1 150 us: shards(): lax.psum_scatter(weight_piece, 'seq', scatter_dimension=1, tiled=True)]
    psum x1 -> x0, waiting for transfers between devices: 177 us -> none  [shards(): lax.psum((jnp.sum(local_exp, axis=-1), jnp.einsum('bhjn,bnhd->bhjd', loca...]
    unnamed x6 -> x0, waiting for transfers between devices: 162 us -> none
    psum x1 -> x0, blocking collectives: 127 us -> none  [shards(): lax.psum((jnp.sum(local_exp, axis=-1), jnp.einsum('bhjn,bnhd->bhjd', loca...]
    pmax x1 -> x0, blocking collectives: 124 us -> none  [shards(): key_peak = lax.pmax(local_peak, 'seq')]
    all_gather x2 -> x0, blocking collectives: 101 us -> none  [the longest x1 54.3 us: shards(): lax.all_gather(local_key_means, 'seq', axis=1, tiled=True)]
    all_to_all x0 -> x4, starting transfers between devices: none -> 50 us  [exchange(): return lax.all_to_all(blocks, axis, 0, 0, tiled=True)]
    ppermute x4 -> x18, starting transfers between devices: 15.8 us -> 64.4 us  [the longest x16 59 us: shift_by(): return lax.ppermute(block, ('seq', 'head'), pairs)]
  transfers between devices with their start and end apart: 9 -> 22, of which waited for: 4 -> 7; matrix products, arithmetic and copies ran while one was open for 9% -> 0% of each run, Pallas kernels for 0% -> 8%
where the time goes in v1:
time: 162 us; the launch traced here: 160 us
  starting transfers between devices  114 us (70%)
  Pallas kernels  17.1 us (11%)
  waiting for transfers between devices  16.2 us (10%)
  local copies, waits for them, and re-layouts  11.5 us (7%)
    ppermute x16, starting transfers between devices, shift_by(): return lax.ppermute(block, ('seq', 'head'), pairs)  59 us
    all_to_all x4, starting transfers between devices, exchange(): return lax.all_to_all(blocks, axis, 0, 0, tiled=True)  50 us
    pallas_call x11, Pallas kernels, call(): pl.pallas_call(kernel, out_shape=[jax.ShapeDtypeStruct(shape, kind) for s...  17.1 us
    ppermute x16, waiting for transfers between devices, shift_by(): return lax.ppermute(block, ('seq', 'head'), pairs)  12.2 us
    unnamed x57, local copies, waits for them, and re-layouts  10.7 us
    all_to_all x4, waiting for transfers between devices, exchange(): return lax.all_to_all(blocks, axis, 0, 0, tiled=True)  4.04 us
    ppermute x1, starting transfers between devices, shards(): above = lax.ppermute(last_rows, 'seq', [(i, i + 1) for i in range(ends)])  3.54 us
  transfers between devices with their start and end apart: 22, of which 7 were waited for; matrix products, arithmetic and copies ran while one was open for 0% of the time, Pallas kernels for 8%

profile of v1, /device:TPU:1, one launch (start us, length us, event | category | flops | bytes accessed | tf_op | source)
XLA Modules:
  0.0 160.5 jit_solution(3676745121453344065)
XLA Ops:
  0.6 0.8 copy-done.6
  1.5 0.8 copy-done.8
  2.3 0.8 shard_map.101
  3.1 15.0 %all-to-all-start = ((f32[64,8,128]{2,1,0:T(8,128)}), f32[64,8,128]{2,1,0:T(8,128)S(1)}, u32[]{:S(2)}, u32[]{:S(2)}) async-start(f32[64,8,128]{2,1,0:T(8,128)} %shard_map.101), calls=%async_computation | async-start | bytes 524288 | tf_op jit(solution)/shard_map/all_to_all | solution.py:416
  18.1 3.2 %collective-permute-start.6 = (bf16[256,256]{1,0:T(8,128)(2,1)S(1)}, bf16[256,256]{1,0:T(8,128)(2,1)S(1)}, u32[]{:S(2)}, u32[]{:S(2)}) collective-permute-start(bf16[256,256]{1,0:T(8,128)(2,1)S(1)} %bitcast.10), channel_id=1, source_target_pairs={{0,7},{1,0},{2,1},{3,2},{4,3},{5,4},{6,5},{7,6},{8,9},{9,10},{10,1... | collective-permute-start | bytes 393224 | tf_op jit(solution)/shard_map/ppermute | solution.py:424
  21.3 4.2 %collective-permute-start.5 = (bf16[256,256]{1,0:T(8,128)(2,1)S(1)}, bf16[256,256]{1,0:T(8,128)(2,1)S(1)}, u32[]{:S(2)}, u32[]{:S(2)}) collective-permute-start(bf16[256,256]{1,0:T(8,128)(2,1)S(1)} %bitcast.11), channel_id=1, source_target_pairs={{0,6},{1,7},{2,0},{3,1},{4,2},{5,3},{6,4},{7,5},{8,10},{9,11},{10,... | collective-permute-start | bytes 393224 | tf_op jit(solution)/shard_map/ppermute | solution.py:424
  25.5 4.6 %collective-permute-start.4 = (bf16[256,256]{1,0:T(8,128)(2,1)S(1)}, bf16[256,256]{1,0:T(8,128)(2,1)S(1)}, u32[]{:S(2)}, u32[]{:S(2)}) collective-permute-start(bf16[256,256]{1,0:T(8,128)(2,1)S(1)} %bitcast.12), channel_id=1, source_target_pairs={{0,5},{1,6},{2,7},{3,0},{4,1},{5,2},{6,3},{7,4},{8,11},{9,12},{10,... | collective-permute-start | bytes 393224 | tf_op jit(solution)/shard_map/ppermute | solution.py:424
  30.2 3.5 %collective-permute-start.3 = (bf16[256,256]{1,0:T(8,128)(2,1)S(1)}, bf16[256,256]{1,0:T(8,128)(2,1)S(1)}, u32[]{:S(2)}, u32[]{:S(2)}) collective-permute-start(bf16[256,256]{1,0:T(8,128)(2,1)S(1)} %bitcast.13), channel_id=1, source_target_pairs={{0,4},{1,5},{2,6},{3,7},{4,0},{5,1},{6,2},{7,3},{8,12},{9,13},{10,... | collective-permute-start | bytes 393224 | tf_op jit(solution)/shard_map/ppermute | solution.py:424
  33.7 4.9 %collective-permute-start.2 = (bf16[256,256]{1,0:T(8,128)(2,1)S(1)}, bf16[256,256]{1,0:T(8,128)(2,1)S(1)}, u32[]{:S(2)}, u32[]{:S(2)}) collective-permute-start(bf16[256,256]{1,0:T(8,128)(2,1)S(1)} %bitcast.14), channel_id=1, source_target_pairs={{0,3},{1,4},{2,5},{3,6},{4,7},{5,0},{6,1},{7,2},{8,13},{9,14},{10,... | collective-permute-start | bytes 393224 | tf_op jit(solution)/shard_map/ppermute | solution.py:424
  38.6 0.0 collective-permute-done.6.refs_7_
  38.6 5.0 %collective-permute-start.1 = (bf16[256,256]{1,0:T(8,128)(2,1)S(1)}, bf16[256,256]{1,0:T(8,128)(2,1)S(1)}, u32[]{:S(2)}, u32[]{:S(2)}) collective-permute-start(bf16[256,256]{1,0:T(8,128)(2,1)S(1)} %bitcast.15), channel_id=1, source_target_pairs={{0,2},{1,3},{2,4},{3,5},{4,6},{5,7},{6,0},{7,1},{8,14},{9,15},{10,... | collective-permute-start | bytes 393224 | tf_op jit(solution)/shard_map/ppermute | solution.py:424
  43.6 3.0 %collective-permute-start = (bf16[256,256]{1,0:T(8,128)(2,1)S(1)}, bf16[256,256]{1,0:T(8,128)(2,1)S(1)}, u32[]{:S(2)}, u32[]{:S(2)}) collective-permute-start(bf16[256,256]{1,0:T(8,128)(2,1)S(1)} %bitcast.16), channel_id=1, source_target_pairs={{0,1},{1,2},{2,3},{3,4},{4,5},{5,6},{6,7},{7,0},{8,15},{9,8},{10,9... | collective-permute-start | bytes 393224 | tf_op jit(solution)/shard_map/ppermute | solution.py:424
  46.6 0.0 all-to-all-done
  46.6 1.1 shard_map.102
  47.7 0.0 collective-permute-done.4.refs_5_
  47.7 0.5 collective-permute-done.2.refs_3_
  48.2 3.3 %collective-permute-done.1.refs_2_ = bf16[256,256]{1,0:T(8,128)(2,1)S(1)} collective-permute-done((bf16[256,256]{1,0:T(8,128)(2,1)S(1)}, bf16[256,256]{1,0:T(8,128)(2,1)S(1)}, u32[]{:S(2)}, u32[]{:S(2)}) %collective-permute-start.1) | collective-permute-done | bytes 131104 | tf_op jit(solution)/shard_map/ppermute | solution.py:424
  51.5 0.2 collective-permute-done.refs_1_
  51.7 1.8 %shard_map.103 = (f32[1024,128]{1,0:T(8,128)}, f32[2,128,128]{2,1,0:T(8,128)S(1)}, bf16[2,48,128]{2,1,0:T(8,128)(2,1)}, bf16[2,48,128]{2,1,0:T(8,128)(2,1)}, bf1...) custom-call(bf16[256,256]{1,0:T(8,128)(2,1)S(1)} %bitcast.17, ...), custom_call_target="tpu_custom_call" | custom-call | flops 100000000 | bytes 2000000 | tf_op jit(solution)/shard_map/pallas_call | solution.py:402
  53.5 0.7 copy-done.11
  54.2 12.0 %all-to-all-start.1 = ((f32[64,16,128]{2,1,0:T(8,128)}), f32[64,16,128]{2,1,0:T(8,128)S(1)}, u32[]{:S(2)}, u32[]{:S(2)}) async-start(f32[64,16,128]{2,1,0:T(8,128)} %bitcast.2), calls=%async_computation.1 | async-start | bytes 1048576 | tf_op jit(solution)/shard_map/all_to_all | solution.py:416
  66.2 3.5 %collective-permute-start.10 = (bf16[2,48,128]{2,1,0:T(8,128)(2,1)}, bf16[2,48,128]{2,1,0:T(8,128)(2,1)S(1)}, u32[]{:S(2)}, u32[]{:S(2)}) collective-permute-start(bf16[2,48,128]{2,1,0:T(8,128)(2,1)} %get-tuple-element.73), channel_id=1, source_target_pairs={{0,8},{8,16},{16,24},{24,32},{32,40},{40,48},{48,56},{56,64},{64,7... | collective-permute-start | bytes 73736 | tf_op jit(solution)/shard_map/ppermute | solution.py:474
  69.8 1.9 %collective-permute-start.11 = (bf16[2,48,128]{2,1,0:T(8,128)(2,1)}, bf16[2,48,128]{2,1,0:T(8,128)(2,1)S(1)}, u32[]{:S(2)}, u32[]{:S(2)}) collective-permute-start(bf16[2,48,128]{2,1,0:T(8,128)(2,1)} %get-tuple-element.74), channel_id=1, source_target_pairs={{8,0},{16,8},{24,16},{32,24},{40,32},{48,40},{56,48},{64,56},{72,6... | collective-permute-start | bytes 73736 | tf_op jit(solution)/shard_map/ppermute | solution.py:475
  71.7 4.0 %collective-permute-start.9 = (bf16[1,128,256]{2,1,0:T(8,128)(2,1)S(1)}, bf16[1,128,256]{2,1,0:T(8,128)(2,1)S(1)}, u32[]{:S(2)}, u32[]{:S(2)}) collective-permute-start(bf16[1,128,256]{2,1,0:T(8,128)(2,1)S(1)} %get-tuple-element.72), channel_id=1, source_target_pairs={{0,4},{1,5},{2,6},{3,7},{4,0},{5,1},{6,2},{7,3},{8,12},{9,13},{10,... | collective-permute-start | bytes 196616 | tf_op jit(solution)/shard_map/ppermute | solution.py:424
  75.8 2.6 %collective-permute-start.7 = (bf16[2,128,256]{2,1,0:T(8,128)(2,1)}, bf16[2,128,256]{2,1,0:T(8,128)(2,1)S(1)}, u32[]{:S(2)}, u32[]{:S(2)}) collective-permute-start(bf16[2,128,256]{2,1,0:T(8,128)(2,1)} %get-tuple-element.70), channel_id=1, source_target_pairs={{0,1},{1,2},{2,3},{3,4},{4,5},{5,6},{6,7},{7,0},{8,15},{9,8},{10,9... | collective-permute-start | bytes 393224 | tf_op jit(solution)/shard_map/ppermute | solution.py:424
  78.4 2.7 %collective-permute-start.8 = (bf16[2,128,256]{2,1,0:T(8,128)(2,1)}, bf16[2,128,256]{2,1,0:T(8,128)(2,1)S(1)}, u32[]{:S(2)}, u32[]{:S(2)}) collective-permute-start(bf16[2,128,256]{2,1,0:T(8,128)(2,1)} %get-tuple-element.71), channel_id=1, source_target_pairs={{0,7},{1,0},{2,1},{3,2},{4,3},{5,4},{6,5},{7,6},{8,9},{9,10},{10,1... | collective-permute-start | bytes 393224 | tf_op jit(solution)/shard_map/ppermute | solution.py:424
  81.1 2.2 %shard_map.104 = (bf16[2048,256]{1,0:T(8,128)(2,1)S(1)}, f32[4,128,128]{2,1,0:T(8,128)S(1)}, f32[2,4,128,128]{3,2,1,0:T(8,128)S(1)}, f32[2,4,128,128]{3,2,1,0:T(...) custom-call(bf16[256,256]{1,0:T(8,128)(2,1)S(1)} %bitcast.18, ...), custom_call_target="tpu_custom_call" | custom-call | flops 3000000000 | bytes 2000000 | tf_op jit(solution)/shard_map/pallas_call | solution.py:402
  83.2 1.0 copy-done.15
  84.3 0.8 copy-done.17
  85.0 0.8 copy-done.19
  85.8 0.8 copy-done.21
  86.6 0.8 copy-done.23
  87.4 0.7 copy-done.25
  88.1 0.0 collective-permute-done.9.refs_8_
  88.2 0.0 copy-start.1
  88.2 0.0 collective-permute-done.8.refs_7_
  88.2 1.0 shard_map.105
  89.2 13.3 %all-to-all-start.2 = ((f32[64,8,128]{2,1,0:T(8,128)}), f32[64,8,128]{2,1,0:T(8,128)S(1)}, u32[]{:S(2)}, u32[]{:S(2)}) async-start(f32[64,8,128]{2,1,0:T(8,128)} %get-tuple-element.83), calls=%async_computation.2 | async-start | bytes 524288 | tf_op jit(solution)/shard_map/all_to_all | solution.py:416
  102.5 0.0 slice-start
  102.6 0.8 slice-done
  103.4 1.9 %collective-permute-start.12 = (bf16[2,128,256]{2,1,0:T(8,128)(2,1)S(1)}, bf16[2,128,256]{2,1,0:T(8,128)(2,1)S(1)}, u32[]{:S(2)}, u32[]{:S(2)}) collective-permute-start(bf16[2,128,256]{2,1,0:T(8,128)(2,1)S(1)} %pad_maximum_fusion.1), channel_id=1, source_target_pairs={{0,2},{1,3},{2,4},{3,5},{4,6},{5,7},{6,0},{7,1},{8,14},{9,15},{10,... | collective-permute-start | bytes 393224 | tf_op jit(solution)/shard_map/ppermute | solution.py:424
  105.3 0.0 copy-start.27
  105.3 0.0 copy-start.14
  105.4 4.4 %collective-permute-start.13 = (bf16[2,128,256]{2,1,0:T(8,128)(2,1)S(1)}, bf16[2,128,256]{2,1,0:T(8,128)(2,1)S(1)}, u32[]{:S(2)}, u32[]{:S(2)}) collective-permute-start(bf16[2,128,256]{2,1,0:T(8,128)(2,1)S(1)} %pad_maximum_fusion.2), channel_id=1, source_target_pairs={{0,6},{1,7},{2,0},{3,1},{4,2},{5,3},{6,4},{7,5},{8,10},{9,11},{10,... | collective-permute-start | bytes 393224 | tf_op jit(solution)/shard_map/ppermute | solution.py:424
  109.8 0.1 copy.11.taps_ref
  109.9 1.5 shard_map.106
  111.4 0.0 collective-permute-done.12.refs_9_
  111.4 4.0 %collective-permute-done.13.refs_10_ = bf16[2,128,256]{2,1,0:T(8,128)(2,1)S(1)} collective-permute-done((bf16[2,128,256]{2,1,0:T(8,128)(2,1)S(1)}, bf16[2,128,256]{2,1,0:T(8,128)(2,1)S(1)}, u32[]{:S(2)}, u32[]{:S(2)}) %collective-permute-start.13) | collective-permute-done | bytes 131104 | tf_op jit(solution)/shard_map/ppermute | solution.py:424
  115.4 0.3 all-to-all-done.2
  115.7 0.6 shard_map.107
  116.2 2.6 %collective-permute-start.15 = (bf16[256,128]{1,0:T(8,128)(2,1)S(1)}, bf16[256,128]{1,0:T(8,128)(2,1)S(1)}, u32[]{:S(2)}, u32[]{:S(2)}) collective-permute-start(bf16[256,128]{1,0:T(8,128)(2,1)S(1)} %get-tuple-element.95.ctx_ref.refs_0_), channel_id=1, source_target_pairs={{0,7},{1,0},{2,1},{3,2},{4,3},{5,4},{6,5},{7,6},{8,9},{9,10},{10,1... | collective-permute-start | bytes 196616 | tf_op jit(solution)/shard_map/ppermute | solution.py:424
  118.9 3.9 %collective-permute-start.14 = (bf16[256,128]{1,0:T(8,128)(2,1)S(1)}, bf16[256,128]{1,0:T(8,128)(2,1)S(1)}, u32[]{:S(2)}, u32[]{:S(2)}) collective-permute-start(bf16[256,128]{1,0:T(8,128)(2,1)S(1)} %get-tuple-element.95.ctx_ref.refs_0_), channel_id=1, source_target_pairs={{0,1},{1,2},{2,3},{3,4},{4,5},{5,6},{6,7},{7,0},{8,15},{9,8},{10,9... | collective-permute-start | bytes 196616 | tf_op jit(solution)/shard_map/ppermute | solution.py:424
  122.8 1.2 copy-done.16
  124.0 3.3 %shard_map.108 = (bf16[64,48,128]{2,1,0:T(8,128)(2,1)}, f32[2,128,128]{2,1,0:T(8,128)S(1)}, f32[2,128,128]{2,1,0:T(8,128)S(1)}, bf16[2,128,128]{2,1,0:T(8,128)(2,1)}) custom-call(f32[8,128]{1,0:T(8,128)S(1)} %get-tuple-element.96.log_ref, f32[2,128,256]{2,1,0:T(8,128)S(1)} %get-tuple-element.66.refs_10_.t_ref, f32[2,128,256]{2,1,0:T(8,128)S(1)} %get-tuple-element.97.s_ref, ...), custom_call_target="tpu_custom_call" | custom-call | flops 1000000000 | bytes 2000000 | tf_op jit(solution)/shard_map/pallas_call | solution.py:402
  127.3 9.7 %all-to-all-start.3 = ((bf16[64,48,128]{2,1,0:T(8,128)(2,1)}), bf16[64,48,128]{2,1,0:T(8,128)(2,1)S(1)}, u32[]{:S(2)}, u32[]{:S(2)}) async-start(bf16[64,48,128]{2,1,0:T(8,128)(2,1)} %get-tuple-element.110), calls=%async_computation.3 | async-start | bytes 1572864 | tf_op jit(solution)/shard_map/all_to_all | solution.py:416
  137.0 5.8 %collective-permute-start.17 = (bf16[512,128]{1,0:T(8,128)(2,1)S(1)}, bf16[512,128]{1,0:T(8,128)(2,1)S(1)}, u32[]{:S(2)}, u32[]{:S(2)}) collective-permute-start(bf16[512,128]{1,0:T(8,128)(2,1)S(1)} %pad_maximum_fusion.3), channel_id=1, source_target_pairs={{0,5},{1,6},{2,7},{3,0},{4,1},{5,2},{6,3},{7,4},{8,11},{9,12},{10,... | collective-permute-start | bytes 393224 | tf_op jit(solution)/shard_map/ppermute | solution.py:424
  142.8 2.6 %collective-permute-start.16 = (bf16[768,128]{1,0:T(8,128)(2,1)S(1)}, bf16[768,128]{1,0:T(8,128)(2,1)S(1)}, u32[]{:S(2)}, u32[]{:S(2)}) collective-permute-start(bf16[768,128]{1,0:T(8,128)(2,1)S(1)} %pad_maximum_fusion), channel_id=1, source_target_pairs={{0,3},{1,4},{2,5},{3,6},{4,7},{5,0},{6,1},{7,2},{8,13},{9,14},{10,... | collective-permute-start | bytes 589832 | tf_op jit(solution)/shard_map/ppermute | solution.py:424
  145.5 1.0 copy-done.22
  146.5 1.0 copy-done.24
  147.6 3.1 %shard_map.110.own_ref = f32[8,128]{1,0:T(8,128)S(1)} custom-call(f32[4,128,128]{2,1,0:T(8,128)S(1)} %copy-done.26, f32[2,4,128,128]{3,2,1,0:T(8,128)S(1)} %copy-done.18, f32[2,4,128,128]{3,2,1,0:T(8,128)S(1)} %copy-done.20, f32[2,4,128,128]{3,2,1,0:T(8,128)S(1)} %copy-done.22, f32[2,4,128,128]{3,2,1,0:T(8,128)S(1)} %copy-done.24, ...), custom_call_target="tpu_custom_call" | custom-call | flops 5000000000 | bytes 2000000 | tf_op jit(solution)/shard_map/pallas_call | solution.py:402
  150.7 4.2 %collective-permute-done.16.refs_3_ = bf16[768,128]{1,0:T(8,128)(2,1)S(1)} collective-permute-done((bf16[768,128]{1,0:T(8,128)(2,1)S(1)}, bf16[768,128]{1,0:T(8,128)(2,1)S(1)}, u32[]{:S(2)}, u32[]{:S(2)}) %collective-permute-start.16) | collective-permute-done | bytes 196640 | tf_op jit(solution)/shard_map/ppermute | solution.py:424
  154.9 1.1 shard_map.109
  156.0 3.7 %all-to-all-done.3.got_ref = bf16[64,48,128]{2,1,0:T(8,128)(2,1)S(1)} async-done(((bf16[64,48,128]{2,1,0:T(8,128)(2,1)}), bf16[64,48,128]{2,1,0:T(8,128)(2,1)S(1)}, u32[]{:S(2)}, u32[]{:S(2)}) %all-to-all-start.3) | async-done | bytes 786464 | tf_op jit(solution)/shard_map/all_to_all | solution.py:416
  159.7 0.8 shard_map.111
  (57 shorter events, 0.2 us)
Async XLA Ops:
  0.6 0.8 copy-start.6
  1.5 0.8 copy-start.8
  2.3 15.7 %copy-start.10 = (bf16[2,128,256]{2,1,0:T(8,128)(2,1)S(1)}, bf16[2,128,256]{2,1,0:T(8,128)(2,1)}, u32[]{:S(2)}) copy-start(bf16[2,128,256]{2,1,0:T(8,128)(2,1)} %param.11) | copy-start | bytes 393220
  2.3 44.3 %copy-start.5 = (bf16[2,128,128]{2,1,0:T(8,128)(2,1)S(1)}, bf16[2,128,128]{2,1,0:T(8,128)(2,1)}, u32[]{:S(2)}) copy-start(bf16[2,128,128]{2,1,0:T(8,128)(2,1)} %v_ref.5) | copy-start | bytes 196612
  2.3 44.3 %copy-start.7 = (bf16[2,128,128]{2,1,0:T(8,128)(2,1)S(1)}, bf16[2,128,128]{2,1,0:T(8,128)(2,1)}, u32[]{:S(2)}) copy-start(bf16[2,128,128]{2,1,0:T(8,128)(2,1)} %q_ref.5) | copy-start | bytes 196612
  2.3 44.3 %copy-start.9 = (bf16[2,128,128]{2,1,0:T(8,128)(2,1)S(1)}, bf16[2,128,128]{2,1,0:T(8,128)(2,1)}, u32[]{:S(2)}) copy-start(bf16[2,128,128]{2,1,0:T(8,128)(2,1)} %k_ref.5) | copy-start | bytes 196612
  3.1 48.7 %copy-start = (bf16[128,2048]{1,0:T(8,128)(2,1)S(1)}, bf16[128,2048]{1,0:T(8,128)(2,1)}, u32[]{:S(2)}) copy-start(bf16[128,2048]{1,0:T(8,128)(2,1)} %refs_8_.1) | copy-start | bytes 1572868
  3.1 43.5 %all-to-all-start = ((f32[64,8,128]{2,1,0:T(8,128)}), f32[64,8,128]{2,1,0:T(8,128)S(1)}, u32[]{:S(2)}, u32[]{:S(2)}) async-start(f32[64,8,128]{2,1,0:T(8,128)} %shard_map.101), calls=%async_computation | async-start | bytes 524288 | tf_op jit(solution)/shard_map/all_to_all | solution.py:416
  18.1 20.5 %collective-permute-start.6 = (bf16[256,256]{1,0:T(8,128)(2,1)S(1)}, bf16[256,256]{1,0:T(8,128)(2,1)S(1)}, u32[]{:S(2)}, u32[]{:S(2)}) collective-permute-start(bf16[256,256]{1,0:T(8,128)(2,1)S(1)} %bitcast.10), channel_id=1, source_target_pairs={{0,7},{1,0},{2,1},{3,2},{4,3},{5,4},{6,5},{7,6},{8,9},{9,10},{10,1... | collective-permute-start | bytes 393224 | tf_op jit(solution)/shard_map/ppermute | solution.py:424
  21.3 22.3 %collective-permute-start.5 = (bf16[256,256]{1,0:T(8,128)(2,1)S(1)}, bf16[256,256]{1,0:T(8,128)(2,1)S(1)}, u32[]{:S(2)}, u32[]{:S(2)}) collective-permute-start(bf16[256,256]{1,0:T(8,128)(2,1)S(1)} %bitcast.11), channel_id=1, source_target_pairs={{0,6},{1,7},{2,0},{3,1},{4,2},{5,3},{6,4},{7,5},{8,10},{9,11},{10,... | collective-permute-start | bytes 393224 | tf_op jit(solution)/shard_map/ppermute | solution.py:424
  25.5 22.2 %collective-permute-start.4 = (bf16[256,256]{1,0:T(8,128)(2,1)S(1)}, bf16[256,256]{1,0:T(8,128)(2,1)S(1)}, u32[]{:S(2)}, u32[]{:S(2)}) collective-permute-start(bf16[256,256]{1,0:T(8,128)(2,1)S(1)} %bitcast.12), channel_id=1, source_target_pairs={{0,5},{1,6},{2,7},{3,0},{4,1},{5,2},{6,3},{7,4},{8,11},{9,12},{10,... | collective-permute-start | bytes 393224 | tf_op jit(solution)/shard_map/ppermute | solution.py:424
  30.2 17.6 %collective-permute-start.3 = (bf16[256,256]{1,0:T(8,128)(2,1)S(1)}, bf16[256,256]{1,0:T(8,128)(2,1)S(1)}, u32[]{:S(2)}, u32[]{:S(2)}) collective-permute-start(bf16[256,256]{1,0:T(8,128)(2,1)S(1)} %bitcast.13), channel_id=1, source_target_pairs={{0,4},{1,5},{2,6},{3,7},{4,0},{5,1},{6,2},{7,3},{8,12},{9,13},{10,... | collective-permute-start | bytes 393224 | tf_op jit(solution)/shard_map/ppermute | solution.py:424
  33.7 14.5 %collective-permute-start.2 = (bf16[256,256]{1,0:T(8,128)(2,1)S(1)}, bf16[256,256]{1,0:T(8,128)(2,1)S(1)}, u32[]{:S(2)}, u32[]{:S(2)}) collective-permute-start(bf16[256,256]{1,0:T(8,128)(2,1)S(1)} %bitcast.14), channel_id=1, source_target_pairs={{0,3},{1,4},{2,5},{3,6},{4,7},{5,0},{6,1},{7,2},{8,13},{9,14},{10,... | collective-permute-start | bytes 393224 | tf_op jit(solution)/shard_map/ppermute | solution.py:424
  38.6 13.0 %collective-permute-start.1 = (bf16[256,256]{1,0:T(8,128)(2,1)S(1)}, bf16[256,256]{1,0:T(8,128)(2,1)S(1)}, u32[]{:S(2)}, u32[]{:S(2)}) collective-permute-start(bf16[256,256]{1,0:T(8,128)(2,1)S(1)} %bitcast.15), channel_id=1, source_target_pairs={{0,2},{1,3},{2,4},{3,5},{4,6},{5,7},{6,0},{7,1},{8,14},{9,15},{10,... | collective-permute-start | bytes 393224 | tf_op jit(solution)/shard_map/ppermute | solution.py:424
  43.6 8.2 %collective-permute-start = (bf16[256,256]{1,0:T(8,128)(2,1)S(1)}, bf16[256,256]{1,0:T(8,128)(2,1)S(1)}, u32[]{:S(2)}, u32[]{:S(2)}) collective-permute-start(bf16[256,256]{1,0:T(8,128)(2,1)S(1)} %bitcast.16), channel_id=1, source_target_pairs={{0,1},{1,2},{2,3},{3,4},{4,5},{5,6},{6,7},{7,0},{8,15},{9,8},{10,9... | collective-permute-start | bytes 393224 | tf_op jit(solution)/shard_map/ppermute | solution.py:424
  53.5 0.7 copy-start.11
  54.2 34.0 %all-to-all-start.1 = ((f32[64,16,128]{2,1,0:T(8,128)}), f32[64,16,128]{2,1,0:T(8,128)S(1)}, u32[]{:S(2)}, u32[]{:S(2)}) async-start(f32[64,16,128]{2,1,0:T(8,128)} %bitcast.2), calls=%async_computation.1 | async-start | bytes 1048576 | tf_op jit(solution)/shard_map/all_to_all | solution.py:416
  66.2 21.9 %collective-permute-start.10 = (bf16[2,48,128]{2,1,0:T(8,128)(2,1)}, bf16[2,48,128]{2,1,0:T(8,128)(2,1)S(1)}, u32[]{:S(2)}, u32[]{:S(2)}) collective-permute-start(bf16[2,48,128]{2,1,0:T(8,128)(2,1)} %get-tuple-element.73), channel_id=1, source_target_pairs={{0,8},{8,16},{16,24},{24,32},{32,40},{40,48},{48,56},{56,64},{64,7... | collective-permute-start | bytes 73736 | tf_op jit(solution)/shard_map/ppermute | solution.py:474
  69.8 18.3 %collective-permute-start.11 = (bf16[2,48,128]{2,1,0:T(8,128)(2,1)}, bf16[2,48,128]{2,1,0:T(8,128)(2,1)S(1)}, u32[]{:S(2)}, u32[]{:S(2)}) collective-permute-start(bf16[2,48,128]{2,1,0:T(8,128)(2,1)} %get-tuple-element.74), channel_id=1, source_target_pairs={{8,0},{16,8},{24,16},{32,24},{40,32},{48,40},{56,48},{64,56},{72,6... | collective-permute-start | bytes 73736 | tf_op jit(solution)/shard_map/ppermute | solution.py:475
  71.7 16.4 %collective-permute-start.9 = (bf16[1,128,256]{2,1,0:T(8,128)(2,1)S(1)}, bf16[1,128,256]{2,1,0:T(8,128)(2,1)S(1)}, u32[]{:S(2)}, u32[]{:S(2)}) collective-permute-start(bf16[1,128,256]{2,1,0:T(8,128)(2,1)S(1)} %get-tuple-element.72), channel_id=1, source_target_pairs={{0,4},{1,5},{2,6},{3,7},{4,0},{5,1},{6,2},{7,3},{8,12},{9,13},{10,... | collective-permute-start | bytes 196616 | tf_op jit(solution)/shard_map/ppermute | solution.py:424
  75.8 12.4 %collective-permute-start.7 = (bf16[2,128,256]{2,1,0:T(8,128)(2,1)}, bf16[2,128,256]{2,1,0:T(8,128)(2,1)S(1)}, u32[]{:S(2)}, u32[]{:S(2)}) collective-permute-start(bf16[2,128,256]{2,1,0:T(8,128)(2,1)} %get-tuple-element.70), channel_id=1, source_target_pairs={{0,1},{1,2},{2,3},{3,4},{4,5},{5,6},{6,7},{7,0},{8,15},{9,8},{10,9... | collective-permute-start | bytes 393224 | tf_op jit(solution)/shard_map/ppermute | solution.py:424
  78.4 9.8 %collective-permute-start.8 = (bf16[2,128,256]{2,1,0:T(8,128)(2,1)}, bf16[2,128,256]{2,1,0:T(8,128)(2,1)S(1)}, u32[]{:S(2)}, u32[]{:S(2)}) collective-permute-start(bf16[2,128,256]{2,1,0:T(8,128)(2,1)} %get-tuple-element.71), channel_id=1, source_target_pairs={{0,7},{1,0},{2,1},{3,2},{4,3},{5,4},{6,5},{7,6},{8,9},{9,10},{10,1... | collective-permute-start | bytes 393224 | tf_op jit(solution)/shard_map/ppermute | solution.py:424
  83.2 1.0 copy-start.15
  84.2 0.8 copy-start.17
  85.0 0.8 copy-start.19
  85.8 0.8 copy-start.21
  86.6 0.8 copy-start.23
  87.4 0.7 copy-start.25
  88.1 1.0 copy-start.13
  88.2 14.4 %copy-start.1 = (bf16[2,128,256]{2,1,0:T(8,128)(2,1)}, bf16[2,128,256]{2,1,0:T(8,128)(2,1)S(1)}, u32[]{:S(2)}) copy-start(bf16[2,128,256]{2,1,0:T(8,128)(2,1)S(1)} %collective-permute-done.7.refs_6_) | copy-start | bytes 393220
  88.2 14.3 %copy-start.3 = (bf16[2,128,256]{2,1,0:T(8,128)(2,1)}, bf16[2,128,256]{2,1,0:T(8,128)(2,1)S(1)}, u32[]{:S(2)}) copy-start(bf16[2,128,256]{2,1,0:T(8,128)(2,1)S(1)} %collective-permute-done.8.refs_7_) | copy-start | bytes 393220
  89.2 26.5 %all-to-all-start.2 = ((f32[64,8,128]{2,1,0:T(8,128)}), f32[64,8,128]{2,1,0:T(8,128)S(1)}, u32[]{:S(2)}, u32[]{:S(2)}) async-start(f32[64,8,128]{2,1,0:T(8,128)} %get-tuple-element.83), calls=%async_computation.2 | async-start | bytes 524288 | tf_op jit(solution)/shard_map/all_to_all | solution.py:416
  102.5 0.8 slice-start
  103.4 1.9 %slice-start.1 = ((bf16[2,128,256]{2,1,0:T(8,128)(2,1)}), bf16[1,128,256]{2,1,0:T(8,128)(2,1)S(1)}, s32[]{:S(2)}) async-start(bf16[2,128,256]{2,1,0:T(8,128)(2,1)} %copy-done.3), calls=%async_computation.5 | async-start | bytes 131072 | tf_op jit(solution)/shard_map/slice | solution.py:505
  103.4 8.0 %collective-permute-start.12 = (bf16[2,128,256]{2,1,0:T(8,128)(2,1)S(1)}, bf16[2,128,256]{2,1,0:T(8,128)(2,1)S(1)}, u32[]{:S(2)}, u32[]{:S(2)}) collective-permute-start(bf16[2,128,256]{2,1,0:T(8,128)(2,1)S(1)} %pad_maximum_fusion.1), channel_id=1, source_target_pairs={{0,2},{1,3},{2,4},{3,5},{4,6},{5,7},{6,0},{7,1},{8,14},{9,15},{10,... | collective-permute-start | bytes 393224 | tf_op jit(solution)/shard_map/ppermute | solution.py:424
  105.3 4.5 %copy-start.27 = (f32[33,2]{0,1:T(2,128)S(1)}, f32[33,2]{0,1:T(2,128)}, u32[]{:S(2)}) copy-start(f32[33,2]{0,1:T(2,128)} %param.9) | copy-start | bytes 796
  105.3 4.6 %copy-start.12 = (f32[2,128,128]{2,1,0:T(8,128)S(1)}, f32[2,128,128]{2,1,0:T(8,128)}, u32[]{:S(2)}) copy-start(f32[2,128,128]{2,1,0:T(8,128)} %copy-done.11) | copy-start | bytes 393220
  105.3 4.6 %copy-start.14 = (bf16[2,48,128]{2,1,0:T(8,128)(2,1)S(1)}, bf16[2,48,128]{2,1,0:T(8,128)(2,1)}, u32[]{:S(2)}) copy-start(bf16[2,48,128]{2,1,0:T(8,128)(2,1)} %copy-done.13) | copy-start | bytes 73732
  105.4 10.0 %collective-permute-start.13 = (bf16[2,128,256]{2,1,0:T(8,128)(2,1)S(1)}, bf16[2,128,256]{2,1,0:T(8,128)(2,1)S(1)}, u32[]{:S(2)}, u32[]{:S(2)}) collective-permute-start(bf16[2,128,256]{2,1,0:T(8,128)(2,1)S(1)} %pad_maximum_fusion.2), channel_id=1, source_target_pairs={{0,6},{1,7},{2,0},{3,1},{4,2},{5,3},{6,4},{7,5},{8,10},{9,11},{10,... | collective-permute-start | bytes 393224 | tf_op jit(solution)/shard_map/ppermute | solution.py:424
  116.2 11.0 %collective-permute-start.15 = (bf16[256,128]{1,0:T(8,128)(2,1)S(1)}, bf16[256,128]{1,0:T(8,128)(2,1)S(1)}, u32[]{:S(2)}, u32[]{:S(2)}) collective-permute-start(bf16[256,128]{1,0:T(8,128)(2,1)S(1)} %get-tuple-element.95.ctx_ref.refs_0_), channel_id=1, source_target_pairs={{0,7},{1,0},{2,1},{3,2},{4,3},{5,4},{6,5},{7,6},{8,9},{9,10},{10,1... | collective-permute-start | bytes 196616 | tf_op jit(solution)/shard_map/ppermute | solution.py:424
  118.9 8.4 %collective-permute-start.14 = (bf16[256,128]{1,0:T(8,128)(2,1)S(1)}, bf16[256,128]{1,0:T(8,128)(2,1)S(1)}, u32[]{:S(2)}, u32[]{:S(2)}) collective-permute-start(bf16[256,128]{1,0:T(8,128)(2,1)S(1)} %get-tuple-element.95.ctx_ref.refs_0_), channel_id=1, source_target_pairs={{0,1},{1,2},{2,3},{3,4},{4,5},{5,6},{6,7},{7,0},{8,15},{9,8},{10,9... | collective-permute-start | bytes 196616 | tf_op jit(solution)/shard_map/ppermute | solution.py:424
  122.8 1.2 copy-start.16
  127.3 18.2 %copy-start.20 = (f32[2,4,128,128]{3,2,1,0:T(8,128)S(1)}, f32[2,4,128,128]{3,2,1,0:T(8,128)}, u32[]{:S(2)}) copy-start(f32[2,4,128,128]{3,2,1,0:T(8,128)} %copy-done.19) | copy-start | bytes 1572868
  127.3 18.2 %copy-start.26 = (f32[4,128,128]{2,1,0:T(8,128)S(1)}, f32[4,128,128]{2,1,0:T(8,128)}, u32[]{:S(2)}) copy-start(f32[4,128,128]{2,1,0:T(8,128)} %copy-done.25) | copy-start | bytes 786436
  127.3 32.4 %all-to-all-start.3 = ((bf16[64,48,128]{2,1,0:T(8,128)(2,1)}), bf16[64,48,128]{2,1,0:T(8,128)(2,1)S(1)}, u32[]{:S(2)}, u32[]{:S(2)}) async-start(bf16[64,48,128]{2,1,0:T(8,128)(2,1)} %get-tuple-element.110), calls=%async_computation.3 | async-start | bytes 1572864 | tf_op jit(solution)/shard_map/all_to_all | solution.py:416
  136.9 8.5 %copy-start.18 = (f32[2,4,128,128]{3,2,1,0:T(8,128)S(1)}, f32[2,4,128,128]{3,2,1,0:T(8,128)}, u32[]{:S(2)}) copy-start(f32[2,4,128,128]{3,2,1,0:T(8,128)} %copy-done.17) | copy-start | bytes 1572868
  137.0 13.7 %collective-permute-start.17 = (bf16[512,128]{1,0:T(8,128)(2,1)S(1)}, bf16[512,128]{1,0:T(8,128)(2,1)S(1)}, u32[]{:S(2)}, u32[]{:S(2)}) collective-permute-start(bf16[512,128]{1,0:T(8,128)(2,1)S(1)} %pad_maximum_fusion.3), channel_id=1, source_target_pairs={{0,5},{1,6},{2,7},{3,0},{4,1},{5,2},{6,3},{7,4},{8,11},{9,12},{10,... | collective-permute-start | bytes 393224 | tf_op jit(solution)/shard_map/ppermute | solution.py:424
  142.8 12.1 %collective-permute-start.16 = (bf16[768,128]{1,0:T(8,128)(2,1)S(1)}, bf16[768,128]{1,0:T(8,128)(2,1)S(1)}, u32[]{:S(2)}, u32[]{:S(2)}) collective-permute-start(bf16[768,128]{1,0:T(8,128)(2,1)S(1)} %pad_maximum_fusion), channel_id=1, source_target_pairs={{0,3},{1,4},{2,5},{3,6},{4,7},{5,0},{6,1},{7,2},{8,13},{9,14},{10,... | collective-permute-start | bytes 589832 | tf_op jit(solution)/shard_map/ppermute | solution.py:424
  145.5 1.0 copy-start.22
  146.5 1.0 copy-start.24
  147.6 7.3 %copy-start.2 = (bf16[2,128,256]{2,1,0:T(8,128)(2,1)S(1)}, bf16[2,128,256]{2,1,0:T(8,128)(2,1)}, u32[]{:S(2)}) copy-start(bf16[2,128,256]{2,1,0:T(8,128)(2,1)} %copy-done.1) | copy-start | bytes 393220
  147.6 7.3 %copy-start.4 = (bf16[2,128,256]{2,1,0:T(8,128)(2,1)S(1)}, bf16[2,128,256]{2,1,0:T(8,128)(2,1)}, u32[]{:S(2)}) copy-start(bf16[2,128,256]{2,1,0:T(8,128)(2,1)} %copy-done.3) | copy-start | bytes 393220

commit v2 on v1

--- a/solution.py
+++ b/solution.py
@@ -154,47 +154,70 @@
         )
 
 
-def newton_kernel(scale, parts, *refs):
-    og_refs = refs[:parts]
-    qm_ref, km_ref, ogt_ref, a_ref, z_ref, p_ref, f2_ref, f3_ref, inv_ref = refs[parts:]
-    documents, count, _ = qm_ref.shape
-    width = og_refs[0].shape[1]
-    for shift in range(parts):
-        block = block_at(shift, parts)
-        ogt_ref[pl.ds(pl.multiple_of(block * width, width), width), :] = og_refs[shift][...].T
-    row = lax.broadcasted_iota(jnp.int32, (count, count), 0)
-    identity = (row == lax.broadcasted_iota(jnp.int32, (count, count), 1)).astype(f32)
+def landmark_units(scale, qm_ref, km_ref):
+    count = qm_ref.shape[1]
     units = []
-    for doc in range(documents):
+    for doc in range(qm_ref.shape[0]):
         scores = prod(stack(qm_ref[doc]), km_ref[doc], NT) * scale
         scores = jnp.exp(scores - jnp.max(scores, axis=1, keepdims=True))
         scores = scores / jnp.sum(scores, axis=1, keepdims=True)
         units += [scores[:count], scores[count:]]
-    approx = []
-    for index, unit in enumerate(units):
-        a_ref[index] = unit
-        sums = jnp.sum(unit, axis=0, keepdims=True)
-        approx.append(unit.T / jnp.max(sums, axis=1, keepdims=True))
+    return units
+
+
+def column_peak(unit):
+    return jnp.max(jnp.sum(unit, axis=0, keepdims=True), axis=1, keepdims=True)
+
+
+def newton(units, keep):
+    every = range(len(units))
+    count = units[0].shape[0]
+    row = lax.broadcasted_iota(jnp.int32, (count, count), 0)
+    identity = (row == lax.broadcasted_iota(jnp.int32, (count, count), 1)).astype(f32)
+    approx = [unit.T / column_peak(unit) for unit in units]
     units = [halves(unit) for unit in units]
-    every = range(len(units))
     for step in range(ITERS):
-        for i in every:
-            z_ref[step, i] = approx[i]
         spread = [halves(approx[i]) for i in every]
         product = [prod(units[i], spread[i]) for i in every]
+        first = [7.0 * identity - product[i] for i in every]
+        split = [halves(product[i]) for i in every]
+        second = [15.0 * identity - prod(split[i], first[i]) for i in every]
+        third = [13.0 * identity - prod(split[i], second[i]) for i in every]
         for i in every:
-            p_ref[step, i] = product[i]
-        factor = [7.0 * identity - product[i] for i in every]
-        product = [halves(product[i]) for i in every]
-        factor = [15.0 * identity - prod(product[i], factor[i]) for i in every]
-        for i in every:
-            f2_ref[step, i] = factor[i]
-        factor = [13.0 * identity - prod(product[i], factor[i]) for i in every]
-        for i in every:
-            f3_ref[step, i] = factor[i]
-        approx = [0.25 * prod(spread[i], factor[i]) for i in every]
-    for i in every:
-        inv_ref[i] = approx[i]
+            keep(step, i, (approx[i], product[i], first[i], second[i], third[i]))
+        if step < ITERS - 1 or not keep.last:
+            approx = [0.25 * prod(spread[i], third[i]) for i in every]
+    return approx
+
+
+class Nothing:
+    last = False
+
+    def __call__(self, step, index, values):
+        pass
+
+
+class Kept:
+    last = True
+
+    def __init__(self, refs):
+        self.refs = refs
+
+    def __call__(self, step, index, values):
+        for ref, value in zip(self.refs, values):
+            ref[step, index] = value.T
+
+
+def inverse_kernel(scale, qm_ref, km_ref, inv_ref):
+    for index, unit in enumerate(newton(landmark_units(scale, qm_ref, km_ref), Nothing())):
+        inv_ref[index] = unit
+
+
+def turn_kernel(parts, *refs):
+    width = refs[0].shape[1]
+    for shift in range(parts):
+        start = pl.multiple_of(block_at(shift, parts) * width, width)
+        refs[parts][pl.ds(start, width), :] = refs[shift][...].T
 
 
 def combine_kernel(got_ref, out_ref, log_ref):
@@ -318,36 +341,32 @@
     out_ref[:, 16:, :] = terms.reshape(groups, terms.shape[0] // groups, channels)
 
 
-def newton_back_kernel(
-    scale, a_ref, z_ref, p_ref, f2_ref, f3_ref, qm_ref, km_ref, mixed_ref, mix_ref, out_ref, held
-):
+def newton_back_kernel(scale, qm_ref, km_ref, mixed_ref, mix_ref, out_ref, held, *kept):
     documents, count, channels = qm_ref.shape
     me = lax.axis_index("seq")
     groups = count // SEGS
-    row = lax.broadcasted_iota(jnp.int32, (count, count), 0)
-    identity = (row == lax.broadcasted_iota(jnp.int32, (count, count), 1)).astype(f32)
     every = range(documents * 2)
+    units = landmark_units(scale, qm_ref, km_ref)
+    newton(units, Kept(kept))
+    approx_t, product_t, first_t, second_t, third_t = kept
     down = []
     for doc in range(documents):
         full = prod(stack(mix_ref[doc]), mixed_ref[doc], NT)
         down += [full[:count], full[count:]]
-    unit_t = [halves(a_ref[i].T) for i in every]
+    unit_t = [halves(units[i].T) for i in every]
     grads = [None for i in every]
     for step in reversed(range(ITERS)):
         down = [halves(0.25 * down[i]) for i in every]
-        turned = [halves(z_ref[step, i].T) for i in every]
-        product = [p_ref[step, i] for i in every]
-        product_t = [halves(product[i].T) for i in every]
+        turned = [halves(approx_t[step, i]) for i in every]
+        product = [halves(product_t[step, i]) for i in every]
         third = [prod(turned[i], down[i]) for i in every]
         third = [halves(third[i]) for i in every]
-        carry = [prod(down[i], f3_ref[step, i].T) for i in every]
-        second = [-prod(product_t[i], third[i]) for i in every]
+        carry = [prod(down[i], third_t[step, i]) for i in every]
+        second = [-prod(product[i], third[i]) for i in every]
         second = [halves(second[i]) for i in every]
-        first = [-prod(product_t[i], second[i]) for i in every]
+        first = [-prod(product[i], second[i]) for i in every]
         flow = [
-            -first[i]
-            - prod(third[i], f2_ref[step, i].T)
-            - prod(second[i], (7.0 * identity - product[i]).T)
+            -first[i] - prod(third[i], second_t[step, i]) - prod(second[i], first_t[step, i])
             for i in every
         ]
         flow = [halves(flow[i]) for i in every]
@@ -358,9 +377,8 @@
         back, turned = [], []
         for head in range(2):
             i = doc * 2 + head
-            unit = a_ref[i]
-            peak = jnp.max(jnp.sum(unit, axis=0, keepdims=True), axis=1, keepdims=True)
-            grad = grads[i] + down[i].T / peak
+            unit = units[i]
+            grad = grads[i] + down[i].T / column_peak(unit)
             part = unit * grad
             part = (part - unit * jnp.sum(part, axis=1, keepdims=True)) * scale
             back.append(part)
@@ -425,7 +443,10 @@
 
 
 def gathered(block, parts):
-    return [block] + [shift_by(block, shift, parts) for shift in range(1, parts)]
+    two, back_two = shift_by(block, 2, parts), shift_by(block, parts - 2, parts)
+    one, back_one = shift_by(block, 1, parts), shift_by(block, parts - 1, parts)
+    three, back_three = shift_by(two, 1, parts), shift_by(back_two, parts - 1, parts)
+    return [block, one, two, three, shift_by(two, 2, parts), back_three, back_two, back_one]
 
 
 def shards(queries, key_vectors, value_vectors, conv_taps, out_weight, out_grad):
@@ -462,6 +483,10 @@
         ],
         got, queries, key_vectors, value_vectors,
     )
+    (inverse,) = call(
+        functools.partial(inverse_kernel, scale), [((units, count, count), f32)], qm, km, flops=2e9
+    )
+    og_parts, inverse = lax.optimization_barrier((og_parts, inverse))
     sent, context_grad, first_rows, last_rows, *pieces = call(
         functools.partial(chunk_kernel, parts, rim),
         [((groups * 16, channels), f32), (rows_shape, f32)]
@@ -477,21 +502,16 @@
     up = shift_by(up, 1, parts)
     down = shift_by(down, parts - 1, parts)
     across = shift_by(across, 4, parts)
-    og_turned, a, z, p, f2, f3, inverse = call(
-        functools.partial(newton_kernel, scale, parts),
-        [((model_width, documents * tokens), bf16), ((units, count, count), f32)]
-        + [(saved, f32)] * 4
-        + [((units, count, count), f32)],
-        *og_parts, qm, km,
-        flops=3e9,
-    )
-    got, up, down, across, above, below, inverse = lax.optimization_barrier(
-        (got, up, down, across, above, below, inverse)
+    got, up, down, across, above, below = lax.optimization_barrier(
+        (got, up, down, across, above, below)
     )
     sent, logs = call(
         combine_kernel, [((groups, 8, channels), f32), ((8, count), f32)], got
     )
-    sent, up, down, stay = lax.optimization_barrier((sent, up, down, stay))
+    sent, up, down, stay, og_parts = lax.optimization_barrier((sent, up, down, stay, og_parts))
+    (og_turned,) = call(
+        functools.partial(turn_kernel, parts), [((model_width, documents * tokens), bf16)], *og_parts
+    )
     got = exchange(sent, "seq").reshape(groups * 8, channels)
     conv, back = call(
         conv_kernel,
@@ -503,8 +523,8 @@
     )
     up_two = shift_by(jnp.concatenate([stay[0:1], up[1:2]], axis=0), 2, parts)
     down_two = shift_by(jnp.concatenate([stay[1:2], down[1:2]], axis=0), parts - 2, parts)
-    got, up_two, down_two, conv, back = lax.optimization_barrier(
-        (got, up_two, down_two, conv, back)
+    got, up_two, down_two, conv, back, og_turned = lax.optimization_barrier(
+        (got, up_two, down_two, conv, back, og_turned)
     )
     weight_parts = [kept, up, down, across, up_two, down_two]
     context_b, mixed, mix, landmark_mix = call(
@@ -540,8 +560,8 @@
     (own,) = call(
         functools.partial(newton_back_kernel, scale),
         [((8, channels), f32)],
-        a, z, p, f2, f3, qm, km, mixed, mix,
-        scratch=[pltpu.VMEM((2 * documents, count, channels), f32)],
+        qm, km, mixed, mix,
+        scratch=[pltpu.VMEM((2 * documents, count, channels), f32)] + [pltpu.VMEM(saved, f32)] * 5,
         flops=5e9,
     )
     blocks = ((0, 0), (1, 0), (3, 2), (3, 1), (3, 0), (4, 1), (4, 0), (2, 0))

time: 162 us -> 154 us (0.951)
  local copies, waits for them, and re-layouts: 11.5 us -> 5.28 us
  waiting for transfers between devices: 16.2 us -> 13.7 us
  Pallas kernels: 17.1 us -> 19.1 us
    ppermute x16, waiting for transfers between devices: 12.2 us -> 3.46 us  [shift_by(): return lax.ppermute(block, ('seq', 'head'), pairs)]
    unnamed x57 -> x59, local copies, waits for them, and re-layouts: 10.7 us -> 4.45 us
    ppermute x16, starting transfers between devices: 59 us -> 55.7 us  [shift_by(): return lax.ppermute(block, ('seq', 'head'), pairs)]
    ppermute x1, waiting for transfers between devices: 0.01 us -> 3.21 us  [shards(): below = lax.ppermute(first_rows, 'seq', [(i + 1, i) for i in range(ends)])]
    all_to_all x4, waiting for transfers between devices: 4.04 us -> 7.07 us  [exchange(): return lax.all_to_all(blocks, axis, 0, 0, tiled=True)]
    pallas_call x11 -> x12, Pallas kernels: 17.1 us -> 19.1 us  [call(): pl.pallas_call(kernel, out_shape=[jax.ShapeDtypeStruct(shape, kind) for s...]
    ppermute x1, starting transfers between devices: 3.54 us -> 5.25 us  [shards(): above = lax.ppermute(last_rows, 'seq', [(i, i + 1) for i in range(ends)])]
  transfers between devices with their start and end apart: 22 -> 22, of which waited for: 7 -> 4; matrix products, arithmetic and copies ran while one was open for 0% -> 1% of each run, Pallas kernels for 8% -> 9%
where the time goes in v2:
time: 154 us; the launch traced here: 153 us
  starting transfers between devices  113 us (73%)
  Pallas kernels  19.1 us (12%)
  waiting for transfers between devices  13.7 us (9%)
  local copies, waits for them, and re-layouts  5.28 us (3%)
    ppermute x16, starting transfers between devices, shift_by(): return lax.ppermute(block, ('seq', 'head'), pairs)  55.7 us
    all_to_all x4, starting transfers between devices, exchange(): return lax.all_to_all(blocks, axis, 0, 0, tiled=True)  49.7 us
    pallas_call x12, Pallas kernels, call(): pl.pallas_call(kernel, out_shape=[jax.ShapeDtypeStruct(shape, kind) for s...  19.1 us
    all_to_all x4, waiting for transfers between devices, exchange(): return lax.all_to_all(blocks, axis, 0, 0, tiled=True)  7.07 us
    ppermute x1, starting transfers between devices, shards(): above = lax.ppermute(last_rows, 'seq', [(i, i + 1) for i in range(ends)])  5.25 us
    unnamed x59, local copies, waits for them, and re-layouts  4.45 us
    ppermute x16, waiting for transfers between devices, shift_by(): return lax.ppermute(block, ('seq', 'head'), pairs)  3.46 us
    ppermute x1, waiting for transfers between devices, shards(): below = lax.ppermute(first_rows, 'seq', [(i + 1, i) for i in range(ends)])  3.21 us
  transfers between devices with their start and end apart: 22, of which 4 were waited for; matrix products, arithmetic and copies ran while one was open for 1% of the time, Pallas kernels for 9%

profile of v2, /device:TPU:1, one launch (start us, length us, event | category | flops | bytes accessed | tf_op | source)
XLA Modules:
  0.0 153.3 jit_solution(10626412849281361644)
XLA Ops:
  0.6 0.0 copy-start.7
  0.6 0.8 copy-done.7
  1.5 0.8 copy-done.9
  2.3 0.8 shard_map.101
  3.1 15.0 %all-to-all-start = ((f32[64,8,128]{2,1,0:T(8,128)}), f32[64,8,128]{2,1,0:T(8,128)S(1)}, u32[]{:S(2)}, u32[]{:S(2)}) async-start(f32[64,8,128]{2,1,0:T(8,128)} %shard_map.101), calls=%async_computation | async-start | bytes 524288 | tf_op jit(solution)/shard_map/all_to_all | solution.py:434
  18.1 5.9 %collective-permute-start.1 = (bf16[256,256]{1,0:T(8,128)(2,1)S(1)}, bf16[256,256]{1,0:T(8,128)(2,1)S(1)}, u32[]{:S(2)}, u32[]{:S(2)}) collective-permute-start(bf16[256,256]{1,0:T(8,128)(2,1)S(1)} %bitcast.10), channel_id=1, source_target_pairs={{0,2},{1,3},{2,4},{3,5},{4,6},{5,7},{6,0},{7,1},{8,14},{9,15},{10,... | collective-permute-start | bytes 393224 | tf_op jit(solution)/shard_map/ppermute | solution.py:442
  24.0 1.9 %collective-permute-start.4 = (bf16[256,256]{1,0:T(8,128)(2,1)S(1)}, bf16[256,256]{1,0:T(8,128)(2,1)S(1)}, u32[]{:S(2)}, u32[]{:S(2)}) collective-permute-start(bf16[256,256]{1,0:T(8,128)(2,1)S(1)} %bitcast.11), channel_id=1, source_target_pairs={{0,6},{1,7},{2,0},{3,1},{4,2},{5,3},{6,4},{7,5},{8,10},{9,11},{10,... | collective-permute-start | bytes 393224 | tf_op jit(solution)/shard_map/ppermute | solution.py:442
  25.9 2.3 %collective-permute-start.6 = (bf16[256,256]{1,0:T(8,128)(2,1)S(1)}, bf16[256,256]{1,0:T(8,128)(2,1)S(1)}, u32[]{:S(2)}, u32[]{:S(2)}) collective-permute-start(bf16[256,256]{1,0:T(8,128)(2,1)S(1)} %bitcast.12), channel_id=1, source_target_pairs={{0,7},{1,0},{2,1},{3,2},{4,3},{5,4},{6,5},{7,6},{8,9},{9,10},{10,1... | collective-permute-start | bytes 393224 | tf_op jit(solution)/shard_map/ppermute | solution.py:442
  28.2 4.3 %collective-permute-start = (bf16[256,256]{1,0:T(8,128)(2,1)S(1)}, bf16[256,256]{1,0:T(8,128)(2,1)S(1)}, u32[]{:S(2)}, u32[]{:S(2)}) collective-permute-start(bf16[256,256]{1,0:T(8,128)(2,1)S(1)} %bitcast.13), channel_id=1, source_target_pairs={{0,1},{1,2},{2,3},{3,4},{4,5},{5,6},{6,7},{7,0},{8,15},{9,8},{10,9... | collective-permute-start | bytes 393224 | tf_op jit(solution)/shard_map/ppermute | solution.py:442
  32.5 0.0 collective-permute-done.1.refs_2_
  32.5 4.1 %collective-permute-start.3 = (bf16[256,256]{1,0:T(8,128)(2,1)S(1)}, bf16[256,256]{1,0:T(8,128)(2,1)S(1)}, u32[]{:S(2)}, u32[]{:S(2)}) collective-permute-start(bf16[256,256]{1,0:T(8,128)(2,1)S(1)} %collective-permute-done.1.refs_2_), channel_id=1, source_target_pairs={{0,2},{1,3},{2,4},{3,5},{4,6},{5,7},{6,0},{7,1},{8,14},{9,15},{10,... | collective-permute-start | bytes 393224 | tf_op jit(solution)/shard_map/ppermute | solution.py:442
  36.7 1.9 %collective-permute-start.2 = (bf16[256,256]{1,0:T(8,128)(2,1)S(1)}, bf16[256,256]{1,0:T(8,128)(2,1)S(1)}, u32[]{:S(2)}, u32[]{:S(2)}) collective-permute-start(bf16[256,256]{1,0:T(8,128)(2,1)S(1)} %collective-permute-done.1.refs_2_), channel_id=1, source_target_pairs={{0,1},{1,2},{2,3},{3,4},{4,5},{5,6},{6,7},{7,0},{8,15},{9,8},{10,9... | collective-permute-start | bytes 393224 | tf_op jit(solution)/shard_map/ppermute | solution.py:442
  38.6 0.0 collective-permute-done.4.refs_6_
  38.6 3.4 %collective-permute-start.5 = (bf16[256,256]{1,0:T(8,128)(2,1)S(1)}, bf16[256,256]{1,0:T(8,128)(2,1)S(1)}, u32[]{:S(2)}, u32[]{:S(2)}) collective-permute-start(bf16[256,256]{1,0:T(8,128)(2,1)S(1)} %collective-permute-done.4.refs_6_), channel_id=1, source_target_pairs={{0,7},{1,0},{2,1},{3,2},{4,3},{5,4},{6,5},{7,6},{8,9},{9,10},{10,1... | collective-permute-start | bytes 393224 | tf_op jit(solution)/shard_map/ppermute | solution.py:442
  42.0 0.0 all-to-all-done
  42.0 1.1 shard_map.102
  43.2 0.7 copy-done.11
  43.8 2.2 %shard_map.103.inv_ref = f32[4,128,128]{2,1,0:T(8,128)S(1)} custom-call(f32[2,128,128]{2,1,0:T(8,128)S(1)} %get-tuple-element.76.qm_ref, f32[2,128,128]{2,1,0:T(8,128)S(1)} %get-tuple-element.77.km_ref), custom_call_target="tpu_custom_call" | custom-call | flops 2000000000 | bytes 2000000 | tf_op jit(solution)/shard_map/pallas_call | solution.py:420
  46.0 0.0 collective-permute-done.6.refs_7_
  46.0 0.0 collective-permute-done.refs_1_
  46.1 0.0 collective-permute-done.3.refs_4_
  46.1 0.0 collective-permute-done.2.refs_3_
  46.1 1.8 %shard_map.104 = (f32[1024,128]{1,0:T(8,128)}, f32[2,128,128]{2,1,0:T(8,128)S(1)}, bf16[2,48,128]{2,1,0:T(8,128)(2,1)S(1)}, bf16[2,48,128]{2,1,0:T(8,128)(2,1)S(...) custom-call(bf16[256,256]{1,0:T(8,128)(2,1)S(1)} %bitcast.14, ...), custom_call_target="tpu_custom_call" | custom-call | flops 100000000 | bytes 2000000 | tf_op jit(solution)/shard_map/pallas_call | solution.py:420
  47.9 0.7 copy-done.19
  48.5 11.8 %all-to-all-start.1 = ((f32[64,16,128]{2,1,0:T(8,128)}), f32[64,16,128]{2,1,0:T(8,128)S(1)}, u32[]{:S(2)}, u32[]{:S(2)}) async-start(f32[64,16,128]{2,1,0:T(8,128)} %bitcast.2), calls=%async_computation.1 | async-start | bytes 1048576 | tf_op jit(solution)/shard_map/all_to_all | solution.py:434
  60.3 3.4 %collective-permute-start.7 = (bf16[2,128,256]{2,1,0:T(8,128)(2,1)S(1)}, bf16[2,128,256]{2,1,0:T(8,128)(2,1)S(1)}, u32[]{:S(2)}, u32[]{:S(2)}) collective-permute-start(bf16[2,128,256]{2,1,0:T(8,128)(2,1)S(1)} %get-tuple-element.90), channel_id=1, source_target_pairs={{0,1},{1,2},{2,3},{3,4},{4,5},{5,6},{6,7},{7,0},{8,15},{9,8},{10,9... | collective-permute-start | bytes 393224 | tf_op jit(solution)/shard_map/ppermute | solution.py:442
  63.7 2.2 %collective-permute-start.8 = (bf16[2,128,256]{2,1,0:T(8,128)(2,1)S(1)}, bf16[2,128,256]{2,1,0:T(8,128)(2,1)S(1)}, u32[]{:S(2)}, u32[]{:S(2)}) collective-permute-start(bf16[2,128,256]{2,1,0:T(8,128)(2,1)S(1)} %get-tuple-element.91), channel_id=1, source_target_pairs={{0,7},{1,0},{2,1},{3,2},{4,3},{5,4},{6,5},{7,6},{8,9},{9,10},{10,1... | collective-permute-start | bytes 393224 | tf_op jit(solution)/shard_map/ppermute | solution.py:442
  65.9 5.1 %collective-permute-start.9 = (bf16[1,128,256]{2,1,0:T(8,128)(2,1)S(1)}, bf16[1,128,256]{2,1,0:T(8,128)(2,1)S(1)}, u32[]{:S(2)}, u32[]{:S(2)}) collective-permute-start(bf16[1,128,256]{2,1,0:T(8,128)(2,1)S(1)} %get-tuple-element.92), channel_id=1, source_target_pairs={{0,4},{1,5},{2,6},{3,7},{4,0},{5,1},{6,2},{7,3},{8,12},{9,13},{10,... | collective-permute-start | bytes 196616 | tf_op jit(solution)/shard_map/ppermute | solution.py:442
  71.0 5.3 %collective-permute-start.10 = (bf16[2,48,128]{2,1,0:T(8,128)(2,1)S(1)}, bf16[2,48,128]{2,1,0:T(8,128)(2,1)S(1)}, u32[]{:S(2)}, u32[]{:S(2)}) collective-permute-start(bf16[2,48,128]{2,1,0:T(8,128)(2,1)S(1)} %get-tuple-element.93), channel_id=1, source_target_pairs={{0,8},{8,16},{16,24},{24,32},{32,40},{40,48},{48,56},{56,64},{64,7... | collective-permute-start | bytes 73736 | tf_op jit(solution)/shard_map/ppermute | solution.py:499
  76.2 1.9 %collective-permute-start.11 = (bf16[2,48,128]{2,1,0:T(8,128)(2,1)S(1)}, bf16[2,48,128]{2,1,0:T(8,128)(2,1)S(1)}, u32[]{:S(2)}, u32[]{:S(2)}) collective-permute-start(bf16[2,48,128]{2,1,0:T(8,128)(2,1)S(1)} %get-tuple-element.94), channel_id=1, source_target_pairs={{8,0},{16,8},{24,16},{32,24},{40,32},{48,40},{56,48},{64,56},{72,6... | collective-permute-start | bytes 73736 | tf_op jit(solution)/shard_map/ppermute | solution.py:500
  78.2 0.0 collective-permute-done.10.above_ref
  78.2 3.2 %collective-permute-done.11.below_ref = bf16[2,48,128]{2,1,0:T(8,128)(2,1)S(1)} collective-permute-done((bf16[2,48,128]{2,1,0:T(8,128)(2,1)S(1)}, bf16[2,48,128]{2,1,0:T(8,128)(2,1)S(1)}, u32[]{:S(2)}, u32[]{:S(2)}) %collective-permute-start.11) | collective-permute-done | bytes 24608 | tf_op jit(solution)/shard_map/ppermute | solution.py:500
  81.4 0.0 collective-permute-done.8.refs_7_
  81.4 1.0 shard_map.105
  82.4 11.9 %all-to-all-start.2 = ((f32[64,8,128]{2,1,0:T(8,128)}), f32[64,8,128]{2,1,0:T(8,128)S(1)}, u32[]{:S(2)}, u32[]{:S(2)}) async-start(f32[64,8,128]{2,1,0:T(8,128)} %get-tuple-element.100), calls=%async_computation.2 | async-start | bytes 524288 | tf_op jit(solution)/shard_map/all_to_all | solution.py:434
  94.4 0.8 slice-done
  95.2 0.7 pad_maximum_fusion.1
  95.9 3.2 %collective-permute-start.12 = (bf16[2,128,256]{2,1,0:T(8,128)(2,1)}, bf16[2,128,256]{2,1,0:T(8,128)(2,1)S(1)}, u32[]{:S(2)}, u32[]{:S(2)}) collective-permute-start(bf16[2,128,256]{2,1,0:T(8,128)(2,1)} %pad_maximum_fusion.1), channel_id=1, source_target_pairs={{0,2},{1,3},{2,4},{3,5},{4,6},{5,7},{6,0},{7,1},{8,14},{9,15},{10,... | collective-permute-start | bytes 393224 | tf_op jit(solution)/shard_map/ppermute | solution.py:442
  99.1 0.0 copy-start.28
  99.1 0.7 pad_maximum_fusion.2
  99.8 2.9 %collective-permute-start.13 = (bf16[2,128,256]{2,1,0:T(8,128)(2,1)}, bf16[2,128,256]{2,1,0:T(8,128)(2,1)S(1)}, u32[]{:S(2)}, u32[]{:S(2)}) collective-permute-start(bf16[2,128,256]{2,1,0:T(8,128)(2,1)} %pad_maximum_fusion.2), channel_id=1, source_target_pairs={{0,6},{1,7},{2,0},{3,1},{4,2},{5,3},{6,4},{7,5},{8,10},{9,11},{10,... | collective-permute-start | bytes 393224 | tf_op jit(solution)/shard_map/ppermute | solution.py:442
  102.7 0.1 copy.11.taps_ref
  102.8 0.3 shard_map.107.ogt_ref
  103.2 0.6 copy-done.20
  103.8 1.5 shard_map.106
  105.2 0.7 copy-done.26
  105.9 0.0 collective-permute-done.12.refs_9_
  105.9 2.4 %collective-permute-done.13.refs_10_ = bf16[2,128,256]{2,1,0:T(8,128)(2,1)S(1)} collective-permute-done((bf16[2,128,256]{2,1,0:T(8,128)(2,1)}, bf16[2,128,256]{2,1,0:T(8,128)(2,1)S(1)}, u32[]{:S(2)}, u32[]{:S(2)}) %collective-permute-start.13) | collective-permute-done | bytes 131104 | tf_op jit(solution)/shard_map/ppermute | solution.py:442
  108.3 0.0 all-to-all-done.2
  108.3 0.0 copy-start.21
  108.3 0.6 shard_map.108
  108.9 3.3 %collective-permute-start.15 = (bf16[256,128]{1,0:T(8,128)(2,1)S(1)}, bf16[256,128]{1,0:T(8,128)(2,1)S(1)}, u32[]{:S(2)}, u32[]{:S(2)}) collective-permute-start(bf16[256,128]{1,0:T(8,128)(2,1)S(1)} %get-tuple-element.120.ctx_ref.refs_0_), channel_id=1, source_target_pairs={{0,7},{1,0},{2,1},{3,2},{4,3},{5,4},{6,5},{7,6},{8,9},{9,10},{10,1... | collective-permute-start | bytes 196616 | tf_op jit(solution)/shard_map/ppermute | solution.py:442
  112.2 3.2 %collective-permute-start.14 = (bf16[256,128]{1,0:T(8,128)(2,1)S(1)}, bf16[256,128]{1,0:T(8,128)(2,1)S(1)}, u32[]{:S(2)}, u32[]{:S(2)}) collective-permute-start(bf16[256,128]{1,0:T(8,128)(2,1)S(1)} %get-tuple-element.120.ctx_ref.refs_0_), channel_id=1, source_target_pairs={{0,1},{1,2},{2,3},{3,4},{4,5},{5,6},{6,7},{7,0},{8,15},{9,8},{10,9... | collective-permute-start | bytes 196616 | tf_op jit(solution)/shard_map/ppermute | solution.py:442
  115.5 3.3 %shard_map.109 = (bf16[64,48,128]{2,1,0:T(8,128)(2,1)}, f32[2,128,128]{2,1,0:T(8,128)S(1)}, f32[2,128,128]{2,1,0:T(8,128)S(1)}, bf16[2,128,128]{2,1,0:T(8,128)(2,1)}) custom-call(f32[8,128]{1,0:T(8,128)S(1)} %get-tuple-element.121.log_ref, f32[2,128,256]{2,1,0:T(8,128)S(1)} %get-tuple-element.86.refs_10_.t_ref, f32[2,128,256]{2,1,0:T(8,128)S(1)} %copy-done.12, ...), custom_call_target="tpu_custom_call" | custom-call | flops 1000000000 | bytes 2000000 | tf_op jit(solution)/shard_map/pallas_call | solution.py:420
  118.8 0.0 collective-permute-done.15.refs_2_
  118.8 11.0 %all-to-all-start.3 = ((bf16[64,48,128]{2,1,0:T(8,128)(2,1)}), bf16[64,48,128]{2,1,0:T(8,128)(2,1)S(1)}, u32[]{:S(2)}, u32[]{:S(2)}) async-start(bf16[64,48,128]{2,1,0:T(8,128)(2,1)} %get-tuple-element.135), calls=%async_computation.3 | async-start | bytes 1572864 | tf_op jit(solution)/shard_map/all_to_all | solution.py:434
  129.9 5.5 %collective-permute-start.17 = (bf16[512,128]{1,0:T(8,128)(2,1)S(1)}, bf16[512,128]{1,0:T(8,128)(2,1)S(1)}, u32[]{:S(2)}, u32[]{:S(2)}) collective-permute-start(bf16[512,128]{1,0:T(8,128)(2,1)S(1)} %pad_maximum_fusion.3), channel_id=1, source_target_pairs={{0,5},{1,6},{2,7},{3,0},{4,1},{5,2},{6,3},{7,4},{8,11},{9,12},{10,... | collective-permute-start | bytes 393224 | tf_op jit(solution)/shard_map/ppermute | solution.py:442
  135.4 3.1 %collective-permute-start.16 = (bf16[768,128]{1,0:T(8,128)(2,1)S(1)}, bf16[768,128]{1,0:T(8,128)(2,1)S(1)}, u32[]{:S(2)}, u32[]{:S(2)}) collective-permute-start(bf16[768,128]{1,0:T(8,128)(2,1)S(1)} %pad_maximum_fusion), channel_id=1, source_target_pairs={{0,3},{1,4},{2,5},{3,6},{4,7},{5,0},{6,1},{7,2},{8,13},{9,14},{10,... | collective-permute-start | bytes 589832 | tf_op jit(solution)/shard_map/ppermute | solution.py:442
  138.5 4.9 %shard_map.111.own_ref = f32[8,128]{1,0:T(8,128)S(1)} custom-call(f32[2,128,128]{2,1,0:T(8,128)S(1)} %copy-done.15, f32[2,128,128]{2,1,0:T(8,128)S(1)} %copy-done.18, f32[2,128,128]{2,1,0:T(8,128)S(1)} %copy-done.23, f32[2,128,128]{2,1,0:T(8,128)S(1)} %copy-done.25), custom_call_target="tpu_custom_call" | custom-call | flops 5000000000 | bytes 2000000 | tf_op jit(solution)/shard_map/pallas_call | solution.py:420
  143.4 0.0 collective-permute-done.17.refs_4_
  143.4 1.0 collective-permute-done.16.refs_3_
  144.4 1.1 shard_map.110
  145.5 7.1 %all-to-all-done.3.got_ref = bf16[64,48,128]{2,1,0:T(8,128)(2,1)S(1)} async-done(((bf16[64,48,128]{2,1,0:T(8,128)(2,1)}), bf16[64,48,128]{2,1,0:T(8,128)(2,1)S(1)}, u32[]{:S(2)}, u32[]{:S(2)}) %all-to-all-start.3) | async-done | bytes 786464 | tf_op jit(solution)/shard_map/all_to_all | solution.py:434
  152.6 0.8 shard_map.112
  (60 shorter events, 0.2 us)
Async XLA Ops:
  0.6 0.8 copy-start.7
  1.5 0.8 copy-start.9
  3.1 15.0 %copy-start = (bf16[2,128,256]{2,1,0:T(8,128)(2,1)S(1)}, bf16[2,128,256]{2,1,0:T(8,128)(2,1)}, u32[]{:S(2)}) copy-start(bf16[2,128,256]{2,1,0:T(8,128)(2,1)} %param.11) | copy-start | bytes 393220
  3.1 38.9 %copy-start.6 = (bf16[2,128,128]{2,1,0:T(8,128)(2,1)S(1)}, bf16[2,128,128]{2,1,0:T(8,128)(2,1)}, u32[]{:S(2)}) copy-start(bf16[2,128,128]{2,1,0:T(8,128)(2,1)} %v_ref.5) | copy-start | bytes 196612
  3.1 38.9 %copy-start.8 = (bf16[2,128,128]{2,1,0:T(8,128)(2,1)S(1)}, bf16[2,128,128]{2,1,0:T(8,128)(2,1)}, u32[]{:S(2)}) copy-start(bf16[2,128,128]{2,1,0:T(8,128)(2,1)} %q_ref.5) | copy-start | bytes 196612
  3.1 39.0 %copy-start.10 = (bf16[2,128,128]{2,1,0:T(8,128)(2,1)S(1)}, bf16[2,128,128]{2,1,0:T(8,128)(2,1)}, u32[]{:S(2)}) copy-start(bf16[2,128,128]{2,1,0:T(8,128)(2,1)} %k_ref.5) | copy-start | bytes 196612
  3.1 38.9 %all-to-all-start = ((f32[64,8,128]{2,1,0:T(8,128)}), f32[64,8,128]{2,1,0:T(8,128)S(1)}, u32[]{:S(2)}, u32[]{:S(2)}) async-start(f32[64,8,128]{2,1,0:T(8,128)} %shard_map.101), calls=%async_computation | async-start | bytes 524288 | tf_op jit(solution)/shard_map/all_to_all | solution.py:434
  18.1 14.4 %collective-permute-start.1 = (bf16[256,256]{1,0:T(8,128)(2,1)S(1)}, bf16[256,256]{1,0:T(8,128)(2,1)S(1)}, u32[]{:S(2)}, u32[]{:S(2)}) collective-permute-start(bf16[256,256]{1,0:T(8,128)(2,1)S(1)} %bitcast.10), channel_id=1, source_target_pairs={{0,2},{1,3},{2,4},{3,5},{4,6},{5,7},{6,0},{7,1},{8,14},{9,15},{10,... | collective-permute-start | bytes 393224 | tf_op jit(solution)/shard_map/ppermute | solution.py:442
  24.0 14.6 %collective-permute-start.4 = (bf16[256,256]{1,0:T(8,128)(2,1)S(1)}, bf16[256,256]{1,0:T(8,128)(2,1)S(1)}, u32[]{:S(2)}, u32[]{:S(2)}) collective-permute-start(bf16[256,256]{1,0:T(8,128)(2,1)S(1)} %bitcast.11), channel_id=1, source_target_pairs={{0,6},{1,7},{2,0},{3,1},{4,2},{5,3},{6,4},{7,5},{8,10},{9,11},{10,... | collective-permute-start | bytes 393224 | tf_op jit(solution)/shard_map/ppermute | solution.py:442
  25.9 20.1 %collective-permute-start.6 = (bf16[256,256]{1,0:T(8,128)(2,1)S(1)}, bf16[256,256]{1,0:T(8,128)(2,1)S(1)}, u32[]{:S(2)}, u32[]{:S(2)}) collective-permute-start(bf16[256,256]{1,0:T(8,128)(2,1)S(1)} %bitcast.12), channel_id=1, source_target_pairs={{0,7},{1,0},{2,1},{3,2},{4,3},{5,4},{6,5},{7,6},{8,9},{9,10},{10,1... | collective-permute-start | bytes 393224 | tf_op jit(solution)/shard_map/ppermute | solution.py:442
  28.2 17.8 %collective-permute-start = (bf16[256,256]{1,0:T(8,128)(2,1)S(1)}, bf16[256,256]{1,0:T(8,128)(2,1)S(1)}, u32[]{:S(2)}, u32[]{:S(2)}) collective-permute-start(bf16[256,256]{1,0:T(8,128)(2,1)S(1)} %bitcast.13), channel_id=1, source_target_pairs={{0,1},{1,2},{2,3},{3,4},{4,5},{5,6},{6,7},{7,0},{8,15},{9,8},{10,9... | collective-permute-start | bytes 393224 | tf_op jit(solution)/shard_map/ppermute | solution.py:442
  32.5 13.5 %collective-permute-start.3 = (bf16[256,256]{1,0:T(8,128)(2,1)S(1)}, bf16[256,256]{1,0:T(8,128)(2,1)S(1)}, u32[]{:S(2)}, u32[]{:S(2)}) collective-permute-start(bf16[256,256]{1,0:T(8,128)(2,1)S(1)} %collective-permute-done.1.refs_2_), channel_id=1, source_target_pairs={{0,2},{1,3},{2,4},{3,5},{4,6},{5,7},{6,0},{7,1},{8,14},{9,15},{10,... | collective-permute-start | bytes 393224 | tf_op jit(solution)/shard_map/ppermute | solution.py:442
  36.7 9.4 %collective-permute-start.2 = (bf16[256,256]{1,0:T(8,128)(2,1)S(1)}, bf16[256,256]{1,0:T(8,128)(2,1)S(1)}, u32[]{:S(2)}, u32[]{:S(2)}) collective-permute-start(bf16[256,256]{1,0:T(8,128)(2,1)S(1)} %collective-permute-done.1.refs_2_), channel_id=1, source_target_pairs={{0,1},{1,2},{2,3},{3,4},{4,5},{5,6},{6,7},{7,0},{8,15},{9,8},{10,9... | collective-permute-start | bytes 393224 | tf_op jit(solution)/shard_map/ppermute | solution.py:442
  38.6 7.4 %collective-permute-start.5 = (bf16[256,256]{1,0:T(8,128)(2,1)S(1)}, bf16[256,256]{1,0:T(8,128)(2,1)S(1)}, u32[]{:S(2)}, u32[]{:S(2)}) collective-permute-start(bf16[256,256]{1,0:T(8,128)(2,1)S(1)} %collective-permute-done.4.refs_6_), channel_id=1, source_target_pairs={{0,7},{1,0},{2,1},{3,2},{4,3},{5,4},{6,5},{7,6},{8,9},{9,10},{10,1... | collective-permute-start | bytes 393224 | tf_op jit(solution)/shard_map/ppermute | solution.py:442
  43.1 0.7 copy-start.11
  43.8 2.2 %copy-start.13 = (f32[2,128,128]{2,1,0:T(8,128)}, f32[2,128,128]{2,1,0:T(8,128)S(1)}, u32[]{:S(2)}) copy-start(f32[2,128,128]{2,1,0:T(8,128)S(1)} %get-tuple-element.76.qm_ref) | copy-start | bytes 393220
  43.8 2.2 %copy-start.16 = (f32[2,128,128]{2,1,0:T(8,128)}, f32[2,128,128]{2,1,0:T(8,128)S(1)}, u32[]{:S(2)}) copy-start(f32[2,128,128]{2,1,0:T(8,128)S(1)} %get-tuple-element.77.km_ref) | copy-start | bytes 393220
  43.8 2.2 %copy-start.1 = (bf16[128,2048]{1,0:T(8,128)(2,1)S(1)}, bf16[128,2048]{1,0:T(8,128)(2,1)}, u32[]{:S(2)}) copy-start(bf16[128,2048]{1,0:T(8,128)(2,1)} %refs_8_.1) | copy-start | bytes 1572868
  47.9 0.7 copy-start.19
  48.5 32.9 %all-to-all-start.1 = ((f32[64,16,128]{2,1,0:T(8,128)}), f32[64,16,128]{2,1,0:T(8,128)S(1)}, u32[]{:S(2)}, u32[]{:S(2)}) async-start(f32[64,16,128]{2,1,0:T(8,128)} %bitcast.2), calls=%async_computation.1 | async-start | bytes 1048576 | tf_op jit(solution)/shard_map/all_to_all | solution.py:434
  60.3 21.1 %collective-permute-start.7 = (bf16[2,128,256]{2,1,0:T(8,128)(2,1)S(1)}, bf16[2,128,256]{2,1,0:T(8,128)(2,1)S(1)}, u32[]{:S(2)}, u32[]{:S(2)}) collective-permute-start(bf16[2,128,256]{2,1,0:T(8,128)(2,1)S(1)} %get-tuple-element.90), channel_id=1, source_target_pairs={{0,1},{1,2},{2,3},{3,4},{4,5},{5,6},{6,7},{7,0},{8,15},{9,8},{10,9... | collective-permute-start | bytes 393224 | tf_op jit(solution)/shard_map/ppermute | solution.py:442
  63.7 17.7 %collective-permute-start.8 = (bf16[2,128,256]{2,1,0:T(8,128)(2,1)S(1)}, bf16[2,128,256]{2,1,0:T(8,128)(2,1)S(1)}, u32[]{:S(2)}, u32[]{:S(2)}) collective-permute-start(bf16[2,128,256]{2,1,0:T(8,128)(2,1)S(1)} %get-tuple-element.91), channel_id=1, source_target_pairs={{0,7},{1,0},{2,1},{3,2},{4,3},{5,4},{6,5},{7,6},{8,9},{9,10},{10,1... | collective-permute-start | bytes 393224 | tf_op jit(solution)/shard_map/ppermute | solution.py:442
  65.9 15.5 %collective-permute-start.9 = (bf16[1,128,256]{2,1,0:T(8,128)(2,1)S(1)}, bf16[1,128,256]{2,1,0:T(8,128)(2,1)S(1)}, u32[]{:S(2)}, u32[]{:S(2)}) collective-permute-start(bf16[1,128,256]{2,1,0:T(8,128)(2,1)S(1)} %get-tuple-element.92), channel_id=1, source_target_pairs={{0,4},{1,5},{2,6},{3,7},{4,0},{5,1},{6,2},{7,3},{8,12},{9,13},{10,... | collective-permute-start | bytes 196616 | tf_op jit(solution)/shard_map/ppermute | solution.py:442
  71.0 7.2 %collective-permute-start.10 = (bf16[2,48,128]{2,1,0:T(8,128)(2,1)S(1)}, bf16[2,48,128]{2,1,0:T(8,128)(2,1)S(1)}, u32[]{:S(2)}, u32[]{:S(2)}) collective-permute-start(bf16[2,48,128]{2,1,0:T(8,128)(2,1)S(1)} %get-tuple-element.93), channel_id=1, source_target_pairs={{0,8},{8,16},{16,24},{24,32},{32,40},{40,48},{48,56},{56,64},{64,7... | collective-permute-start | bytes 73736 | tf_op jit(solution)/shard_map/ppermute | solution.py:499
  76.2 5.1 %collective-permute-start.11 = (bf16[2,48,128]{2,1,0:T(8,128)(2,1)S(1)}, bf16[2,48,128]{2,1,0:T(8,128)(2,1)S(1)}, u32[]{:S(2)}, u32[]{:S(2)}) collective-permute-start(bf16[2,48,128]{2,1,0:T(8,128)(2,1)S(1)} %get-tuple-element.94), channel_id=1, source_target_pairs={{8,0},{16,8},{24,16},{32,24},{40,32},{48,40},{56,48},{64,56},{72,6... | collective-permute-start | bytes 73736 | tf_op jit(solution)/shard_map/ppermute | solution.py:500
  81.4 13.0 %copy-start.2 = (bf16[2,128,256]{2,1,0:T(8,128)(2,1)}, bf16[2,128,256]{2,1,0:T(8,128)(2,1)S(1)}, u32[]{:S(2)}) copy-start(bf16[2,128,256]{2,1,0:T(8,128)(2,1)S(1)} %collective-permute-done.7.refs_6_) | copy-start | bytes 393220
  81.4 13.0 %copy-start.4 = (bf16[2,128,256]{2,1,0:T(8,128)(2,1)}, bf16[2,128,256]{2,1,0:T(8,128)(2,1)S(1)}, u32[]{:S(2)}) copy-start(bf16[2,128,256]{2,1,0:T(8,128)(2,1)S(1)} %collective-permute-done.8.refs_7_) | copy-start | bytes 393220
  82.4 25.9 %all-to-all-start.2 = ((f32[64,8,128]{2,1,0:T(8,128)}), f32[64,8,128]{2,1,0:T(8,128)S(1)}, u32[]{:S(2)}, u32[]{:S(2)}) async-start(f32[64,8,128]{2,1,0:T(8,128)} %get-tuple-element.100), calls=%async_computation.2 | async-start | bytes 524288 | tf_op jit(solution)/shard_map/all_to_all | solution.py:434
  94.4 0.8 slice-start
  95.2 3.9 %slice-start.1 = ((bf16[2,128,256]{2,1,0:T(8,128)(2,1)}), bf16[1,128,256]{2,1,0:T(8,128)(2,1)S(1)}, s32[]{:S(2)}) async-start(bf16[2,128,256]{2,1,0:T(8,128)(2,1)} %copy-done.4), calls=%async_computation.5 | async-start | bytes 131072 | tf_op jit(solution)/shard_map/slice | solution.py:525
  95.9 10.0 %collective-permute-start.12 = (bf16[2,128,256]{2,1,0:T(8,128)(2,1)}, bf16[2,128,256]{2,1,0:T(8,128)(2,1)S(1)}, u32[]{:S(2)}, u32[]{:S(2)}) collective-permute-start(bf16[2,128,256]{2,1,0:T(8,128)(2,1)} %pad_maximum_fusion.1), channel_id=1, source_target_pairs={{0,2},{1,3},{2,4},{3,5},{4,6},{5,7},{6,0},{7,1},{8,14},{9,15},{10,... | collective-permute-start | bytes 393224 | tf_op jit(solution)/shard_map/ppermute | solution.py:442
  99.1 3.6 %copy-start.28 = (f32[33,2]{0,1:T(2,128)S(1)}, f32[33,2]{0,1:T(2,128)}, u32[]{:S(2)}) copy-start(f32[33,2]{0,1:T(2,128)} %param.9) | copy-start | bytes 796
  99.8 8.5 %collective-permute-start.13 = (bf16[2,128,256]{2,1,0:T(8,128)(2,1)}, bf16[2,128,256]{2,1,0:T(8,128)(2,1)S(1)}, u32[]{:S(2)}, u32[]{:S(2)}) collective-permute-start(bf16[2,128,256]{2,1,0:T(8,128)(2,1)} %pad_maximum_fusion.2), channel_id=1, source_target_pairs={{0,6},{1,7},{2,0},{3,1},{4,2},{5,3},{6,4},{7,5},{8,10},{9,11},{10,... | collective-permute-start | bytes 393224 | tf_op jit(solution)/shard_map/ppermute | solution.py:442
  102.8 0.9 copy-start.20
  105.2 0.7 copy-start.26
  108.3 7.1 %copy-start.12 = (f32[2,128,256]{2,1,0:T(8,128)S(1)}, f32[2,128,256]{2,1,0:T(8,128)}, u32[]{:S(2)}) copy-start(f32[2,128,256]{2,1,0:T(8,128)} %copy-done.11) | copy-start | bytes 786436
  108.3 7.2 %copy-start.14 = (f32[2,128,128]{2,1,0:T(8,128)S(1)}, f32[2,128,128]{2,1,0:T(8,128)}, u32[]{:S(2)}) copy-start(f32[2,128,128]{2,1,0:T(8,128)} %copy-done.13) | copy-start | bytes 393220
  108.3 7.2 %copy-start.17 = (f32[2,128,128]{2,1,0:T(8,128)S(1)}, f32[2,128,128]{2,1,0:T(8,128)}, u32[]{:S(2)}) copy-start(f32[2,128,128]{2,1,0:T(8,128)} %copy-done.16) | copy-start | bytes 393220
  108.3 7.2 %copy-start.21 = (f32[2,128,128]{2,1,0:T(8,128)S(1)}, f32[2,128,128]{2,1,0:T(8,128)}, u32[]{:S(2)}) copy-start(f32[2,128,128]{2,1,0:T(8,128)} %copy-done.19) | copy-start | bytes 393220
  108.3 7.2 %copy-start.27 = (f32[2,128,128]{2,1,0:T(8,128)S(1)}, f32[2,128,128]{2,1,0:T(8,128)}, u32[]{:S(2)}) copy-start(f32[2,128,128]{2,1,0:T(8,128)} %copy-done.26) | copy-start | bytes 393220
  108.9 9.9 %copy-start.22 = (f32[2,128,128]{2,1,0:T(8,128)}, f32[2,128,128]{2,1,0:T(8,128)S(1)}, u32[]{:S(2)}) copy-start(f32[2,128,128]{2,1,0:T(8,128)S(1)} %get-tuple-element.125.mixed_ref) | copy-start | bytes 393220
  108.9 9.9 %copy-start.24 = (f32[2,128,128]{2,1,0:T(8,128)}, f32[2,128,128]{2,1,0:T(8,128)S(1)}, u32[]{:S(2)}) copy-start(f32[2,128,128]{2,1,0:T(8,128)S(1)} %get-tuple-element.136.mix_ref) | copy-start | bytes 393220
  108.9 9.9 %collective-permute-start.15 = (bf16[256,128]{1,0:T(8,128)(2,1)S(1)}, bf16[256,128]{1,0:T(8,128)(2,1)S(1)}, u32[]{:S(2)}, u32[]{:S(2)}) collective-permute-start(bf16[256,128]{1,0:T(8,128)(2,1)S(1)} %get-tuple-element.120.ctx_ref.refs_0_), channel_id=1, source_target_pairs={{0,7},{1,0},{2,1},{3,2},{4,3},{5,4},{6,5},{7,6},{8,9},{9,10},{10,1... | collective-permute-start | bytes 196616 | tf_op jit(solution)/shard_map/ppermute | solution.py:442
  112.2 6.6 %collective-permute-start.14 = (bf16[256,128]{1,0:T(8,128)(2,1)S(1)}, bf16[256,128]{1,0:T(8,128)(2,1)S(1)}, u32[]{:S(2)}, u32[]{:S(2)}) collective-permute-start(bf16[256,128]{1,0:T(8,128)(2,1)S(1)} %get-tuple-element.120.ctx_ref.refs_0_), channel_id=1, source_target_pairs={{0,1},{1,2},{2,3},{3,4},{4,5},{5,6},{6,7},{7,0},{8,15},{9,8},{10,9... | collective-permute-start | bytes 196616 | tf_op jit(solution)/shard_map/ppermute | solution.py:442
  118.8 33.7 %all-to-all-start.3 = ((bf16[64,48,128]{2,1,0:T(8,128)(2,1)}), bf16[64,48,128]{2,1,0:T(8,128)(2,1)S(1)}, u32[]{:S(2)}, u32[]{:S(2)}) async-start(bf16[64,48,128]{2,1,0:T(8,128)(2,1)} %get-tuple-element.135), calls=%async_computation.3 | async-start | bytes 1572864 | tf_op jit(solution)/shard_map/all_to_all | solution.py:434
  129.8 8.7 %copy-start.25 = (f32[2,128,128]{2,1,0:T(8,128)S(1)}, f32[2,128,128]{2,1,0:T(8,128)}, u32[]{:S(2)}) copy-start(f32[2,128,128]{2,1,0:T(8,128)} %copy-done.24) | copy-start | bytes 393220
  129.8 8.7 %copy-start.15 = (f32[2,128,128]{2,1,0:T(8,128)S(1)}, f32[2,128,128]{2,1,0:T(8,128)}, u32[]{:S(2)}) copy-start(f32[2,128,128]{2,1,0:T(8,128)} %copy-done.13) | copy-start | bytes 393220
  129.8 8.7 %copy-start.18 = (f32[2,128,128]{2,1,0:T(8,128)S(1)}, f32[2,128,128]{2,1,0:T(8,128)}, u32[]{:S(2)}) copy-start(f32[2,128,128]{2,1,0:T(8,128)} %copy-done.16) | copy-start | bytes 393220
  129.9 8.7 %copy-start.23 = (f32[2,128,128]{2,1,0:T(8,128)S(1)}, f32[2,128,128]{2,1,0:T(8,128)}, u32[]{:S(2)}) copy-start(f32[2,128,128]{2,1,0:T(8,128)} %copy-done.22) | copy-start | bytes 393220
  129.9 13.5 %collective-permute-start.17 = (bf16[512,128]{1,0:T(8,128)(2,1)S(1)}, bf16[512,128]{1,0:T(8,128)(2,1)S(1)}, u32[]{:S(2)}, u32[]{:S(2)}) collective-permute-start(bf16[512,128]{1,0:T(8,128)(2,1)S(1)} %pad_maximum_fusion.3), channel_id=1, source_target_pairs={{0,5},{1,6},{2,7},{3,0},{4,1},{5,2},{6,3},{7,4},{8,11},{9,12},{10,... | collective-permute-start | bytes 393224 | tf_op jit(solution)/shard_map/ppermute | solution.py:442
  135.4 9.0 %copy-start.3 = (bf16[2,128,256]{2,1,0:T(8,128)(2,1)S(1)}, bf16[2,128,256]{2,1,0:T(8,128)(2,1)}, u32[]{:S(2)}) copy-start(bf16[2,128,256]{2,1,0:T(8,128)(2,1)} %copy-done.2) | copy-start | bytes 393220
  135.4 9.0 %copy-start.5 = (bf16[2,128,256]{2,1,0:T(8,128)(2,1)S(1)}, bf16[2,128,256]{2,1,0:T(8,128)(2,1)}, u32[]{:S(2)}) copy-start(bf16[2,128,256]{2,1,0:T(8,128)(2,1)} %copy-done.4) | copy-start | bytes 393220
  135.4 9.0 %collective-permute-start.16 = (bf16[768,128]{1,0:T(8,128)(2,1)S(1)}, bf16[768,128]{1,0:T(8,128)(2,1)S(1)}, u32[]{:S(2)}, u32[]{:S(2)}) collective-permute-start(bf16[768,128]{1,0:T(8,128)(2,1)S(1)} %pad_maximum_fusion), channel_id=1, source_target_pairs={{0,3},{1,4},{2,5},{3,6},{4,7},{5,0},{6,1},{7,2},{8,13},{9,14},{10,... | collective-permute-start | bytes 589832 | tf_op jit(solution)/shard_map/ppermute | solution.py:442

commit v3 on v2

--- a/solution.py
+++ b/solution.py
@@ -11,7 +11,6 @@
 SEGS = 2
 f32 = jnp.float32
 bf16 = jnp.bfloat16
-PIECES = ((0,), (2, 6), (1, 3), (7, 5), (4,))
 NN = (((1,), (0,)), ((), ()))
 NT = (((1,), (1,)), ((), ()))
 
@@ -116,10 +115,30 @@
     log_ref[...] = jnp.concatenate(logs, axis=0)
 
 
-def chunk_kernel(parts, rim, *refs):
+def pack_kernel(parts, og_ref, w_ref, up_ref, down_ref, up_two_ref, down_two_ref, kept_ref):
+    width = og_ref.shape[1]
+    for ref, items in (
+        (up_ref, (None, 1)),
+        (down_ref, (None, 7)),
+        (up_two_ref, (4, None, 3, 2)),
+        (down_two_ref, (None, 5, 6)),
+        (kept_ref, (0,)),
+    ):
+        row = 0
+        for shift in items:
+            if shift is None:
+                block = og_ref[...]
+            else:
+                start = pl.multiple_of(block_at(-shift, parts) * width, width)
+                block = w_ref[:, pl.ds(start, width)]
+            ref[row : row + block.shape[0], :] = block
+            row += block.shape[0]
+
+
+def chunk_kernel(parts, rim, starts, *refs):
     og_refs = refs[:parts]
     w_ref, v_ref, t_ref, o_ref, log_ref = refs[parts : parts + 5]
-    out_ref, cg_ref, head_ref, tail_ref = refs[parts + 5 : parts + 9]
+    out_ref, cg_ref, head_ref, tail_ref = refs[parts + 5 :]
     documents, tokens, channels = cg_ref.shape
     groups = out_ref.shape[0] // 16
     width = w_ref.shape[1] // parts
@@ -129,11 +148,9 @@
 
     total = None
     for shift in range(parts):
-        part = dot(og_refs[shift][...], w_ref[:, columns(shift)], NT)
+        block = og_refs[shift][starts[shift] : starts[shift] + documents * tokens, :]
+        part = dot(block, w_ref[:, columns(shift)], NT)
         total = part if total is None else total + part
-    for ref, shifts in zip(refs[parts + 9 :], PIECES):
-        for slot, shift in enumerate(shifts):
-            ref[slot] = w_ref[:, columns(-shift)]
     for doc in range(documents):
         grad = total[doc * tokens : (doc + 1) * tokens]
         cg_ref[doc] = grad
@@ -213,11 +230,11 @@
         inv_ref[index] = unit
 
 
-def turn_kernel(parts, *refs):
-    width = refs[0].shape[1]
+def turn_kernel(parts, starts, *refs):
+    count, width = refs[parts].shape[1], refs[0].shape[1]
     for shift in range(parts):
         start = pl.multiple_of(block_at(shift, parts) * width, width)
-        refs[parts][pl.ds(start, width), :] = refs[shift][...].T
+        refs[parts][pl.ds(start, width), :] = refs[shift][starts[shift] : starts[shift] + count, :].T
 
 
 def combine_kernel(got_ref, out_ref, log_ref):
@@ -408,8 +425,10 @@
 def output_kernel(blocks, weights, *refs):
     total = None
     tokens = refs[-1].shape[0]
-    for (index, block), (source, slot) in zip(blocks, weights):
-        part = dot(refs[index][block * tokens : (block + 1) * tokens, :], refs[source][slot])
+    channels = refs[0].shape[1]
+    for (index, block), (source, row) in zip(blocks, weights):
+        weight = refs[source][row : row + channels, :]
+        part = dot(refs[index][block * tokens : (block + 1) * tokens, :], weight)
         total = part if total is None else total + part
     refs[-1][...] = total.astype(bf16)
 
@@ -440,13 +459,6 @@
         step = shift if i % 2 == 0 else parts - shift
         pairs += [(i * parts + j, i * parts + (j + step) % parts) for j in range(parts)]
     return lax.ppermute(block, ("seq", "head"), pairs)
-
-
-def gathered(block, parts):
-    two, back_two = shift_by(block, 2, parts), shift_by(block, parts - 2, parts)
-    one, back_one = shift_by(block, 1, parts), shift_by(block, parts - 1, parts)
-    three, back_three = shift_by(two, 1, parts), shift_by(back_two, parts - 1, parts)
-    return [block, one, two, three, shift_by(two, 2, parts), back_three, back_two, back_one]
 
 
 def shards(queries, key_vectors, value_vectors, conv_taps, out_weight, out_grad):
@@ -469,7 +481,22 @@
     (sent,) = call(means_kernel, [((groups, 8, channels), f32)], queries, key_vectors)
     own_grad, sent = lax.optimization_barrier((out_grad, sent))
     got = exchange(sent, "seq").reshape(groups * 8, channels)
-    og_parts = gathered(own_grad.reshape(documents * tokens, own_width), parts)
+    own_grad = own_grad.reshape(documents * tokens, own_width)
+    rows = documents * tokens
+    up, down, up_two, down_two, kept = call(
+        functools.partial(pack_kernel, parts),
+        [((rows + pieces * channels, own_width), bf16) for pieces in (1, 1, 3, 2)]
+        + [((channels, own_width), bf16)],
+        own_grad, out_weight,
+    )
+    up_two, down_two = shift_by(up_two, 2, parts), shift_by(down_two, parts - 2, parts)
+    up, down = shift_by(up, 1, parts), shift_by(down, parts - 1, parts)
+    up_three = shift_by(up_two[channels : rows + 2 * channels], 1, parts)
+    down_three = shift_by(down_two[: rows + channels], parts - 1, parts)
+    across = shift_by(up_two[: rows + channels], 2, parts)
+    og_parts = [own_grad, up, up_two, up_three, across, down_three, down_two, down]
+    og_starts = (0, 0, channels, 0, channels, 0, 0, 0)
+    w_starts = (0, rows, rows + 2 * channels, rows, 0, rows, rows + channels, rows)
 
     weights, scores, local_mixed, local_log, qm, km = call(
         functools.partial(stats_kernel, scale),
@@ -483,34 +510,27 @@
         ],
         got, queries, key_vectors, value_vectors,
     )
-    (inverse,) = call(
-        functools.partial(inverse_kernel, scale), [((units, count, count), f32)], qm, km, flops=2e9
-    )
-    og_parts, inverse = lax.optimization_barrier((og_parts, inverse))
-    sent, context_grad, first_rows, last_rows, *pieces = call(
-        functools.partial(chunk_kernel, parts, rim),
+    sent, context_grad, first_rows, last_rows = call(
+        functools.partial(chunk_kernel, parts, rim, og_starts),
         [((groups * 16, channels), f32), (rows_shape, f32)]
-        + [((documents, 3 * rim, channels), bf16)] * 2
-        + [((len(shifts), channels, own_width), bf16) for shifts in PIECES],
+        + [((documents, 3 * rim, channels), bf16)] * 2,
         *og_parts, out_weight, value_vectors, weights, local_mixed, local_log,
     )
+    sent, qm, km = lax.optimization_barrier((sent, qm, km))
     got = exchange(sent, "seq")
     ends = groups - 1
     above = lax.ppermute(last_rows, "seq", [(i, i + 1) for i in range(ends)])
     below = lax.ppermute(first_rows, "seq", [(i + 1, i) for i in range(ends)])
-    kept, stay, up, down, across = pieces
-    up = shift_by(up, 1, parts)
-    down = shift_by(down, parts - 1, parts)
-    across = shift_by(across, 4, parts)
-    got, up, down, across, above, below = lax.optimization_barrier(
-        (got, up, down, across, above, below)
-    )
+    (inverse,) = call(
+        functools.partial(inverse_kernel, scale), [((units, count, count), f32)], qm, km, flops=2e9
+    )
+    got, above, below, inverse = lax.optimization_barrier((got, above, below, inverse))
     sent, logs = call(
         combine_kernel, [((groups, 8, channels), f32), ((8, count), f32)], got
     )
-    sent, up, down, stay, og_parts = lax.optimization_barrier((sent, up, down, stay, og_parts))
+    sent, og_parts = lax.optimization_barrier((sent, og_parts))
     (og_turned,) = call(
-        functools.partial(turn_kernel, parts), [((model_width, documents * tokens), bf16)], *og_parts
+        functools.partial(turn_kernel, parts, og_starts), [((model_width, documents * tokens), bf16)], *og_parts
     )
     got = exchange(sent, "seq").reshape(groups * 8, channels)
     conv, back = call(
@@ -521,12 +541,8 @@
         smem=(0,),
         flops=1e9,
     )
-    up_two = shift_by(jnp.concatenate([stay[0:1], up[1:2]], axis=0), 2, parts)
-    down_two = shift_by(jnp.concatenate([stay[1:2], down[1:2]], axis=0), parts - 2, parts)
-    got, up_two, down_two, conv, back, og_turned = lax.optimization_barrier(
-        (got, up_two, down_two, conv, back, og_turned)
-    )
-    weight_parts = [kept, up, down, across, up_two, down_two]
+    got, conv, back, og_turned = lax.optimization_barrier((got, conv, back, og_turned))
+    weight_parts = [kept] + og_parts[1:]
     context_b, mixed, mix, landmark_mix = call(
         context_kernel,
         [
@@ -565,7 +581,7 @@
         flops=5e9,
     )
     blocks = ((0, 0), (1, 0), (3, 2), (3, 1), (3, 0), (4, 1), (4, 0), (2, 0))
-    slots = ((5, 0), (6, 0), (9, 0), (9, 1), (8, 0), (10, 1), (10, 0), (7, 0))
+    slots = tuple((5 + shift, start) for shift, start in enumerate(w_starts))
     (layer_output,) = call(
         functools.partial(output_kernel, blocks, slots),
         [((documents * tokens, own_width), bf16)],

time: 154 us -> 147 us (0.955)
  starting transfers between devices: 113 us -> 82.8 us
  waiting for transfers between devices: 13.7 us -> 29.8 us
  local copies, waits for them, and re-layouts: 5.28 us -> 13.3 us
    ppermute x16 -> x11, starting transfers between devices: 55.7 us -> 39.7 us  [shift_by(): return lax.ppermute(block, ('seq', 'head'), pairs)]
    all_to_all x4, waiting for transfers between devices: 7.07 us -> 22.5 us  [exchange(): return lax.all_to_all(blocks, axis, 0, 0, tiled=True)]
    all_to_all x4, starting transfers between devices: 49.7 us -> 37.6 us  [exchange(): return lax.all_to_all(blocks, axis, 0, 0, tiled=True)]
    unnamed x59 -> x89, local copies, waits for them, and re-layouts: 4.45 us -> 11.8 us
    ppermute x16 -> x11, waiting for transfers between devices: 3.46 us -> 6.51 us  [shift_by(): return lax.ppermute(block, ('seq', 'head'), pairs)]
    ppermute x1, waiting for transfers between devices: 3.21 us -> 0.79 us  [shards(): below = lax.ppermute(first_rows, 'seq', [(i + 1, i) for i in range(ends)])]
    ppermute x1, starting transfers between devices: 5.25 us -> 3.54 us  [shards(): above = lax.ppermute(last_rows, 'seq', [(i, i + 1) for i in range(ends)])]
    pallas_call x12 -> x13, Pallas kernels: 19.1 us -> 18.6 us  [call(): pl.pallas_call(kernel, out_shape=[jax.ShapeDtypeStruct(shape, kind) for s...]
  transfers between devices with their start and end apart: 22 -> 17, of which waited for: 4 -> 7; matrix products, arithmetic and copies ran while one was open for 1% -> 1% of each run, Pallas kernels for 9% -> 9%
where the time goes in v3:
time: 147 us; the launch traced here: 146 us
  starting transfers between devices  82.8 us (56%)
  waiting for transfers between devices  29.8 us (20%)
  Pallas kernels  18.6 us (13%)
  local copies, waits for them, and re-layouts  13.3 us (9%)
    ppermute x11, starting transfers between devices, shift_by(): return lax.ppermute(block, ('seq', 'head'), pairs)  39.7 us
    all_to_all x4, starting transfers between devices, exchange(): return lax.all_to_all(blocks, axis, 0, 0, tiled=True)  37.6 us
    all_to_all x4, waiting for transfers between devices, exchange(): return lax.all_to_all(blocks, axis, 0, 0, tiled=True)  22.5 us
    pallas_call x13, Pallas kernels, call(): pl.pallas_call(kernel, out_shape=[jax.ShapeDtypeStruct(shape, kind) for s...  18.6 us
    unnamed x89, local copies, waits for them, and re-layouts  11.8 us
    ppermute x11, waiting for transfers between devices, shift_by(): return lax.ppermute(block, ('seq', 'head'), pairs)  6.51 us
    ppermute x1, starting transfers between devices, shards(): above = lax.ppermute(last_rows, 'seq', [(i, i + 1) for i in range(ends)])  3.54 us
  transfers between devices with their start and end apart: 17, of which 7 were waited for; matrix products, arithmetic and copies ran while one was open for 1% of the time, Pallas kernels for 9%

profile of v3, /device:TPU:1, one launch (start us, length us, event | category | flops | bytes accessed | tf_op | source)
XLA Modules:
  0.0 145.8 jit_solution(8326025153864991565)
XLA Ops:
  0.6 0.0 copy-start.9
  0.7 0.9 copy-done.9
  1.5 0.8 copy-done.11
  2.4 0.8 shard_map.101
  3.1 1.0 copy-done
  4.2 0.1 shard_map.102
  4.3 0.0 copy-start.20
  4.3 6.7 %collective-permute-start.1 = (bf16[640,256]{1,0:T(8,128)(2,1)S(1)}, bf16[640,256]{1,0:T(8,128)(2,1)S(1)}, u32[]{:S(2)}, u32[]{:S(2)}) collective-permute-start(bf16[640,256]{1,0:T(8,128)(2,1)S(1)} %get-tuple-element.63), channel_id=1, source_target_pairs={{0,2},{1,3},{2,4},{3,5},{4,6},{5,7},{6,0},{7,1},{8,14},{9,15},{10,... | collective-permute-start | bytes 983048 | tf_op jit(solution)/shard_map/ppermute | solution.py:461
  11.0 1.9 %collective-permute-start.4 = (bf16[512,256]{1,0:T(8,128)(2,1)S(1)}, bf16[512,256]{1,0:T(8,128)(2,1)S(1)}, u32[]{:S(2)}, u32[]{:S(2)}) collective-permute-start(bf16[512,256]{1,0:T(8,128)(2,1)S(1)} %get-tuple-element.64), channel_id=1, source_target_pairs={{0,6},{1,7},{2,0},{3,1},{4,2},{5,3},{6,4},{7,5},{8,10},{9,11},{10,... | collective-permute-start | bytes 786440 | tf_op jit(solution)/shard_map/ppermute | solution.py:461
  12.9 14.3 %all-to-all-start = ((f32[64,8,128]{2,1,0:T(8,128)}), f32[64,8,128]{2,1,0:T(8,128)S(1)}, u32[]{:S(2)}, u32[]{:S(2)}) async-start(f32[64,8,128]{2,1,0:T(8,128)} %shard_map.101), calls=%async_computation | async-start | bytes 524288 | tf_op jit(solution)/shard_map/all_to_all | solution.py:453
  27.2 3.8 %collective-permute-start = (bf16[384,256]{1,0:T(8,128)(2,1)S(1)}, bf16[384,256]{1,0:T(8,128)(2,1)S(1)}, u32[]{:S(2)}, u32[]{:S(2)}) collective-permute-start(bf16[384,256]{1,0:T(8,128)(2,1)S(1)} %get-tuple-element.62), channel_id=1, source_target_pairs={{0,1},{1,2},{2,3},{3,4},{4,5},{5,6},{6,7},{7,0},{8,15},{9,8},{10,9... | collective-permute-start | bytes 589832 | tf_op jit(solution)/shard_map/ppermute | solution.py:461
  31.1 1.9 %collective-permute-start.6 = (bf16[384,256]{1,0:T(8,128)(2,1)S(1)}, bf16[384,256]{1,0:T(8,128)(2,1)S(1)}, u32[]{:S(2)}, u32[]{:S(2)}) collective-permute-start(bf16[384,256]{1,0:T(8,128)(2,1)S(1)} %get-tuple-element.65), channel_id=1, source_target_pairs={{0,7},{1,0},{2,1},{3,2},{4,3},{5,4},{6,5},{7,6},{8,9},{9,10},{10,1... | collective-permute-start | bytes 589832 | tf_op jit(solution)/shard_map/ppermute | solution.py:461
  33.0 0.7 slice.14
  33.7 2.7 %collective-permute-start.5 = (bf16[384,256]{1,0:T(8,128)(2,1)}, bf16[384,256]{1,0:T(8,128)(2,1)S(1)}, u32[]{:S(2)}, u32[]{:S(2)}) collective-permute-start(bf16[384,256]{1,0:T(8,128)(2,1)} %slice.14), channel_id=1, source_target_pairs={{0,7},{1,0},{2,1},{3,2},{4,3},{5,4},{6,5},{7,6},{8,9},{9,10},{10,1... | collective-permute-start | bytes 589832 | tf_op jit(solution)/shard_map/ppermute | solution.py:461
  36.5 0.8 fusion
  37.3 5.1 %collective-permute-start.3 = (bf16[384,256]{1,0:T(8,128)(2,1)}, bf16[384,256]{1,0:T(8,128)(2,1)S(1)}, u32[]{:S(2)}, u32[]{:S(2)}) collective-permute-start(bf16[384,256]{1,0:T(8,128)(2,1)} %get-tuple-element.117), channel_id=1, source_target_pairs={{0,2},{1,3},{2,4},{3,5},{4,6},{5,7},{6,0},{7,1},{8,14},{9,15},{10,... | collective-permute-start | bytes 589832 | tf_op jit(solution)/shard_map/ppermute | solution.py:461
  42.3 2.5 %collective-permute-start.2 = (bf16[384,256]{1,0:T(8,128)(2,1)}, bf16[384,256]{1,0:T(8,128)(2,1)S(1)}, u32[]{:S(2)}, u32[]{:S(2)}) collective-permute-start(bf16[384,256]{1,0:T(8,128)(2,1)} %get-tuple-element.118), channel_id=1, source_target_pairs={{0,1},{1,2},{2,3},{3,4},{4,5},{5,6},{6,7},{7,0},{8,15},{9,8},{10,9... | collective-permute-start | bytes 589832 | tf_op jit(solution)/shard_map/ppermute | solution.py:461
  44.8 0.0 all-to-all-done
  44.9 1.1 shard_map.103
  46.0 0.7 copy-done.22
  46.7 0.0 collective-permute-done.refs_1_.refs_6_
  46.7 1.5 %collective-permute-done.3.refs_4_.refs_9_ = bf16[384,256]{1,0:T(8,128)(2,1)S(1)} collective-permute-done((bf16[384,256]{1,0:T(8,128)(2,1)}, bf16[384,256]{1,0:T(8,128)(2,1)S(1)}, u32[]{:S(2)}, u32[]{:S(2)}) %collective-permute-start.3) | collective-permute-done | bytes 196640 | tf_op jit(solution)/shard_map/ppermute | solution.py:461
  48.2 1.6 %collective-permute-done.2.refs_3_.refs_8_ = bf16[384,256]{1,0:T(8,128)(2,1)S(1)} collective-permute-done((bf16[384,256]{1,0:T(8,128)(2,1)}, bf16[384,256]{1,0:T(8,128)(2,1)S(1)}, u32[]{:S(2)}, u32[]{:S(2)}) %collective-permute-start.2) | collective-permute-done | bytes 196640 | tf_op jit(solution)/shard_map/ppermute | solution.py:461
  49.8 1.7 %shard_map.104 = (f32[1024,128]{1,0:T(8,128)}, f32[2,128,128]{2,1,0:T(8,128)S(1)}, bf16[2,48,128]{2,1,0:T(8,128)(2,1)S(1)}, bf16[2,48,128]{2,1,0:T(8,128)(2,1)S(1)}) custom-call(bf16[256,256]{1,0:T(8,128)(2,1)S(1)} %bitcast.9, bf16[384,256]{1,0:T(8,128)(2,1)S(1)} %collective-permute-done.refs_1_.refs_6_, ...), custom_call_target="tpu_custom_call" | custom-call | flops 100000000 | bytes 2000000 | tf_op jit(solution)/shard_map/pallas_call | solution.py:439
  51.6 0.7 copy-done.30
  52.2 13.0 %all-to-all-start.1 = ((f32[64,16,128]{2,1,0:T(8,128)}), f32[64,16,128]{2,1,0:T(8,128)S(1)}, u32[]{:S(2)}, u32[]{:S(2)}) async-start(f32[64,16,128]{2,1,0:T(8,128)} %bitcast.2), calls=%async_computation.1 | async-start | bytes 1048576 | tf_op jit(solution)/shard_map/all_to_all | solution.py:453
  65.2 3.5 %collective-permute-start.7 = (bf16[2,48,128]{2,1,0:T(8,128)(2,1)S(1)}, bf16[2,48,128]{2,1,0:T(8,128)(2,1)S(1)}, u32[]{:S(2)}, u32[]{:S(2)}) collective-permute-start(bf16[2,48,128]{2,1,0:T(8,128)(2,1)S(1)} %get-tuple-element.74), channel_id=1, source_target_pairs={{0,8},{8,16},{16,24},{24,32},{32,40},{40,48},{48,56},{56,64},{64,7... | collective-permute-start | bytes 73736 | tf_op jit(solution)/shard_map/ppermute | solution.py:522
  68.8 1.9 %collective-permute-start.8 = (bf16[2,48,128]{2,1,0:T(8,128)(2,1)S(1)}, bf16[2,48,128]{2,1,0:T(8,128)(2,1)S(1)}, u32[]{:S(2)}, u32[]{:S(2)}) collective-permute-start(bf16[2,48,128]{2,1,0:T(8,128)(2,1)S(1)} %get-tuple-element.75), channel_id=1, source_target_pairs={{8,0},{16,8},{24,16},{32,24},{40,32},{48,40},{56,48},{64,56},{72,6... | collective-permute-start | bytes 73736 | tf_op jit(solution)/shard_map/ppermute | solution.py:523
  70.7 2.2 %shard_map.105.inv_ref = f32[4,128,128]{2,1,0:T(8,128)S(1)} custom-call(f32[2,128,128]{2,1,0:T(8,128)S(1)} %get-tuple-element.76.qm_ref, f32[2,128,128]{2,1,0:T(8,128)S(1)} %get-tuple-element.77.km_ref), custom_call_target="tpu_custom_call" | custom-call | flops 2000000000 | bytes 2000000 | tf_op jit(solution)/shard_map/pallas_call | solution.py:439
  72.9 0.7 copy-done.6
  73.6 0.0 collective-permute-done.7.above_ref
  73.6 0.8 collective-permute-done.8.below_ref
  74.4 8.6 %all-to-all-done.1 = f32[64,16,128]{2,1,0:T(8,128)S(1)} async-done(((f32[64,16,128]{2,1,0:T(8,128)}), f32[64,16,128]{2,1,0:T(8,128)S(1)}, u32[]{:S(2)}, u32[]{:S(2)}) %all-to-all-start.1) | async-done | bytes 524320 | tf_op jit(solution)/shard_map/all_to_all | solution.py:453
  83.0 1.0 shard_map.106
  83.9 6.0 %all-to-all-start.2 = ((f32[64,8,128]{2,1,0:T(8,128)}), f32[64,8,128]{2,1,0:T(8,128)S(1)}, u32[]{:S(2)}, u32[]{:S(2)}) async-start(f32[64,8,128]{2,1,0:T(8,128)} %get-tuple-element.80), calls=%async_computation.2 | async-start | bytes 524288 | tf_op jit(solution)/shard_map/all_to_all | solution.py:453
  89.9 0.1 copy.11.taps_ref
  90.0 0.3 shard_map.108.ogt_ref
  90.4 0.6 copy-done.31
  90.9 1.5 %shard_map.107 = (f32[2,128,128]{2,1,0:T(8,128)S(1)}, f32[2,128,128]{2,1,0:T(8,128)S(1)}) custom-call(f32[33,2]{1,0:T(8,128)S(1)} %copy.11.taps_ref, bf16[2,128,128]{2,1,0:T(8,128)(2,1)S(1)} %copy-done.13, f32[2,128,128]{2,1,0:T(8,128)S(1)} %copy-done.31, bf16[2,48,128]{2,1,0:T(8,128)(2,1)S(1)} %copy-done.38, bf16[2,48,128]{2,1,0:T(8,128)(2,1)S(1)} %copy-done.40), custom_call_target="tpu_custom_call" | custom-call | flops 1000000000 | bytes 2000000 | tf_op jit(solution)/shard_map/pallas_call | solution.py:439
  92.4 0.6 copy-done.14
  93.1 0.7 copy-done.41
  93.7 9.4 %all-to-all-done.2 = f32[64,8,128]{2,1,0:T(8,128)S(1)} async-done(((f32[64,8,128]{2,1,0:T(8,128)}), f32[64,8,128]{2,1,0:T(8,128)S(1)}, u32[]{:S(2)}, u32[]{:S(2)}) %all-to-all-start.2) | async-done | bytes 262176 | tf_op jit(solution)/shard_map/all_to_all | solution.py:453
  103.1 0.9 copy-done.7
  104.0 0.9 copy-done.15
  105.0 0.0 copy-start.32
  105.0 0.6 shard_map.109
  105.6 1.9 %collective-permute-start.10 = (bf16[256,128]{1,0:T(8,128)(2,1)S(1)}, bf16[256,128]{1,0:T(8,128)(2,1)S(1)}, u32[]{:S(2)}, u32[]{:S(2)}) collective-permute-start(bf16[256,128]{1,0:T(8,128)(2,1)S(1)} %get-tuple-element.97.ctx_ref.refs_0_), channel_id=1, source_target_pairs={{0,7},{1,0},{2,1},{3,2},{4,3},{5,4},{6,5},{7,6},{8,9},{9,10},{10,1... | collective-permute-start | bytes 196616 | tf_op jit(solution)/shard_map/ppermute | solution.py:461
  107.5 4.6 %collective-permute-start.9 = (bf16[256,128]{1,0:T(8,128)(2,1)S(1)}, bf16[256,128]{1,0:T(8,128)(2,1)S(1)}, u32[]{:S(2)}, u32[]{:S(2)}) collective-permute-start(bf16[256,128]{1,0:T(8,128)(2,1)S(1)} %get-tuple-element.97.ctx_ref.refs_0_), channel_id=1, source_target_pairs={{0,1},{1,2},{2,3},{3,4},{4,5},{5,6},{6,7},{7,0},{8,15},{9,8},{10,9... | collective-permute-start | bytes 196616 | tf_op jit(solution)/shard_map/ppermute | solution.py:461
  112.1 0.9 copy-done.42
  113.0 2.7 %shard_map.110 = (bf16[64,48,128]{2,1,0:T(8,128)(2,1)S(1)}, f32[2,128,128]{2,1,0:T(8,128)S(1)}, f32[2,128,128]{2,1,0:T(8,128)S(1)}, bf16[2,128,128]{2,1,0:T(8,128)(2,1)}) custom-call(f32[8,128]{1,0:T(8,128)S(1)} %get-tuple-element.98.log_ref, f32[2,128,256]{2,1,0:T(8,128)S(1)} %copy-done.4, f32[2,128,256]{2,1,0:T(8,128)S(1)} %copy-done.23, ...), custom_call_target="tpu_custom_call" | custom-call | flops 1000000000 | bytes 2000000 | tf_op jit(solution)/shard_map/pallas_call | solution.py:439
  115.7 0.9 copy-done.5
  116.6 0.6 copy-done.16
  117.3 0.0 collective-permute-done.10.refs_2_
  117.3 0.0 collective-permute-done.9.refs_1_
  117.3 0.6 copy-done.18
  117.9 4.4 %all-to-all-start.3 = ((bf16[64,48,128]{2,1,0:T(8,128)(2,1)}), bf16[64,48,128]{2,1,0:T(8,128)(2,1)S(1)}, u32[]{:S(2)}, u32[]{:S(2)}) async-start(bf16[64,48,128]{2,1,0:T(8,128)(2,1)} %copy-done.5), calls=%async_computation.3 | async-start | bytes 1572864 | tf_op jit(solution)/shard_map/all_to_all | solution.py:453
  122.4 5.6 %collective-permute-start.12 = (bf16[512,128]{1,0:T(8,128)(2,1)S(1)}, bf16[512,128]{1,0:T(8,128)(2,1)S(1)}, u32[]{:S(2)}, u32[]{:S(2)}) collective-permute-start(bf16[512,128]{1,0:T(8,128)(2,1)S(1)} %pad_maximum_fusion.1), channel_id=1, source_target_pairs={{0,5},{1,6},{2,7},{3,0},{4,1},{5,2},{6,3},{7,4},{8,11},{9,12},{10,... | collective-permute-start | bytes 393224 | tf_op jit(solution)/shard_map/ppermute | solution.py:461
  128.0 0.0 copy-start.21
  128.1 2.9 %collective-permute-start.11 = (bf16[768,128]{1,0:T(8,128)(2,1)S(1)}, bf16[768,128]{1,0:T(8,128)(2,1)S(1)}, u32[]{:S(2)}, u32[]{:S(2)}) collective-permute-start(bf16[768,128]{1,0:T(8,128)(2,1)S(1)} %pad_maximum_fusion), channel_id=1, source_target_pairs={{0,3},{1,4},{2,5},{3,6},{4,7},{5,0},{6,1},{7,2},{8,13},{9,14},{10,... | collective-permute-start | bytes 589832 | tf_op jit(solution)/shard_map/ppermute | solution.py:461
  131.0 4.9 %shard_map.112.own_ref = f32[8,128]{1,0:T(8,128)S(1)} custom-call(f32[2,128,128]{2,1,0:T(8,128)S(1)} %copy-done.26, f32[2,128,128]{2,1,0:T(8,128)S(1)} %copy-done.29, f32[2,128,128]{2,1,0:T(8,128)S(1)} %copy-done.34, f32[2,128,128]{2,1,0:T(8,128)S(1)} %copy-done.36), custom_call_target="tpu_custom_call" | custom-call | flops 5000000000 | bytes 2000000 | tf_op jit(solution)/shard_map/pallas_call | solution.py:439
  135.9 3.4 %collective-permute-done.11.refs_3_ = bf16[768,128]{1,0:T(8,128)(2,1)S(1)} collective-permute-done((bf16[768,128]{1,0:T(8,128)(2,1)S(1)}, bf16[768,128]{1,0:T(8,128)(2,1)S(1)}, u32[]{:S(2)}, u32[]{:S(2)}) %collective-permute-start.11) | collective-permute-done | bytes 196640 | tf_op jit(solution)/shard_map/ppermute | solution.py:461
  139.3 1.1 shard_map.111
  140.4 4.6 %all-to-all-done.3.got_ref = bf16[64,48,128]{2,1,0:T(8,128)(2,1)S(1)} async-done(((bf16[64,48,128]{2,1,0:T(8,128)(2,1)}), bf16[64,48,128]{2,1,0:T(8,128)(2,1)S(1)}, u32[]{:S(2)}, u32[]{:S(2)}) %all-to-all-start.3) | async-done | bytes 786464 | tf_op jit(solution)/shard_map/all_to_all | solution.py:453
  145.0 0.8 shard_map.113
  (76 shorter events, 0.2 us)
Async XLA Ops:
  0.6 2.5 %copy-start.2 = (bf16[2,128,256]{2,1,0:T(8,128)(2,1)S(1)}, bf16[2,128,256]{2,1,0:T(8,128)(2,1)}, u32[]{:S(2)}) copy-start(bf16[2,128,256]{2,1,0:T(8,128)(2,1)} %param.11) | copy-start | bytes 393220
  0.6 0.9 copy-start.9
  1.5 0.8 copy-start.11
  3.1 1.0 copy-start
  4.3 8.7 %copy-start.20 = (bf16[128,256]{1,0:T(8,128)(2,1)}, bf16[128,256]{1,0:T(8,128)(2,1)S(1)}, u32[]{:S(2)}) copy-start(bf16[128,256]{1,0:T(8,128)(2,1)S(1)} %get-tuple-element.108.refs_5_) | copy-start | bytes 196612
  4.3 32.2 %collective-permute-start.1 = (bf16[640,256]{1,0:T(8,128)(2,1)S(1)}, bf16[640,256]{1,0:T(8,128)(2,1)S(1)}, u32[]{:S(2)}, u32[]{:S(2)}) collective-permute-start(bf16[640,256]{1,0:T(8,128)(2,1)S(1)} %get-tuple-element.63), channel_id=1, source_target_pairs={{0,2},{1,3},{2,4},{3,5},{4,6},{5,7},{6,0},{7,1},{8,14},{9,15},{10,... | collective-permute-start | bytes 983048 | tf_op jit(solution)/shard_map/ppermute | solution.py:461
  11.0 22.0 %collective-permute-start.4 = (bf16[512,256]{1,0:T(8,128)(2,1)S(1)}, bf16[512,256]{1,0:T(8,128)(2,1)S(1)}, u32[]{:S(2)}, u32[]{:S(2)}) collective-permute-start(bf16[512,256]{1,0:T(8,128)(2,1)S(1)} %get-tuple-element.64), channel_id=1, source_target_pairs={{0,6},{1,7},{2,0},{3,1},{4,2},{5,3},{6,4},{7,5},{8,10},{9,11},{10,... | collective-permute-start | bytes 786440 | tf_op jit(solution)/shard_map/ppermute | solution.py:461
  12.9 31.9 %all-to-all-start = ((f32[64,8,128]{2,1,0:T(8,128)}), f32[64,8,128]{2,1,0:T(8,128)S(1)}, u32[]{:S(2)}, u32[]{:S(2)}) async-start(f32[64,8,128]{2,1,0:T(8,128)} %shard_map.101), calls=%async_computation | async-start | bytes 524288 | tf_op jit(solution)/shard_map/all_to_all | solution.py:453
  27.2 19.5 %collective-permute-start = (bf16[384,256]{1,0:T(8,128)(2,1)S(1)}, bf16[384,256]{1,0:T(8,128)(2,1)S(1)}, u32[]{:S(2)}, u32[]{:S(2)}) collective-permute-start(bf16[384,256]{1,0:T(8,128)(2,1)S(1)} %get-tuple-element.62), channel_id=1, source_target_pairs={{0,1},{1,2},{2,3},{3,4},{4,5},{5,6},{6,7},{7,0},{8,15},{9,8},{10,9... | collective-permute-start | bytes 589832 | tf_op jit(solution)/shard_map/ppermute | solution.py:461
  31.1 15.6 %collective-permute-start.6 = (bf16[384,256]{1,0:T(8,128)(2,1)S(1)}, bf16[384,256]{1,0:T(8,128)(2,1)S(1)}, u32[]{:S(2)}, u32[]{:S(2)}) collective-permute-start(bf16[384,256]{1,0:T(8,128)(2,1)S(1)} %get-tuple-element.65), channel_id=1, source_target_pairs={{0,7},{1,0},{2,1},{3,2},{4,3},{5,4},{6,5},{7,6},{8,9},{9,10},{10,1... | collective-permute-start | bytes 589832 | tf_op jit(solution)/shard_map/ppermute | solution.py:461
  33.7 11.1 %copy-start.10 = (bf16[2,128,128]{2,1,0:T(8,128)(2,1)S(1)}, bf16[2,128,128]{2,1,0:T(8,128)(2,1)}, u32[]{:S(2)}) copy-start(bf16[2,128,128]{2,1,0:T(8,128)(2,1)} %q_ref.5) | copy-start | bytes 196612
  33.7 11.2 %copy-start.12 = (bf16[2,128,128]{2,1,0:T(8,128)(2,1)S(1)}, bf16[2,128,128]{2,1,0:T(8,128)(2,1)}, u32[]{:S(2)}) copy-start(bf16[2,128,128]{2,1,0:T(8,128)(2,1)} %k_ref.5) | copy-start | bytes 196612
  33.7 11.2 %copy-start.13 = (bf16[2,128,128]{2,1,0:T(8,128)(2,1)S(1)}, bf16[2,128,128]{2,1,0:T(8,128)(2,1)}, u32[]{:S(2)}) copy-start(bf16[2,128,128]{2,1,0:T(8,128)(2,1)} %v_ref.5) | copy-start | bytes 196612
  33.7 16.1 %copy-start.1 = (bf16[128,2048]{1,0:T(8,128)(2,1)S(1)}, bf16[128,2048]{1,0:T(8,128)(2,1)}, u32[]{:S(2)}) copy-start(bf16[128,2048]{1,0:T(8,128)(2,1)} %refs_8_.1) | copy-start | bytes 1572868
  33.7 13.0 %collective-permute-start.5 = (bf16[384,256]{1,0:T(8,128)(2,1)}, bf16[384,256]{1,0:T(8,128)(2,1)S(1)}, u32[]{:S(2)}, u32[]{:S(2)}) collective-permute-start(bf16[384,256]{1,0:T(8,128)(2,1)} %slice.14), channel_id=1, source_target_pairs={{0,7},{1,0},{2,1},{3,2},{4,3},{5,4},{6,5},{7,6},{8,9},{9,10},{10,1... | collective-permute-start | bytes 589832 | tf_op jit(solution)/shard_map/ppermute | solution.py:461
  37.3 11.0 %collective-permute-start.3 = (bf16[384,256]{1,0:T(8,128)(2,1)}, bf16[384,256]{1,0:T(8,128)(2,1)S(1)}, u32[]{:S(2)}, u32[]{:S(2)}) collective-permute-start(bf16[384,256]{1,0:T(8,128)(2,1)} %get-tuple-element.117), channel_id=1, source_target_pairs={{0,2},{1,3},{2,4},{3,5},{4,6},{5,7},{6,0},{7,1},{8,14},{9,15},{10,... | collective-permute-start | bytes 589832 | tf_op jit(solution)/shard_map/ppermute | solution.py:461
  42.3 7.5 %collective-permute-start.2 = (bf16[384,256]{1,0:T(8,128)(2,1)}, bf16[384,256]{1,0:T(8,128)(2,1)S(1)}, u32[]{:S(2)}, u32[]{:S(2)}) collective-permute-start(bf16[384,256]{1,0:T(8,128)(2,1)} %get-tuple-element.118), channel_id=1, source_target_pairs={{0,1},{1,2},{2,3},{3,4},{4,5},{5,6},{6,7},{7,0},{8,15},{9,8},{10,9... | collective-permute-start | bytes 589832 | tf_op jit(solution)/shard_map/ppermute | solution.py:461
  46.0 0.7 copy-start.22
  46.7 4.9 %copy-start.3 = (f32[2,128,256]{2,1,0:T(8,128)}, f32[2,128,256]{2,1,0:T(8,128)S(1)}, u32[]{:S(2)}) copy-start(f32[2,128,256]{2,1,0:T(8,128)S(1)} %get-tuple-element.67.refs_10_.t_ref) | copy-start | bytes 786436
  46.7 24.0 %copy-start.24 = (f32[2,128,128]{2,1,0:T(8,128)}, f32[2,128,128]{2,1,0:T(8,128)S(1)}, u32[]{:S(2)}) copy-start(f32[2,128,128]{2,1,0:T(8,128)S(1)} %get-tuple-element.76.qm_ref) | copy-start | bytes 393220
  46.7 24.0 %copy-start.27 = (f32[2,128,128]{2,1,0:T(8,128)}, f32[2,128,128]{2,1,0:T(8,128)S(1)}, u32[]{:S(2)}) copy-start(f32[2,128,128]{2,1,0:T(8,128)S(1)} %get-tuple-element.77.km_ref) | copy-start | bytes 393220
  51.6 0.7 copy-start.30
  52.2 30.7 %all-to-all-start.1 = ((f32[64,16,128]{2,1,0:T(8,128)}), f32[64,16,128]{2,1,0:T(8,128)S(1)}, u32[]{:S(2)}, u32[]{:S(2)}) async-start(f32[64,16,128]{2,1,0:T(8,128)} %bitcast.2), calls=%async_computation.1 | async-start | bytes 1048576 | tf_op jit(solution)/shard_map/all_to_all | solution.py:453
  65.2 8.4 %collective-permute-start.7 = (bf16[2,48,128]{2,1,0:T(8,128)(2,1)S(1)}, bf16[2,48,128]{2,1,0:T(8,128)(2,1)S(1)}, u32[]{:S(2)}, u32[]{:S(2)}) collective-permute-start(bf16[2,48,128]{2,1,0:T(8,128)(2,1)S(1)} %get-tuple-element.74), channel_id=1, source_target_pairs={{0,8},{8,16},{16,24},{24,32},{32,40},{40,48},{48,56},{56,64},{64,7... | collective-permute-start | bytes 73736 | tf_op jit(solution)/shard_map/ppermute | solution.py:522
  68.8 5.6 %collective-permute-start.8 = (bf16[2,48,128]{2,1,0:T(8,128)(2,1)S(1)}, bf16[2,48,128]{2,1,0:T(8,128)(2,1)S(1)}, u32[]{:S(2)}, u32[]{:S(2)}) collective-permute-start(bf16[2,48,128]{2,1,0:T(8,128)(2,1)S(1)} %get-tuple-element.75), channel_id=1, source_target_pairs={{8,0},{16,8},{24,16},{32,24},{40,32},{48,40},{56,48},{64,56},{72,6... | collective-permute-start | bytes 73736 | tf_op jit(solution)/shard_map/ppermute | solution.py:523
  72.9 0.7 copy-start.6
  73.6 10.3 %copy-start.37 = (bf16[2,48,128]{2,1,0:T(8,128)(2,1)}, bf16[2,48,128]{2,1,0:T(8,128)(2,1)S(1)}, u32[]{:S(2)}) copy-start(bf16[2,48,128]{2,1,0:T(8,128)(2,1)S(1)} %collective-permute-done.7.above_ref) | copy-start | bytes 73732
  74.4 9.5 %copy-start.39 = (bf16[2,48,128]{2,1,0:T(8,128)(2,1)}, bf16[2,48,128]{2,1,0:T(8,128)(2,1)S(1)}, u32[]{:S(2)}) copy-start(bf16[2,48,128]{2,1,0:T(8,128)(2,1)S(1)} %collective-permute-done.8.below_ref) | copy-start | bytes 73732
  83.9 6.0 %copy-start.43 = (f32[33,2]{0,1:T(2,128)S(1)}, f32[33,2]{0,1:T(2,128)}, u32[]{:S(2)}) copy-start(f32[33,2]{0,1:T(2,128)} %param.9) | copy-start | bytes 796
  83.9 19.2 %all-to-all-start.2 = ((f32[64,8,128]{2,1,0:T(8,128)}), f32[64,8,128]{2,1,0:T(8,128)S(1)}, u32[]{:S(2)}, u32[]{:S(2)}) async-start(f32[64,8,128]{2,1,0:T(8,128)} %get-tuple-element.80), calls=%async_computation.2 | async-start | bytes 524288 | tf_op jit(solution)/shard_map/all_to_all | solution.py:453
  90.0 0.9 copy-start.31
  90.0 0.9 copy-start.38
  90.0 0.9 copy-start.40
  90.9 12.1 %copy-start.4 = (f32[2,128,256]{2,1,0:T(8,128)S(1)}, f32[2,128,256]{2,1,0:T(8,128)}, u32[]{:S(2)}) copy-start(f32[2,128,256]{2,1,0:T(8,128)} %copy-done.3) | copy-start | bytes 786436
  92.4 0.7 copy-start.14
  93.1 0.7 copy-start.41
  103.1 1.0 copy-start.7
  104.0 0.9 copy-start.15
  104.9 7.1 %copy-start.8 = (f32[4,128,128]{2,1,0:T(8,128)S(1)}, f32[4,128,128]{2,1,0:T(8,128)}, u32[]{:S(2)}) copy-start(f32[4,128,128]{2,1,0:T(8,128)} %copy-done.6) | copy-start | bytes 786436
  104.9 7.1 %copy-start.23 = (f32[2,128,256]{2,1,0:T(8,128)S(1)}, f32[2,128,256]{2,1,0:T(8,128)}, u32[]{:S(2)}) copy-start(f32[2,128,256]{2,1,0:T(8,128)} %copy-done.22) | copy-start | bytes 786436
  104.9 7.2 %copy-start.25 = (f32[2,128,128]{2,1,0:T(8,128)S(1)}, f32[2,128,128]{2,1,0:T(8,128)}, u32[]{:S(2)}) copy-start(f32[2,128,128]{2,1,0:T(8,128)} %copy-done.24) | copy-start | bytes 393220
  104.9 7.2 %copy-start.28 = (f32[2,128,128]{2,1,0:T(8,128)S(1)}, f32[2,128,128]{2,1,0:T(8,128)}, u32[]{:S(2)}) copy-start(f32[2,128,128]{2,1,0:T(8,128)} %copy-done.27) | copy-start | bytes 393220
  105.0 7.2 %copy-start.32 = (f32[2,128,128]{2,1,0:T(8,128)S(1)}, f32[2,128,128]{2,1,0:T(8,128)}, u32[]{:S(2)}) copy-start(f32[2,128,128]{2,1,0:T(8,128)} %copy-done.30) | copy-start | bytes 393220
  105.5 10.2 %copy-start.33 = (f32[2,128,128]{2,1,0:T(8,128)}, f32[2,128,128]{2,1,0:T(8,128)S(1)}, u32[]{:S(2)}) copy-start(f32[2,128,128]{2,1,0:T(8,128)S(1)} %get-tuple-element.102.mixed_ref) | copy-start | bytes 393220
  105.6 10.2 %copy-start.35 = (f32[2,128,128]{2,1,0:T(8,128)}, f32[2,128,128]{2,1,0:T(8,128)S(1)}, u32[]{:S(2)}) copy-start(f32[2,128,128]{2,1,0:T(8,128)S(1)} %get-tuple-element.110.mix_ref) | copy-start | bytes 393220
  105.6 11.7 %collective-permute-start.10 = (bf16[256,128]{1,0:T(8,128)(2,1)S(1)}, bf16[256,128]{1,0:T(8,128)(2,1)S(1)}, u32[]{:S(2)}, u32[]{:S(2)}) collective-permute-start(bf16[256,128]{1,0:T(8,128)(2,1)S(1)} %get-tuple-element.97.ctx_ref.refs_0_), channel_id=1, source_target_pairs={{0,7},{1,0},{2,1},{3,2},{4,3},{5,4},{6,5},{7,6},{8,9},{9,10},{10,1... | collective-permute-start | bytes 196616 | tf_op jit(solution)/shard_map/ppermute | solution.py:461
  107.5 9.8 %collective-permute-start.9 = (bf16[256,128]{1,0:T(8,128)(2,1)S(1)}, bf16[256,128]{1,0:T(8,128)(2,1)S(1)}, u32[]{:S(2)}, u32[]{:S(2)}) collective-permute-start(bf16[256,128]{1,0:T(8,128)(2,1)S(1)} %get-tuple-element.97.ctx_ref.refs_0_), channel_id=1, source_target_pairs={{0,1},{1,2},{2,3},{3,4},{4,5},{5,6},{6,7},{7,0},{8,15},{9,8},{10,9... | collective-permute-start | bytes 196616 | tf_op jit(solution)/shard_map/ppermute | solution.py:461
  112.1 0.9 copy-start.42
  115.7 0.9 copy-start.5
  116.6 0.6 copy-start.16
  117.3 0.7 copy-start.18
  117.9 27.0 %all-to-all-start.3 = ((bf16[64,48,128]{2,1,0:T(8,128)(2,1)}), bf16[64,48,128]{2,1,0:T(8,128)(2,1)S(1)}, u32[]{:S(2)}, u32[]{:S(2)}) async-start(bf16[64,48,128]{2,1,0:T(8,128)(2,1)} %copy-done.5), calls=%async_computation.3 | async-start | bytes 1572864 | tf_op jit(solution)/shard_map/all_to_all | solution.py:453
  122.3 8.7 %copy-start.36 = (f32[2,128,128]{2,1,0:T(8,128)S(1)}, f32[2,128,128]{2,1,0:T(8,128)}, u32[]{:S(2)}) copy-start(f32[2,128,128]{2,1,0:T(8,128)} %copy-done.35) | copy-start | bytes 393220
  122.4 8.6 %copy-start.26 = (f32[2,128,128]{2,1,0:T(8,128)S(1)}, f32[2,128,128]{2,1,0:T(8,128)}, u32[]{:S(2)}) copy-start(f32[2,128,128]{2,1,0:T(8,128)} %copy-done.24) | copy-start | bytes 393220
  122.4 8.6 %copy-start.29 = (f32[2,128,128]{2,1,0:T(8,128)S(1)}, f32[2,128,128]{2,1,0:T(8,128)}, u32[]{:S(2)}) copy-start(f32[2,128,128]{2,1,0:T(8,128)} %copy-done.27) | copy-start | bytes 393220
  122.4 8.6 %copy-start.34 = (f32[2,128,128]{2,1,0:T(8,128)S(1)}, f32[2,128,128]{2,1,0:T(8,128)}, u32[]{:S(2)}) copy-start(f32[2,128,128]{2,1,0:T(8,128)} %copy-done.33) | copy-start | bytes 393220
  122.4 13.5 %collective-permute-start.12 = (bf16[512,128]{1,0:T(8,128)(2,1)S(1)}, bf16[512,128]{1,0:T(8,128)(2,1)S(1)}, u32[]{:S(2)}, u32[]{:S(2)}) collective-permute-start(bf16[512,128]{1,0:T(8,128)(2,1)S(1)} %pad_maximum_fusion.1), channel_id=1, source_target_pairs={{0,5},{1,6},{2,7},{3,0},{4,1},{5,2},{6,3},{7,4},{8,11},{9,12},{10,... | collective-permute-start | bytes 393224 | tf_op jit(solution)/shard_map/ppermute | solution.py:461
  128.0 11.3 %copy-start.21 = (bf16[128,256]{1,0:T(8,128)(2,1)S(1)}, bf16[128,256]{1,0:T(8,128)(2,1)}, u32[]{:S(2)}) copy-start(bf16[128,256]{1,0:T(8,128)(2,1)} %copy-done.20) | copy-start | bytes 196612
  128.1 11.2 %collective-permute-start.11 = (bf16[768,128]{1,0:T(8,128)(2,1)S(1)}, bf16[768,128]{1,0:T(8,128)(2,1)S(1)}, u32[]{:S(2)}, u32[]{:S(2)}) collective-permute-start(bf16[768,128]{1,0:T(8,128)(2,1)S(1)} %pad_maximum_fusion), channel_id=1, source_target_pairs={{0,3},{1,4},{2,5},{3,6},{4,7},{5,0},{6,1},{7,2},{8,13},{9,14},{10,... | collective-permute-start | bytes 589832 | tf_op jit(solution)/shard_map/ppermute | solution.py:461
  139.3 5.7 %copy-start.17 = (f32[2,128,128]{2,1,0:T(8,128)S(1)}, f32[2,128,128]{2,1,0:T(8,128)}, u32[]{:S(2)}) copy-start(f32[2,128,128]{2,1,0:T(8,128)} %copy-done.16) | copy-start | bytes 393220
  139.3 5.7 %copy-start.19 = (f32[2,128,128]{2,1,0:T(8,128)S(1)}, f32[2,128,128]{2,1,0:T(8,128)}, u32[]{:S(2)}) copy-start(f32[2,128,128]{2,1,0:T(8,128)} %copy-done.18) | copy-start | bytes 393220

commit v4 on v3

--- a/solution.py
+++ b/solution.py
@@ -140,7 +140,7 @@
     w_ref, v_ref, t_ref, o_ref, log_ref = refs[parts : parts + 5]
     out_ref, cg_ref, head_ref, tail_ref = refs[parts + 5 :]
     documents, tokens, channels = cg_ref.shape
-    groups = out_ref.shape[0] // 16
+    groups = out_ref.shape[0] // 12
     width = w_ref.shape[1] // parts
 
     def columns(shift):
@@ -163,10 +163,10 @@
         for seg in range(SEGS):
             row = doc * SEGS + seg
             rows = slice(seg * groups, (seg + 1) * groups)
-            out_ref[pl.ds(row, groups, stride=16), :] = o_ref[doc, rows, :]
-            out_ref[pl.ds(4 + row, groups, stride=16), :] = mix[rows]
-    for row in range(8):
-        out_ref[pl.ds(8 + row, groups, stride=16), :] = jnp.broadcast_to(
+            out_ref[pl.ds(row, groups, stride=12), :] = o_ref[doc, rows, :]
+            out_ref[pl.ds(4 + row, groups, stride=12), :] = mix[rows]
+    for row in range(4):
+        out_ref[pl.ds(8 + row, groups, stride=12), :] = jnp.broadcast_to(
             log_ref[row : row + 1, :], (groups, channels)
         )
 
@@ -238,13 +238,13 @@
 
 
 def combine_kernel(got_ref, out_ref, log_ref):
-    groups = got_ref.shape[0] // 16
+    groups = got_ref.shape[0] // 12
     channels = got_ref.shape[1]
     me = lax.axis_index("seq")
     lane = lax.broadcasted_iota(jnp.int32, (groups, channels), 1)
     shares, logs = [], []
     for unit in range(4):
-        log = got_ref[pl.ds(8 + unit, groups, stride=16), :]
+        log = got_ref[pl.ds(8 + unit, groups, stride=12), :]
         top = jnp.max(log, axis=0, keepdims=True)
         part = jnp.exp(log - top)
         total = jnp.sum(part, axis=0, keepdims=True)
@@ -266,9 +266,9 @@
             ]
             weight = jnp.where(lane < channels // 2, weight[0], weight[1])
             mixed.append(
-                jnp.sum(weight * got_ref[pl.ds(row, groups, stride=16), :], axis=0, keepdims=True)
+                jnp.sum(weight * got_ref[pl.ds(row, groups, stride=12), :], axis=0, keepdims=True)
             )
-            mix.append(jnp.sum(got_ref[pl.ds(4 + row, groups, stride=16), :], axis=0, keepdims=True))
+            mix.append(jnp.sum(got_ref[pl.ds(4 + row, groups, stride=12), :], axis=0, keepdims=True))
     block = jnp.concatenate(mixed + mix, axis=0)
     out_ref[...] = jnp.broadcast_to(block[None], out_ref.shape)
 
@@ -297,7 +297,17 @@
         back_ref[doc] = back
 
 
-def context_kernel(got_ref, t_ref, inv_ref, conv_ref, ctx_ref, mixed_ref, mix_ref, lm_ref):
+def context_kernel(
+    got_ref, t_ref, inv_far, conv_far, ctx_ref, mixed_ref, mix_ref, lm_ref, inv_ref, conv_ref, sems
+):
+    fetches = [
+        pltpu.make_async_copy(inv_far, inv_ref, sems.at[0]),
+        pltpu.make_async_copy(conv_far, conv_ref, sems.at[1]),
+    ]
+    for fetch in fetches:
+        fetch.start()
+    for fetch in fetches:
+        fetch.wait()
     documents, tokens, _ = conv_ref.shape
     groups = got_ref.shape[0] // 8
     for doc in range(documents):
@@ -311,40 +321,47 @@
         ctx_ref[doc * tokens : (doc + 1) * tokens, :] = ctx
 
 
+def token_back(scale, weights, grad, landmark):
+    count = weights.shape[1] // 2
+    back = weights * prod(grad, landmark, NT)
+    return jnp.concatenate(
+        [
+            back[:, part] - weights[:, part] * jnp.sum(back[:, part], axis=1, keepdims=True)
+            for part in (slice(0, count), slice(count, 2 * count))
+        ],
+        axis=1,
+    ) * scale
+
+
+def key_side(scale, doc, log_ref, s_ref, inv_ref, v_ref, mixed_ref, mix_ref):
+    turned = jnp.concatenate([inv_ref[doc * 2].T, inv_ref[doc * 2 + 1].T], axis=0)
+    mixed_grad = own_blocks(prod(turned, mix_ref[doc]))
+    ones = jnp.ones((8, mixed_grad.shape[1]), bf16)
+    mixed_dot = prod(ones, mixed_grad * stack(mixed_ref[doc]), NT)[0:1]
+    mixed_grad = halves(mixed_grad)
+    log = jnp.concatenate(
+        [log_ref[doc * 2 : doc * 2 + 1, :], log_ref[doc * 2 + 1 : doc * 2 + 2, :]], axis=1
+    )
+    key_weights = jnp.exp(s_ref[doc] - log)
+    key_back = key_weights * (prod(v_ref[doc], mixed_grad, NT) - mixed_dot) * scale
+    return key_weights, key_back, mixed_grad
+
+
 def main_kernel(
-    scale, log_ref, t_ref, s_ref, cg_ref, qm_ref, km_ref, inv_ref, q_ref, k_ref, v_ref,
-    back_ref, ogt_ref, ctx_ref, mixed_ref, mix_ref, lm_ref, out_ref, qd_ref, kd_ref, vg_ref, held,
+    scale, log_ref, t_ref, s_ref, cg_ref, inv_ref, q_ref, k_ref, v_ref, ogt_ref, ctx_ref,
+    mixed_ref, mix_ref, lm_ref, out_far, out_ref, held, sems,
 ):
     documents, tokens, channels = q_ref.shape
-    count = qm_ref.shape[1]
-    groups = count // SEGS
-    for doc in range(documents):
-        mixed = mixed_ref[doc]
-        weights = t_ref[doc]
-        upstream = prod(cg_ref[doc], lm_ref[doc], NT)
-        back = weights * upstream
-        back = jnp.concatenate(
-            [
-                back[:, part] - weights[:, part] * jnp.sum(back[:, part], axis=1, keepdims=True)
-                for part in (slice(0, count), slice(count, 2 * count))
-            ],
-            axis=1,
-        ) * scale
-        qd_ref[doc] = prod(back, stack(km_ref[doc]))
+    groups = out_ref.shape[0]
+    terms = dot(ogt_ref[...], ctx_ref[...]).astype(bf16)
+    out_ref[:, 16:, :] = terms.reshape(groups, terms.shape[0] // groups, channels)
+    rest = pltpu.make_async_copy(out_ref.at[:, 16:, :], out_far.at[:, 16:, :], sems.at[0])
+    rest.start()
+    for doc in range(documents):
+        back = token_back(scale, t_ref[doc], cg_ref[doc], lm_ref[doc])
         key_terms = pick(prod(back.T, q_ref[doc]))
-        turned = jnp.concatenate([inv_ref[doc * 2].T, inv_ref[doc * 2 + 1].T], axis=0)
-        mixed_grad = own_blocks(prod(turned, mix_ref[doc]))
-        ones = jnp.ones((8, channels), bf16)
-        mixed_dot = prod(ones, mixed_grad * stack(mixed), NT)[0:1]
-        mixed_grad = halves(mixed_grad)
-        log = jnp.concatenate(
-            [log_ref[doc * 2 : doc * 2 + 1, :], log_ref[doc * 2 + 1 : doc * 2 + 2, :]], axis=1
-        )
-        key_weights = jnp.exp(s_ref[doc] - log)
-        key_back = key_weights * (prod(v_ref[doc], mixed_grad, NT) - mixed_dot) * scale
+        _, key_back, _ = key_side(scale, doc, log_ref, s_ref, inv_ref, v_ref, mixed_ref, mix_ref)
         query_terms = pick(prod(key_back.T, k_ref[doc]))
-        kd_ref[doc] = prod(key_back, stack(qm_ref[doc]))
-        vg_ref[doc] = (prod(key_weights, mixed_grad) + back_ref[doc]).astype(bf16)
         for base, terms in ((0, query_terms), (4, key_terms)):
             high = terms.astype(bf16).astype(f32)
             low = terms - high
@@ -354,8 +371,26 @@
                 held[pl.ds(row, groups, stride=16), :] = high[rows]
                 held[pl.ds(8 + row, groups, stride=16), :] = low[rows]
     out_ref[:, 0:16, :] = held[...].astype(bf16).reshape(groups, 16, channels)
-    terms = dot(ogt_ref[...], ctx_ref[...]).astype(bf16)
-    out_ref[:, 16:, :] = terms.reshape(groups, terms.shape[0] // groups, channels)
+    first = pltpu.make_async_copy(out_ref.at[:, 0:16, :], out_far.at[:, 0:16, :], sems.at[1])
+    first.start()
+    rest.wait()
+    first.wait()
+
+
+def direct_kernel(
+    scale, log_ref, t_ref, s_ref, cg_ref, qm_ref, km_ref, inv_ref, v_ref, back_ref, mixed_ref,
+    mix_ref, qd_ref, kd_ref, vg_ref,
+):
+    for doc in range(v_ref.shape[0]):
+        inverse = jnp.concatenate([inv_ref[doc * 2], inv_ref[doc * 2 + 1]], axis=0)
+        landmark = own_blocks(prod(inverse, mixed_ref[doc]))
+        back = token_back(scale, t_ref[doc], cg_ref[doc], landmark)
+        qd_ref[doc] = prod(back, stack(km_ref[doc]))
+        key_weights, key_back, mixed_grad = key_side(
+            scale, doc, log_ref, s_ref, inv_ref, v_ref, mixed_ref, mix_ref
+        )
+        kd_ref[doc] = prod(key_back, stack(qm_ref[doc]))
+        vg_ref[doc] = (prod(key_weights, mixed_grad) + back_ref[doc]).astype(bf16)
 
 
 def newton_back_kernel(scale, qm_ref, km_ref, mixed_ref, mix_ref, out_ref, held, *kept):
@@ -433,14 +468,17 @@
     refs[-1][...] = total.astype(bf16)
 
 
-def call(kernel, outs, *operands, scratch=(), smem=(), flops=1e8, size=2e6):
+def call(kernel, outs, *operands, scratch=(), smem=(), far=(), far_out=False, flops=1e8, size=2e6):
     vmem = pl.BlockSpec(memory_space=pltpu.VMEM)
     scalar = pl.BlockSpec(memory_space=pltpu.SMEM)
+    anywhere = pl.BlockSpec(memory_space=pl.ANY)
     return pl.pallas_call(
         kernel,
         out_shape=[jax.ShapeDtypeStruct(shape, kind) for shape, kind in outs],
-        in_specs=[scalar if i in smem else vmem for i in range(len(operands))],
-        out_specs=[vmem for _ in outs],
+        in_specs=[
+            scalar if i in smem else anywhere if i in far else vmem for i in range(len(operands))
+        ],
+        out_specs=[anywhere if far_out else vmem for _ in outs],
         scratch_shapes=list(scratch),
         compiler_params=pltpu.CompilerParams(vmem_limit_bytes=16 * 1024 * 1024),
         cost_estimate=pl.CostEstimate(
@@ -512,12 +550,12 @@
     )
     sent, context_grad, first_rows, last_rows = call(
         functools.partial(chunk_kernel, parts, rim, og_starts),
-        [((groups * 16, channels), f32), (rows_shape, f32)]
+        [((groups * 12, channels), f32), (rows_shape, f32)]
         + [((documents, 3 * rim, channels), bf16)] * 2,
         *og_parts, out_weight, value_vectors, weights, local_mixed, local_log,
     )
     sent, qm, km = lax.optimization_barrier((sent, qm, km))
-    got = exchange(sent, "seq")
+    got = exchange(sent.reshape(groups, 3, 4, channels), "seq").reshape(groups * 12, channels)
     ends = groups - 1
     above = lax.ppermute(last_rows, "seq", [(i, i + 1) for i in range(ends)])
     below = lax.ppermute(first_rows, "seq", [(i + 1, i) for i in range(ends)])
@@ -552,23 +590,36 @@
             ((documents, 2 * count, channels), f32),
         ],
         got, weights, inverse, conv,
+        scratch=[
+            pltpu.VMEM((units, count, count), f32),
+            pltpu.VMEM(rows_shape, f32),
+            pltpu.SemaphoreType.DMA((2,)),
+        ],
+        far=(2, 3),
     )
     near = [shift_by(context_b, 1, parts), shift_by(context_b, parts - 1, parts)]
-    sent, query_direct, key_direct, value_grad = call(
+    sent_shape = (groups, 16 + column_rows, channels)
+    (sent,) = call(
         functools.partial(main_kernel, scale),
-        [
-            ((groups, 16 + column_rows, channels), bf16),
-            (rows_shape, f32),
-            (rows_shape, f32),
-            (rows_shape, bf16),
+        [(sent_shape, bf16)],
+        logs, weights, scores, context_grad, inverse, queries, key_vectors, value_vectors,
+        og_turned, context_b, mixed, mix, landmark_mix,
+        scratch=[
+            pltpu.VMEM(sent_shape, bf16),
+            pltpu.VMEM((groups * 16, channels), f32),
+            pltpu.SemaphoreType.DMA((2,)),
         ],
-        logs, weights, scores, context_grad, qm, km, inverse, queries, key_vectors,
-        value_vectors, back, og_turned, context_b, mixed, mix, landmark_mix,
-        scratch=[pltpu.VMEM((groups * 16, channels), f32)],
+        far_out=True,
         flops=1e9,
     )
     sent, near, mix = lax.optimization_barrier((sent, near, mix))
     got = exchange(sent, "seq")
+    query_direct, key_direct, value_grad = call(
+        functools.partial(direct_kernel, scale),
+        [(rows_shape, f32), (rows_shape, f32), (rows_shape, bf16)],
+        logs, weights, scores, context_grad, qm, km, inverse, value_vectors, back, mixed, mix,
+        flops=1e9,
+    )
     far = [
         shift_by(jnp.concatenate([near[0], context_b, near[1]], axis=0), 3, parts),
         shift_by(jnp.concatenate([near[0], context_b], axis=0), parts - 3, parts),

time: 147 us -> 143 us (0.973)
  waiting for transfers between devices: 29.8 us -> 23.3 us
  Pallas kernels: 18.6 us -> 21.9 us
  local copies, waits for them, and re-layouts: 13.3 us -> 11.8 us
    ppermute x11, waiting for transfers between devices: 6.51 us -> 3.14 us  [shift_by(): return lax.ppermute(block, ('seq', 'head'), pairs)]
    all_to_all x4, waiting for transfers between devices: 22.5 us -> 19.2 us  [exchange(): return lax.all_to_all(blocks, axis, 0, 0, tiled=True)]
    pallas_call x13 -> x14, Pallas kernels: 18.6 us -> 21.9 us  [call(): pl.pallas_call(kernel, out_shape=[jax.ShapeDtypeStruct(shape, kind) for s...]
    unnamed x89, local copies, waits for them, and re-layouts: 11.8 us -> 10.3 us
  transfers between devices with their start and end apart: 17 -> 17, of which waited for: 7 -> 6; matrix products, arithmetic and copies ran while one was open for 1% -> 1% of each run, Pallas kernels for 9% -> 12%
where the time goes in v4:
time: 143 us; the launch traced here: 142 us
  starting transfers between devices  83.5 us (58%)
  waiting for transfers between devices  23.3 us (16%)
  Pallas kernels  21.9 us (15%)
  local copies, waits for them, and re-layouts  11.8 us (8%)
    ppermute x11, starting transfers between devices, shift_by(): return lax.ppermute(block, ('seq', 'head'), pairs)  39.9 us
    all_to_all x4, starting transfers between devices, exchange(): return lax.all_to_all(blocks, axis, 0, 0, tiled=True)  38.2 us
    pallas_call x14, Pallas kernels, call(): pl.pallas_call(kernel, out_shape=[jax.ShapeDtypeStruct(shape, kind) for s...  21.9 us
    all_to_all x4, waiting for transfers between devices, exchange(): return lax.all_to_all(blocks, axis, 0, 0, tiled=True)  19.2 us
    unnamed x89, local copies, waits for them, and re-layouts  10.3 us
    ppermute x1, starting transfers between devices, shards(): above = lax.ppermute(last_rows, 'seq', [(i, i + 1) for i in range(ends)])  3.54 us
    ppermute x11, waiting for transfers between devices, shift_by(): return lax.ppermute(block, ('seq', 'head'), pairs)  3.14 us
  transfers between devices with their start and end apart: 17, of which 6 were waited for; matrix products, arithmetic and copies ran while one was open for 1% of the time, Pallas kernels for 12%

profile of v4, /device:TPU:1, one launch (start us, length us, event | category | flops | bytes accessed | tf_op | source)
XLA Modules:
  0.0 141.7 jit_solution(18243661834317554131)
XLA Ops:
  0.6 0.0 copy-start.11
  0.7 0.9 copy-done.11
  1.5 0.8 copy-done.13
  2.4 0.8 shard_map.101
  3.1 1.0 copy-done
  4.2 0.1 shard_map.102
  4.3 0.0 copy-start.20
  4.3 6.7 %collective-permute-start.1 = (bf16[640,256]{1,0:T(8,128)(2,1)S(1)}, bf16[640,256]{1,0:T(8,128)(2,1)S(1)}, u32[]{:S(2)}, u32[]{:S(2)}) collective-permute-start(bf16[640,256]{1,0:T(8,128)(2,1)S(1)} %get-tuple-element.62), channel_id=1, source_target_pairs={{0,2},{1,3},{2,4},{3,5},{4,6},{5,7},{6,0},{7,1},{8,14},{9,15},{10,... | collective-permute-start | bytes 983048 | tf_op jit(solution)/shard_map/ppermute | solution.py:499
  11.0 1.9 %collective-permute-start.4 = (bf16[512,256]{1,0:T(8,128)(2,1)S(1)}, bf16[512,256]{1,0:T(8,128)(2,1)S(1)}, u32[]{:S(2)}, u32[]{:S(2)}) collective-permute-start(bf16[512,256]{1,0:T(8,128)(2,1)S(1)} %get-tuple-element.63), channel_id=1, source_target_pairs={{0,6},{1,7},{2,0},{3,1},{4,2},{5,3},{6,4},{7,5},{8,10},{9,11},{10,... | collective-permute-start | bytes 786440 | tf_op jit(solution)/shard_map/ppermute | solution.py:499
  12.9 14.3 %all-to-all-start = ((f32[64,8,128]{2,1,0:T(8,128)}), f32[64,8,128]{2,1,0:T(8,128)S(1)}, u32[]{:S(2)}, u32[]{:S(2)}) async-start(f32[64,8,128]{2,1,0:T(8,128)} %shard_map.101), calls=%async_computation | async-start | bytes 524288 | tf_op jit(solution)/shard_map/all_to_all | solution.py:491
  27.2 3.8 %collective-permute-start = (bf16[384,256]{1,0:T(8,128)(2,1)S(1)}, bf16[384,256]{1,0:T(8,128)(2,1)S(1)}, u32[]{:S(2)}, u32[]{:S(2)}) collective-permute-start(bf16[384,256]{1,0:T(8,128)(2,1)S(1)} %get-tuple-element.61), channel_id=1, source_target_pairs={{0,1},{1,2},{2,3},{3,4},{4,5},{5,6},{6,7},{7,0},{8,15},{9,8},{10,9... | collective-permute-start | bytes 589832 | tf_op jit(solution)/shard_map/ppermute | solution.py:499
  31.1 1.9 %collective-permute-start.6 = (bf16[384,256]{1,0:T(8,128)(2,1)S(1)}, bf16[384,256]{1,0:T(8,128)(2,1)S(1)}, u32[]{:S(2)}, u32[]{:S(2)}) collective-permute-start(bf16[384,256]{1,0:T(8,128)(2,1)S(1)} %get-tuple-element.64), channel_id=1, source_target_pairs={{0,7},{1,0},{2,1},{3,2},{4,3},{5,4},{6,5},{7,6},{8,9},{9,10},{10,1... | collective-permute-start | bytes 589832 | tf_op jit(solution)/shard_map/ppermute | solution.py:499
  33.0 0.7 slice.14
  33.7 2.7 %collective-permute-start.5 = (bf16[384,256]{1,0:T(8,128)(2,1)}, bf16[384,256]{1,0:T(8,128)(2,1)S(1)}, u32[]{:S(2)}, u32[]{:S(2)}) collective-permute-start(bf16[384,256]{1,0:T(8,128)(2,1)} %slice.14), channel_id=1, source_target_pairs={{0,7},{1,0},{2,1},{3,2},{4,3},{5,4},{6,5},{7,6},{8,9},{9,10},{10,1... | collective-permute-start | bytes 589832 | tf_op jit(solution)/shard_map/ppermute | solution.py:499
  36.5 0.0 collective-permute-done.1.refs_2_.refs_7_
  36.5 0.8 fusion
  37.2 5.1 %collective-permute-start.3 = (bf16[384,256]{1,0:T(8,128)(2,1)}, bf16[384,256]{1,0:T(8,128)(2,1)S(1)}, u32[]{:S(2)}, u32[]{:S(2)}) collective-permute-start(bf16[384,256]{1,0:T(8,128)(2,1)} %get-tuple-element.115), channel_id=1, source_target_pairs={{0,2},{1,3},{2,4},{3,5},{4,6},{5,7},{6,0},{7,1},{8,14},{9,15},{10,... | collective-permute-start | bytes 589832 | tf_op jit(solution)/shard_map/ppermute | solution.py:499
  42.3 2.5 %collective-permute-start.2 = (bf16[384,256]{1,0:T(8,128)(2,1)}, bf16[384,256]{1,0:T(8,128)(2,1)S(1)}, u32[]{:S(2)}, u32[]{:S(2)}) collective-permute-start(bf16[384,256]{1,0:T(8,128)(2,1)} %get-tuple-element.116), channel_id=1, source_target_pairs={{0,1},{1,2},{2,3},{3,4},{4,5},{5,6},{6,7},{7,0},{8,15},{9,8},{10,9... | collective-permute-start | bytes 589832 | tf_op jit(solution)/shard_map/ppermute | solution.py:499
  44.9 1.1 shard_map.103
  46.0 0.7 copy-done.22
  46.7 0.0 collective-permute-done.refs_1_.refs_6_
  46.7 0.0 collective-permute-done.6.refs_7_.refs_12_
  46.7 0.0 collective-permute-done.5.refs_5_.refs_10_
  46.7 1.5 %collective-permute-done.3.refs_4_.refs_9_ = bf16[384,256]{1,0:T(8,128)(2,1)S(1)} collective-permute-done((bf16[384,256]{1,0:T(8,128)(2,1)}, bf16[384,256]{1,0:T(8,128)(2,1)S(1)}, u32[]{:S(2)}, u32[]{:S(2)}) %collective-permute-start.3) | collective-permute-done | bytes 196640 | tf_op jit(solution)/shard_map/ppermute | solution.py:499
  48.2 1.6 %collective-permute-done.2.refs_3_.refs_8_ = bf16[384,256]{1,0:T(8,128)(2,1)S(1)} collective-permute-done((bf16[384,256]{1,0:T(8,128)(2,1)}, bf16[384,256]{1,0:T(8,128)(2,1)S(1)}, u32[]{:S(2)}, u32[]{:S(2)}) %collective-permute-start.2) | collective-permute-done | bytes 196640 | tf_op jit(solution)/shard_map/ppermute | solution.py:499
  49.8 1.6 %shard_map.104 = (f32[768,128]{1,0:T(8,128)}, f32[2,128,128]{2,1,0:T(8,128)S(1)}, bf16[2,48,128]{2,1,0:T(8,128)(2,1)S(1)}, bf16[2,48,128]{2,1,0:T(8,128)(2,1)S(1)}) custom-call(bf16[256,256]{1,0:T(8,128)(2,1)S(1)} %bitcast.9, bf16[384,256]{1,0:T(8,128)(2,1)S(1)} %collective-permute-done.refs_1_.refs_6_, ...), custom_call_target="tpu_custom_call" | custom-call | flops 100000000 | bytes 2000000 | tf_op jit(solution)/shard_map/pallas_call | solution.py:475
  51.4 0.7 copy-done.29
  52.1 13.0 %all-to-all-start.1 = ((f32[64,3,4,128]{3,2,1,0:T(4,128)}), f32[64,3,4,128]{3,2,1,0:T(4,128)S(1)}, u32[]{:S(2)}, u32[]{:S(2)}) async-start(f32[64,3,4,128]{3,2,1,0:T(4,128)} %bitcast.2), calls=%async_computation.1 | async-start | bytes 786432 | tf_op jit(solution)/shard_map/all_to_all | solution.py:491
  65.0 3.5 %collective-permute-start.7 = (bf16[2,48,128]{2,1,0:T(8,128)(2,1)S(1)}, bf16[2,48,128]{2,1,0:T(8,128)(2,1)S(1)}, u32[]{:S(2)}, u32[]{:S(2)}) collective-permute-start(bf16[2,48,128]{2,1,0:T(8,128)(2,1)S(1)} %get-tuple-element.73), channel_id=1, source_target_pairs={{0,8},{8,16},{16,24},{24,32},{32,40},{40,48},{48,56},{56,64},{64,7... | collective-permute-start | bytes 73736 | tf_op jit(solution)/shard_map/ppermute | solution.py:560
  68.6 1.9 %collective-permute-start.8 = (bf16[2,48,128]{2,1,0:T(8,128)(2,1)S(1)}, bf16[2,48,128]{2,1,0:T(8,128)(2,1)S(1)}, u32[]{:S(2)}, u32[]{:S(2)}) collective-permute-start(bf16[2,48,128]{2,1,0:T(8,128)(2,1)S(1)} %get-tuple-element.74), channel_id=1, source_target_pairs={{8,0},{16,8},{24,16},{32,24},{40,32},{48,40},{56,48},{64,56},{72,6... | collective-permute-start | bytes 73736 | tf_op jit(solution)/shard_map/ppermute | solution.py:561
  70.5 2.2 %shard_map.105.inv_far.inv_ref = f32[4,128,128]{2,1,0:T(8,128)S(1)} custom-call(f32[2,128,128]{2,1,0:T(8,128)S(1)} %get-tuple-element.75.qm_ref, f32[2,128,128]{2,1,0:T(8,128)S(1)} %get-tuple-element.76.km_ref), custom_call_target="tpu_custom_call" | custom-call | flops 2000000000 | bytes 2000000 | tf_op jit(solution)/shard_map/pallas_call | solution.py:475
  72.7 0.7 copy-done.7
  73.4 0.9 collective-permute-done.8.below_ref
  74.3 5.8 %all-to-all-done.1 = f32[64,3,4,128]{3,2,1,0:T(4,128)S(1)} async-done(((f32[64,3,4,128]{3,2,1,0:T(4,128)}), f32[64,3,4,128]{3,2,1,0:T(4,128)S(1)}, u32[]{:S(2)}, u32[]{:S(2)}) %all-to-all-start.1) | async-done | bytes 393248 | tf_op jit(solution)/shard_map/all_to_all | solution.py:491
  80.1 0.9 shard_map.106
  81.1 5.9 %all-to-all-start.2 = ((f32[64,8,128]{2,1,0:T(8,128)}), f32[64,8,128]{2,1,0:T(8,128)S(1)}, u32[]{:S(2)}, u32[]{:S(2)}) async-start(f32[64,8,128]{2,1,0:T(8,128)} %get-tuple-element.79), calls=%async_computation.2 | async-start | bytes 524288 | tf_op jit(solution)/shard_map/all_to_all | solution.py:491
  87.0 0.1 copy.11.taps_ref
  87.1 0.3 shard_map.108.ogt_ref
  87.4 0.6 copy-done.30
  88.0 1.5 %shard_map.107 = (f32[2,128,128]{2,1,0:T(8,128)S(1)}, f32[2,128,128]{2,1,0:T(8,128)S(1)}) custom-call(f32[33,2]{1,0:T(8,128)S(1)} %copy.11.taps_ref, bf16[2,128,128]{2,1,0:T(8,128)(2,1)S(1)} %copy-done.15, f32[2,128,128]{2,1,0:T(8,128)S(1)} %copy-done.30, bf16[2,48,128]{2,1,0:T(8,128)(2,1)S(1)} %copy-done.38, bf16[2,48,128]{2,1,0:T(8,128)(2,1)S(1)} %copy-done.40), custom_call_target="tpu_custom_call" | custom-call | flops 1000000000 | bytes 2000000 | tf_op jit(solution)/shard_map/pallas_call | solution.py:475
  89.5 0.6 copy-done.16
  90.1 0.6 copy-done.41
  90.7 9.4 %all-to-all-done.2 = f32[64,8,128]{2,1,0:T(8,128)S(1)} async-done(((f32[64,8,128]{2,1,0:T(8,128)}), f32[64,8,128]{2,1,0:T(8,128)S(1)}, u32[]{:S(2)}, u32[]{:S(2)}) %all-to-all-start.2) | async-done | bytes 262176 | tf_op jit(solution)/shard_map/all_to_all | solution.py:491
  100.1 0.9 copy-done.8
  101.1 0.9 copy-done.17
  102.0 0.8 shard_map.109
  102.8 1.9 %collective-permute-start.10 = (bf16[256,128]{1,0:T(8,128)(2,1)S(1)}, bf16[256,128]{1,0:T(8,128)(2,1)S(1)}, u32[]{:S(2)}, u32[]{:S(2)}) collective-permute-start(bf16[256,128]{1,0:T(8,128)(2,1)S(1)} %get-tuple-element.96.ctx_ref.refs_0_), channel_id=1, source_target_pairs={{0,7},{1,0},{2,1},{3,2},{4,3},{5,4},{6,5},{7,6},{8,9},{9,10},{10,1... | collective-permute-start | bytes 196616 | tf_op jit(solution)/shard_map/ppermute | solution.py:499
  104.7 4.6 %collective-permute-start.9 = (bf16[256,128]{1,0:T(8,128)(2,1)S(1)}, bf16[256,128]{1,0:T(8,128)(2,1)S(1)}, u32[]{:S(2)}, u32[]{:S(2)}) collective-permute-start(bf16[256,128]{1,0:T(8,128)(2,1)S(1)} %get-tuple-element.96.ctx_ref.refs_0_), channel_id=1, source_target_pairs={{0,1},{1,2},{2,3},{3,4},{4,5},{5,6},{6,7},{7,0},{8,15},{9,8},{10,9... | collective-permute-start | bytes 196616 | tf_op jit(solution)/shard_map/ppermute | solution.py:499
  109.3 2.9 %shard_map.110 = bf16[64,48,128]{2,1,0:T(8,128)(2,1)S(1)} custom-call(f32[8,128]{1,0:T(8,128)S(1)} %get-tuple-element.97.log_ref, f32[2,128,256]{2,1,0:T(8,128)S(1)} %copy-done.4, f32[2,128,256]{2,1,0:T(8,128)S(1)} %copy-done.23, f32[2,128,128]{2,1,0:T(8,128)S(1)} %copy-done.31, f32[4,128,128]{2,1,0:T(8,128)S(1)} %copy-done.9, ...), custom_call_target="tpu_custom_call" | custom-call | flops 1000000000 | bytes 2000000 | tf_op jit(solution)/shard_map/pallas_call | solution.py:475
  112.2 0.9 copy-done.6
  113.2 0.0 collective-permute-done.10.refs_2_
  113.2 0.0 collective-permute-done.9.refs_1_
  113.2 5.0 %all-to-all-start.3 = ((bf16[64,48,128]{2,1,0:T(8,128)(2,1)}), bf16[64,48,128]{2,1,0:T(8,128)(2,1)S(1)}, u32[]{:S(2)}, u32[]{:S(2)}) async-start(bf16[64,48,128]{2,1,0:T(8,128)(2,1)} %copy-done.6), calls=%async_computation.3 | async-start | bytes 1572864 | tf_op jit(solution)/shard_map/all_to_all | solution.py:491
  118.2 5.0 %collective-permute-start.12 = (bf16[512,128]{1,0:T(8,128)(2,1)S(1)}, bf16[512,128]{1,0:T(8,128)(2,1)S(1)}, u32[]{:S(2)}, u32[]{:S(2)}) collective-permute-start(bf16[512,128]{1,0:T(8,128)(2,1)S(1)} %pad_maximum_fusion.1), channel_id=1, source_target_pairs={{0,5},{1,6},{2,7},{3,0},{4,1},{5,2},{6,3},{7,4},{8,11},{9,12},{10,... | collective-permute-start | bytes 393224 | tf_op jit(solution)/shard_map/ppermute | solution.py:499
  123.3 0.0 copy-start.32
  123.3 3.7 %collective-permute-start.11 = (bf16[768,128]{1,0:T(8,128)(2,1)S(1)}, bf16[768,128]{1,0:T(8,128)(2,1)S(1)}, u32[]{:S(2)}, u32[]{:S(2)}) collective-permute-start(bf16[768,128]{1,0:T(8,128)(2,1)S(1)} %pad_maximum_fusion), channel_id=1, source_target_pairs={{0,3},{1,4},{2,5},{3,6},{4,7},{5,0},{6,1},{7,2},{8,13},{9,14},{10,... | collective-permute-start | bytes 589832 | tf_op jit(solution)/shard_map/ppermute | solution.py:499
  127.1 4.9 %shard_map.112.own_ref = f32[8,128]{1,0:T(8,128)S(1)} custom-call(f32[2,128,128]{2,1,0:T(8,128)S(1)} %copy-done.26, f32[2,128,128]{2,1,0:T(8,128)S(1)} %copy-done.28, f32[2,128,128]{2,1,0:T(8,128)S(1)} %copy-done.34, f32[2,128,128]{2,1,0:T(8,128)S(1)} %copy-done.36), custom_call_target="tpu_custom_call" | custom-call | flops 5000000000 | bytes 2000000 | tf_op jit(solution)/shard_map/pallas_call | solution.py:475
  132.0 0.0 copy-start.21
  132.0 3.1 %shard_map.113 = (f32[2,128,128]{2,1,0:T(8,128)S(1)}, f32[2,128,128]{2,1,0:T(8,128)S(1)}, bf16[2,128,128]{2,1,0:T(8,128)(2,1)}) custom-call(f32[8,128]{1,0:T(8,128)S(1)} %get-tuple-element.97.log_ref, f32[2,128,256]{2,1,0:T(8,128)S(1)} %copy-done.5, f32[2,128,256]{2,1,0:T(8,128)S(1)} %copy-done.24, f32[2,128,128]{2,1,0:T(8,128)S(1)} %copy-done.32, ...), custom_call_target="tpu_custom_call" | custom-call | flops 1000000000 | bytes 2000000 | tf_op jit(solution)/shard_map/pallas_call | solution.py:475
  135.2 0.6 copy-done.18
  135.8 0.0 collective-permute-done.11.refs_3_
  135.8 1.1 shard_map.111
  136.9 4.0 %all-to-all-done.3.got_ref = bf16[64,48,128]{2,1,0:T(8,128)(2,1)S(1)} async-done(((bf16[64,48,128]{2,1,0:T(8,128)(2,1)}), bf16[64,48,128]{2,1,0:T(8,128)(2,1)S(1)}, u32[]{:S(2)}, u32[]{:S(2)}) %all-to-all-start.3) | async-done | bytes 786464 | tf_op jit(solution)/shard_map/all_to_all | solution.py:491
  140.9 0.8 shard_map.114
  (77 shorter events, 0.2 us)
Async XLA Ops:
  0.6 2.5 %copy-start.2 = (bf16[2,128,256]{2,1,0:T(8,128)(2,1)S(1)}, bf16[2,128,256]{2,1,0:T(8,128)(2,1)}, u32[]{:S(2)}) copy-start(bf16[2,128,256]{2,1,0:T(8,128)(2,1)} %param.11) | copy-start | bytes 393220
  0.6 0.9 copy-start.11
  1.5 0.8 copy-start.13
  3.1 1.0 copy-start
  4.3 8.7 %copy-start.20 = (bf16[128,256]{1,0:T(8,128)(2,1)}, bf16[128,256]{1,0:T(8,128)(2,1)S(1)}, u32[]{:S(2)}) copy-start(bf16[128,256]{1,0:T(8,128)(2,1)S(1)} %get-tuple-element.105.refs_5_) | copy-start | bytes 196612
  4.3 32.2 %collective-permute-start.1 = (bf16[640,256]{1,0:T(8,128)(2,1)S(1)}, bf16[640,256]{1,0:T(8,128)(2,1)S(1)}, u32[]{:S(2)}, u32[]{:S(2)}) collective-permute-start(bf16[640,256]{1,0:T(8,128)(2,1)S(1)} %get-tuple-element.62), channel_id=1, source_target_pairs={{0,2},{1,3},{2,4},{3,5},{4,6},{5,7},{6,0},{7,1},{8,14},{9,15},{10,... | collective-permute-start | bytes 983048 | tf_op jit(solution)/shard_map/ppermute | solution.py:499
  11.0 22.0 %collective-permute-start.4 = (bf16[512,256]{1,0:T(8,128)(2,1)S(1)}, bf16[512,256]{1,0:T(8,128)(2,1)S(1)}, u32[]{:S(2)}, u32[]{:S(2)}) collective-permute-start(bf16[512,256]{1,0:T(8,128)(2,1)S(1)} %get-tuple-element.63), channel_id=1, source_target_pairs={{0,6},{1,7},{2,0},{3,1},{4,2},{5,3},{6,4},{7,5},{8,10},{9,11},{10,... | collective-permute-start | bytes 786440 | tf_op jit(solution)/shard_map/ppermute | solution.py:499
  12.9 31.9 %all-to-all-start = ((f32[64,8,128]{2,1,0:T(8,128)}), f32[64,8,128]{2,1,0:T(8,128)S(1)}, u32[]{:S(2)}, u32[]{:S(2)}) async-start(f32[64,8,128]{2,1,0:T(8,128)} %shard_map.101), calls=%async_computation | async-start | bytes 524288 | tf_op jit(solution)/shard_map/all_to_all | solution.py:491
  27.2 19.5 %collective-permute-start = (bf16[384,256]{1,0:T(8,128)(2,1)S(1)}, bf16[384,256]{1,0:T(8,128)(2,1)S(1)}, u32[]{:S(2)}, u32[]{:S(2)}) collective-permute-start(bf16[384,256]{1,0:T(8,128)(2,1)S(1)} %get-tuple-element.61), channel_id=1, source_target_pairs={{0,1},{1,2},{2,3},{3,4},{4,5},{5,6},{6,7},{7,0},{8,15},{9,8},{10,9... | collective-permute-start | bytes 589832 | tf_op jit(solution)/shard_map/ppermute | solution.py:499
  31.1 15.6 %collective-permute-start.6 = (bf16[384,256]{1,0:T(8,128)(2,1)S(1)}, bf16[384,256]{1,0:T(8,128)(2,1)S(1)}, u32[]{:S(2)}, u32[]{:S(2)}) collective-permute-start(bf16[384,256]{1,0:T(8,128)(2,1)S(1)} %get-tuple-element.64), channel_id=1, source_target_pairs={{0,7},{1,0},{2,1},{3,2},{4,3},{5,4},{6,5},{7,6},{8,9},{9,10},{10,1... | collective-permute-start | bytes 589832 | tf_op jit(solution)/shard_map/ppermute | solution.py:499
  33.7 11.1 %copy-start.12 = (bf16[2,128,128]{2,1,0:T(8,128)(2,1)S(1)}, bf16[2,128,128]{2,1,0:T(8,128)(2,1)}, u32[]{:S(2)}) copy-start(bf16[2,128,128]{2,1,0:T(8,128)(2,1)} %q_ref.5) | copy-start | bytes 196612
  33.7 11.1 %copy-start.14 = (bf16[2,128,128]{2,1,0:T(8,128)(2,1)S(1)}, bf16[2,128,128]{2,1,0:T(8,128)(2,1)}, u32[]{:S(2)}) copy-start(bf16[2,128,128]{2,1,0:T(8,128)(2,1)} %k_ref.5) | copy-start | bytes 196612
  33.7 11.1 %copy-start.15 = (bf16[2,128,128]{2,1,0:T(8,128)(2,1)S(1)}, bf16[2,128,128]{2,1,0:T(8,128)(2,1)}, u32[]{:S(2)}) copy-start(bf16[2,128,128]{2,1,0:T(8,128)(2,1)} %v_ref.7) | copy-start | bytes 196612
  33.7 16.1 %copy-start.1 = (bf16[128,2048]{1,0:T(8,128)(2,1)S(1)}, bf16[128,2048]{1,0:T(8,128)(2,1)}, u32[]{:S(2)}) copy-start(bf16[128,2048]{1,0:T(8,128)(2,1)} %refs_8_.1) | copy-start | bytes 1572868
  33.7 13.0 %collective-permute-start.5 = (bf16[384,256]{1,0:T(8,128)(2,1)}, bf16[384,256]{1,0:T(8,128)(2,1)S(1)}, u32[]{:S(2)}, u32[]{:S(2)}) collective-permute-start(bf16[384,256]{1,0:T(8,128)(2,1)} %slice.14), channel_id=1, source_target_pairs={{0,7},{1,0},{2,1},{3,2},{4,3},{5,4},{6,5},{7,6},{8,9},{9,10},{10,1... | collective-permute-start | bytes 589832 | tf_op jit(solution)/shard_map/ppermute | solution.py:499
  37.2 11.0 %collective-permute-start.3 = (bf16[384,256]{1,0:T(8,128)(2,1)}, bf16[384,256]{1,0:T(8,128)(2,1)S(1)}, u32[]{:S(2)}, u32[]{:S(2)}) collective-permute-start(bf16[384,256]{1,0:T(8,128)(2,1)} %get-tuple-element.115), channel_id=1, source_target_pairs={{0,2},{1,3},{2,4},{3,5},{4,6},{5,7},{6,0},{7,1},{8,14},{9,15},{10,... | collective-permute-start | bytes 589832 | tf_op jit(solution)/shard_map/ppermute | solution.py:499
  42.3 7.5 %collective-permute-start.2 = (bf16[384,256]{1,0:T(8,128)(2,1)}, bf16[384,256]{1,0:T(8,128)(2,1)S(1)}, u32[]{:S(2)}, u32[]{:S(2)}) collective-permute-start(bf16[384,256]{1,0:T(8,128)(2,1)} %get-tuple-element.116), channel_id=1, source_target_pairs={{0,1},{1,2},{2,3},{3,4},{4,5},{5,6},{6,7},{7,0},{8,15},{9,8},{10,9... | collective-permute-start | bytes 589832 | tf_op jit(solution)/shard_map/ppermute | solution.py:499
  46.0 0.7 copy-start.22
  46.7 4.7 %copy-start.3 = (f32[2,128,256]{2,1,0:T(8,128)}, f32[2,128,256]{2,1,0:T(8,128)S(1)}, u32[]{:S(2)}) copy-start(f32[2,128,256]{2,1,0:T(8,128)S(1)} %get-tuple-element.66.refs_10_.t_ref) | copy-start | bytes 786436
  46.7 23.8 %copy-start.25 = (f32[2,128,128]{2,1,0:T(8,128)}, f32[2,128,128]{2,1,0:T(8,128)S(1)}, u32[]{:S(2)}) copy-start(f32[2,128,128]{2,1,0:T(8,128)S(1)} %get-tuple-element.75.qm_ref) | copy-start | bytes 393220
  46.7 23.9 %copy-start.27 = (f32[2,128,128]{2,1,0:T(8,128)}, f32[2,128,128]{2,1,0:T(8,128)S(1)}, u32[]{:S(2)}) copy-start(f32[2,128,128]{2,1,0:T(8,128)S(1)} %get-tuple-element.76.km_ref) | copy-start | bytes 393220
  51.4 0.7 copy-start.29
  52.1 28.1 %all-to-all-start.1 = ((f32[64,3,4,128]{3,2,1,0:T(4,128)}), f32[64,3,4,128]{3,2,1,0:T(4,128)S(1)}, u32[]{:S(2)}, u32[]{:S(2)}) async-start(f32[64,3,4,128]{3,2,1,0:T(4,128)} %bitcast.2), calls=%async_computation.1 | async-start | bytes 786432 | tf_op jit(solution)/shard_map/all_to_all | solution.py:491
  65.0 8.4 %collective-permute-start.7 = (bf16[2,48,128]{2,1,0:T(8,128)(2,1)S(1)}, bf16[2,48,128]{2,1,0:T(8,128)(2,1)S(1)}, u32[]{:S(2)}, u32[]{:S(2)}) collective-permute-start(bf16[2,48,128]{2,1,0:T(8,128)(2,1)S(1)} %get-tuple-element.73), channel_id=1, source_target_pairs={{0,8},{8,16},{16,24},{24,32},{32,40},{40,48},{48,56},{56,64},{64,7... | collective-permute-start | bytes 73736 | tf_op jit(solution)/shard_map/ppermute | solution.py:560
  68.6 5.7 %collective-permute-start.8 = (bf16[2,48,128]{2,1,0:T(8,128)(2,1)S(1)}, bf16[2,48,128]{2,1,0:T(8,128)(2,1)S(1)}, u32[]{:S(2)}, u32[]{:S(2)}) collective-permute-start(bf16[2,48,128]{2,1,0:T(8,128)(2,1)S(1)} %get-tuple-element.74), channel_id=1, source_target_pairs={{8,0},{16,8},{24,16},{32,24},{40,32},{48,40},{56,48},{64,56},{72,6... | collective-permute-start | bytes 73736 | tf_op jit(solution)/shard_map/ppermute | solution.py:561
  72.7 0.7 copy-start.7
  73.4 7.7 %copy-start.37 = (bf16[2,48,128]{2,1,0:T(8,128)(2,1)}, bf16[2,48,128]{2,1,0:T(8,128)(2,1)S(1)}, u32[]{:S(2)}) copy-start(bf16[2,48,128]{2,1,0:T(8,128)(2,1)S(1)} %collective-permute-done.7.above_ref) | copy-start | bytes 73732
  74.3 6.7 %copy-start.39 = (bf16[2,48,128]{2,1,0:T(8,128)(2,1)}, bf16[2,48,128]{2,1,0:T(8,128)(2,1)S(1)}, u32[]{:S(2)}) copy-start(bf16[2,48,128]{2,1,0:T(8,128)(2,1)S(1)} %collective-permute-done.8.below_ref) | copy-start | bytes 73732
  81.1 5.9 %copy-start.43 = (f32[33,2]{0,1:T(2,128)S(1)}, f32[33,2]{0,1:T(2,128)}, u32[]{:S(2)}) copy-start(f32[33,2]{0,1:T(2,128)} %param.9) | copy-start | bytes 796
  81.1 19.1 %all-to-all-start.2 = ((f32[64,8,128]{2,1,0:T(8,128)}), f32[64,8,128]{2,1,0:T(8,128)S(1)}, u32[]{:S(2)}, u32[]{:S(2)}) async-start(f32[64,8,128]{2,1,0:T(8,128)} %get-tuple-element.79), calls=%async_computation.2 | async-start | bytes 524288 | tf_op jit(solution)/shard_map/all_to_all | solution.py:491
  87.1 0.9 copy-start.30
  87.1 0.9 copy-start.38
  87.1 0.9 copy-start.40
  88.0 12.1 %copy-start.4 = (f32[2,128,256]{2,1,0:T(8,128)S(1)}, f32[2,128,256]{2,1,0:T(8,128)}, u32[]{:S(2)}) copy-start(f32[2,128,256]{2,1,0:T(8,128)} %copy-done.3) | copy-start | bytes 786436
  89.4 0.6 copy-start.16
  90.1 0.7 copy-start.41
  100.1 1.0 copy-start.8
  101.1 0.9 copy-start.17
  102.0 7.3 %copy-start.9 = (f32[4,128,128]{2,1,0:T(8,128)S(1)}, f32[4,128,128]{2,1,0:T(8,128)}, u32[]{:S(2)}) copy-start(f32[4,128,128]{2,1,0:T(8,128)} %copy-done.7) | copy-start | bytes 786436
  102.0 7.3 %copy-start.23 = (f32[2,128,256]{2,1,0:T(8,128)S(1)}, f32[2,128,256]{2,1,0:T(8,128)}, u32[]{:S(2)}) copy-start(f32[2,128,256]{2,1,0:T(8,128)} %copy-done.22) | copy-start | bytes 786436
  102.0 7.4 %copy-start.31 = (f32[2,128,128]{2,1,0:T(8,128)S(1)}, f32[2,128,128]{2,1,0:T(8,128)}, u32[]{:S(2)}) copy-start(f32[2,128,128]{2,1,0:T(8,128)} %copy-done.29) | copy-start | bytes 393220
  102.8 9.4 %copy-start.33 = (f32[2,128,128]{2,1,0:T(8,128)}, f32[2,128,128]{2,1,0:T(8,128)S(1)}, u32[]{:S(2)}) copy-start(f32[2,128,128]{2,1,0:T(8,128)S(1)} %get-tuple-element.100.mixed_ref) | copy-start | bytes 393220
  102.8 9.4 %copy-start.35 = (f32[2,128,128]{2,1,0:T(8,128)}, f32[2,128,128]{2,1,0:T(8,128)S(1)}, u32[]{:S(2)}) copy-start(f32[2,128,128]{2,1,0:T(8,128)S(1)} %get-tuple-element.107.mix_ref) | copy-start | bytes 393220
  102.8 10.4 %collective-permute-start.10 = (bf16[256,128]{1,0:T(8,128)(2,1)S(1)}, bf16[256,128]{1,0:T(8,128)(2,1)S(1)}, u32[]{:S(2)}, u32[]{:S(2)}) collective-permute-start(bf16[256,128]{1,0:T(8,128)(2,1)S(1)} %get-tuple-element.96.ctx_ref.refs_0_), channel_id=1, source_target_pairs={{0,7},{1,0},{2,1},{3,2},{4,3},{5,4},{6,5},{7,6},{8,9},{9,10},{10,1... | collective-permute-start | bytes 196616 | tf_op jit(solution)/shard_map/ppermute | solution.py:499
  104.7 8.4 %collective-permute-start.9 = (bf16[256,128]{1,0:T(8,128)(2,1)S(1)}, bf16[256,128]{1,0:T(8,128)(2,1)S(1)}, u32[]{:S(2)}, u32[]{:S(2)}) collective-permute-start(bf16[256,128]{1,0:T(8,128)(2,1)S(1)} %get-tuple-element.96.ctx_ref.refs_0_), channel_id=1, source_target_pairs={{0,1},{1,2},{2,3},{3,4},{4,5},{5,6},{6,7},{7,0},{8,15},{9,8},{10,9... | collective-permute-start | bytes 196616 | tf_op jit(solution)/shard_map/ppermute | solution.py:499
  112.2 0.9 copy-start.6
  113.2 27.8 %all-to-all-start.3 = ((bf16[64,48,128]{2,1,0:T(8,128)(2,1)}), bf16[64,48,128]{2,1,0:T(8,128)(2,1)S(1)}, u32[]{:S(2)}, u32[]{:S(2)}) async-start(bf16[64,48,128]{2,1,0:T(8,128)(2,1)} %copy-done.6), calls=%async_computation.3 | async-start | bytes 1572864 | tf_op jit(solution)/shard_map/all_to_all | solution.py:491
  118.2 8.9 %copy-start.36 = (f32[2,128,128]{2,1,0:T(8,128)S(1)}, f32[2,128,128]{2,1,0:T(8,128)}, u32[]{:S(2)}) copy-start(f32[2,128,128]{2,1,0:T(8,128)} %copy-done.35) | copy-start | bytes 393220
  118.2 8.9 %copy-start.26 = (f32[2,128,128]{2,1,0:T(8,128)S(1)}, f32[2,128,128]{2,1,0:T(8,128)}, u32[]{:S(2)}) copy-start(f32[2,128,128]{2,1,0:T(8,128)} %copy-done.25) | copy-start | bytes 393220
  118.2 8.9 %copy-start.28 = (f32[2,128,128]{2,1,0:T(8,128)S(1)}, f32[2,128,128]{2,1,0:T(8,128)}, u32[]{:S(2)}) copy-start(f32[2,128,128]{2,1,0:T(8,128)} %copy-done.27) | copy-start | bytes 393220
  118.2 8.9 %copy-start.34 = (f32[2,128,128]{2,1,0:T(8,128)S(1)}, f32[2,128,128]{2,1,0:T(8,128)}, u32[]{:S(2)}) copy-start(f32[2,128,128]{2,1,0:T(8,128)} %copy-done.33) | copy-start | bytes 393220
  118.2 17.6 %collective-permute-start.12 = (bf16[512,128]{1,0:T(8,128)(2,1)S(1)}, bf16[512,128]{1,0:T(8,128)(2,1)S(1)}, u32[]{:S(2)}, u32[]{:S(2)}) collective-permute-start(bf16[512,128]{1,0:T(8,128)(2,1)S(1)} %pad_maximum_fusion.1), channel_id=1, source_target_pairs={{0,5},{1,6},{2,7},{3,0},{4,1},{5,2},{6,3},{7,4},{8,11},{9,12},{10,... | collective-permute-start | bytes 393224 | tf_op jit(solution)/shard_map/ppermute | solution.py:499
  123.3 8.7 %copy-start.5 = (f32[2,128,256]{2,1,0:T(8,128)S(1)}, f32[2,128,256]{2,1,0:T(8,128)}, u32[]{:S(2)}) copy-start(f32[2,128,256]{2,1,0:T(8,128)} %copy-done.3) | copy-start | bytes 786436
  123.3 8.7 %copy-start.10 = (f32[4,128,128]{2,1,0:T(8,128)S(1)}, f32[4,128,128]{2,1,0:T(8,128)}, u32[]{:S(2)}) copy-start(f32[4,128,128]{2,1,0:T(8,128)} %copy-done.7) | copy-start | bytes 786436
  123.3 8.7 %copy-start.24 = (f32[2,128,256]{2,1,0:T(8,128)S(1)}, f32[2,128,256]{2,1,0:T(8,128)}, u32[]{:S(2)}) copy-start(f32[2,128,256]{2,1,0:T(8,128)} %copy-done.22) | copy-start | bytes 786436
  123.3 8.7 %copy-start.32 = (f32[2,128,128]{2,1,0:T(8,128)S(1)}, f32[2,128,128]{2,1,0:T(8,128)}, u32[]{:S(2)}) copy-start(f32[2,128,128]{2,1,0:T(8,128)} %copy-done.29) | copy-start | bytes 393220
  123.3 8.7 %copy-start.42 = (f32[2,128,128]{2,1,0:T(8,128)S(1)}, f32[2,128,128]{2,1,0:T(8,128)}, u32[]{:S(2)}) copy-start(f32[2,128,128]{2,1,0:T(8,128)} %copy-done.41) | copy-start | bytes 393220
  123.3 12.5 %collective-permute-start.11 = (bf16[768,128]{1,0:T(8,128)(2,1)S(1)}, bf16[768,128]{1,0:T(8,128)(2,1)S(1)}, u32[]{:S(2)}, u32[]{:S(2)}) collective-permute-start(bf16[768,128]{1,0:T(8,128)(2,1)S(1)} %pad_maximum_fusion), channel_id=1, source_target_pairs={{0,3},{1,4},{2,5},{3,6},{4,7},{5,0},{6,1},{7,2},{8,13},{9,14},{10,... | collective-permute-start | bytes 589832 | tf_op jit(solution)/shard_map/ppermute | solution.py:499
  132.0 3.8 %copy-start.21 = (bf16[128,256]{1,0:T(8,128)(2,1)S(1)}, bf16[128,256]{1,0:T(8,128)(2,1)}, u32[]{:S(2)}) copy-start(bf16[128,256]{1,0:T(8,128)(2,1)} %copy-done.20) | copy-start | bytes 196612
  135.2 0.6 copy-start.18
  135.8 5.1 %copy-start.19 = (f32[2,128,128]{2,1,0:T(8,128)S(1)}, f32[2,128,128]{2,1,0:T(8,128)}, u32[]{:S(2)}) copy-start(f32[2,128,128]{2,1,0:T(8,128)} %copy-done.18) | copy-start | bytes 393220

commit v5 on v4

--- a/solution.py
+++ b/solution.py
@@ -468,7 +468,7 @@
     refs[-1][...] = total.astype(bf16)
 
 
-def call(kernel, outs, *operands, scratch=(), smem=(), far=(), far_out=False, flops=1e8, size=2e6):
+def call(kernel, outs, *operands, scratch=(), smem=(), far=(), far_out=False, grant=16, flops=1e8, size=2e6):
     vmem = pl.BlockSpec(memory_space=pltpu.VMEM)
     scalar = pl.BlockSpec(memory_space=pltpu.SMEM)
     anywhere = pl.BlockSpec(memory_space=pl.ANY)
@@ -480,7 +480,7 @@
         ],
         out_specs=[anywhere if far_out else vmem for _ in outs],
         scratch_shapes=list(scratch),
-        compiler_params=pltpu.CompilerParams(vmem_limit_bytes=16 * 1024 * 1024),
+        compiler_params=pltpu.CompilerParams(vmem_limit_bytes=grant * 1024 * 1024),
         cost_estimate=pl.CostEstimate(
             flops=int(flops), bytes_accessed=int(size), transcendentals=0
         ),
@@ -516,7 +516,9 @@
     units = 2 * documents
     saved = (ITERS, units, count, count)
 
-    (sent,) = call(means_kernel, [((groups, 8, channels), f32)], queries, key_vectors)
+    (sent,) = call(
+        means_kernel, [((groups, 8, channels), f32)], queries, key_vectors, grant=60
+    )
     own_grad, sent = lax.optimization_barrier((out_grad, sent))
     got = exchange(sent, "seq").reshape(groups * 8, channels)
     own_grad = own_grad.reshape(documents * tokens, own_width)
@@ -526,6 +528,7 @@
         [((rows + pieces * channels, own_width), bf16) for pieces in (1, 1, 3, 2)]
         + [((channels, own_width), bf16)],
         own_grad, out_weight,
+        grant=60,
     )
     up_two, down_two = shift_by(up_two, 2, parts), shift_by(down_two, parts - 2, parts)
     up, down = shift_by(up, 1, parts), shift_by(down, parts - 1, parts)
@@ -596,6 +599,7 @@
             pltpu.SemaphoreType.DMA((2,)),
         ],
         far=(2, 3),
+        grant=60,
     )
     near = [shift_by(context_b, 1, parts), shift_by(context_b, parts - 1, parts)]
     sent_shape = (groups, 16 + column_rows, channels)
@@ -610,6 +614,7 @@
             pltpu.SemaphoreType.DMA((2,)),
         ],
         far_out=True,
+        grant=60,
         flops=1e9,
     )
     sent, near, mix = lax.optimization_barrier((sent, near, mix))

time: 143 us -> 142 us (level)
  local copies, waits for them, and re-layouts: 11.8 us -> 3.85 us
  Pallas kernels: 21.9 us -> 29 us
    pallas_call x14, Pallas kernels: 21.9 us -> 29 us  [call(): pl.pallas_call(kernel, out_shape=[jax.ShapeDtypeStruct(shape, kind) for s...]
    unnamed x89 -> x49, local copies, waits for them, and re-layouts: 10.3 us -> 3.81 us
  transfers between devices with their start and end apart: 17 -> 17, of which waited for: 6 -> 7; matrix products, arithmetic and copies ran while one was open for 1% -> 0% of each run, Pallas kernels for 12% -> 13%
where the time goes in v5:
time: 142 us; the launch traced here: 141 us
  starting transfers between devices  82.8 us (58%)
  Pallas kernels  29 us (20%)
  waiting for transfers between devices  24.6 us (17%)
  local copies, waits for them, and re-layouts  3.85 us (3%)
    ppermute x11, starting transfers between devices, shift_by(): return lax.ppermute(block, ('seq', 'head'), pairs)  39.9 us
    all_to_all x4, starting transfers between devices, exchange(): return lax.all_to_all(blocks, axis, 0, 0, tiled=True)  37.4 us
    pallas_call x14, Pallas kernels, call(): pl.pallas_call(kernel, out_shape=[jax.ShapeDtypeStruct(shape, kind) for s...  29 us
    all_to_all x4, waiting for transfers between devices, exchange(): return lax.all_to_all(blocks, axis, 0, 0, tiled=True)  19.8 us
    ppermute x11, waiting for transfers between devices, shift_by(): return lax.ppermute(block, ('seq', 'head'), pairs)  3.89 us
    unnamed x49, local copies, waits for them, and re-layouts  3.81 us
    ppermute x1, starting transfers between devices, shards(): above = lax.ppermute(last_rows, 'seq', [(i, i + 1) for i in range(ends)])  3.54 us
  transfers between devices with their start and end apart: 17, of which 7 were waited for; matrix products, arithmetic and copies ran while one was open for 0% of the time, Pallas kernels for 13%

profile of v5, /device:TPU:1, one launch (start us, length us, event | category | flops | bytes accessed | tf_op | source)
XLA Modules:
  0.0 141.5 jit_solution(9212105403531064432)
XLA Ops:
  0.6 1.6 %shard_map.101 = f32[64,8,128]{2,1,0:T(8,128)} custom-call(bf16[2,128,128]{2,1,0:T(8,128)(2,1)} %q_ref.5, bf16[2,128,128]{2,1,0:T(8,128)(2,1)} %k_ref.5), custom_call_target="tpu_custom_call" | custom-call | flops 100000000 | bytes 2000000 | tf_op jit(solution)/shard_map/pallas_call | solution.py:475
  2.3 2.1 %shard_map.102 = (bf16[384,256]{1,0:T(8,128)(2,1)}, bf16[384,256]{1,0:T(8,128)(2,1)}, bf16[640,256]{1,0:T(8,128)(2,1)}, bf16[512,256]{1,0:T(8,128)(2,1)}, bf16[128,256]{1,0:T(8,128)(2,1)}) custom-call(bf16[256,256]{1,0:T(8,128)(2,1)} %bitcast.8, bf16[128,2048]{1,0:T(8,128)(2,1)} %refs_8_.1), custom_call_target="tpu_custom_call" | custom-call | flops 100000000 | bytes 2000000 | tf_op jit(solution)/shard_map/pallas_call | solution.py:475
  4.4 6.7 %collective-permute-start.1 = (bf16[640,256]{1,0:T(8,128)(2,1)}, bf16[640,256]{1,0:T(8,128)(2,1)S(1)}, u32[]{:S(2)}, u32[]{:S(2)}) collective-permute-start(bf16[640,256]{1,0:T(8,128)(2,1)} %get-tuple-element.62), channel_id=1, source_target_pairs={{0,2},{1,3},{2,4},{3,5},{4,6},{5,7},{6,0},{7,1},{8,14},{9,15},{10,... | collective-permute-start | bytes 983048 | tf_op jit(solution)/shard_map/ppermute | solution.py:499
  11.1 1.9 %collective-permute-start.4 = (bf16[512,256]{1,0:T(8,128)(2,1)}, bf16[512,256]{1,0:T(8,128)(2,1)S(1)}, u32[]{:S(2)}, u32[]{:S(2)}) collective-permute-start(bf16[512,256]{1,0:T(8,128)(2,1)} %get-tuple-element.63), channel_id=1, source_target_pairs={{0,6},{1,7},{2,0},{3,1},{4,2},{5,3},{6,4},{7,5},{8,10},{9,11},{10,... | collective-permute-start | bytes 786440 | tf_op jit(solution)/shard_map/ppermute | solution.py:499
  13.0 14.3 %all-to-all-start = ((f32[64,8,128]{2,1,0:T(8,128)}), f32[64,8,128]{2,1,0:T(8,128)S(1)}, u32[]{:S(2)}, u32[]{:S(2)}) async-start(f32[64,8,128]{2,1,0:T(8,128)} %shard_map.101), calls=%async_computation | async-start | bytes 524288 | tf_op jit(solution)/shard_map/all_to_all | solution.py:491
  27.4 3.8 %collective-permute-start = (bf16[384,256]{1,0:T(8,128)(2,1)}, bf16[384,256]{1,0:T(8,128)(2,1)S(1)}, u32[]{:S(2)}, u32[]{:S(2)}) collective-permute-start(bf16[384,256]{1,0:T(8,128)(2,1)} %get-tuple-element.61), channel_id=1, source_target_pairs={{0,1},{1,2},{2,3},{3,4},{4,5},{5,6},{6,7},{7,0},{8,15},{9,8},{10,9... | collective-permute-start | bytes 589832 | tf_op jit(solution)/shard_map/ppermute | solution.py:499
  31.2 1.9 %collective-permute-start.6 = (bf16[384,256]{1,0:T(8,128)(2,1)}, bf16[384,256]{1,0:T(8,128)(2,1)S(1)}, u32[]{:S(2)}, u32[]{:S(2)}) collective-permute-start(bf16[384,256]{1,0:T(8,128)(2,1)} %get-tuple-element.64), channel_id=1, source_target_pairs={{0,7},{1,0},{2,1},{3,2},{4,3},{5,4},{6,5},{7,6},{8,9},{9,10},{10,1... | collective-permute-start | bytes 589832 | tf_op jit(solution)/shard_map/ppermute | solution.py:499
  33.1 0.0 collective-permute-done.4.refs_6_.refs_11_
  33.2 0.0 copy-start.8
  33.2 0.0 copy-start.9
  33.2 0.0 copy-start.10
  33.2 0.0 copy-start
  33.2 2.7 %collective-permute-start.5 = (bf16[384,256]{1,0:T(8,128)(2,1)S(1)}, bf16[384,256]{1,0:T(8,128)(2,1)S(1)}, u32[]{:S(2)}, u32[]{:S(2)}) collective-permute-start(bf16[384,256]{1,0:T(8,128)(2,1)S(1)} %slice.14), channel_id=1, source_target_pairs={{0,7},{1,0},{2,1},{3,2},{4,3},{5,4},{6,5},{7,6},{8,9},{9,10},{10,1... | collective-permute-start | bytes 589832 | tf_op jit(solution)/shard_map/ppermute | solution.py:499
  35.9 0.0 collective-permute-done.1.refs_2_.refs_7_
  36.0 5.1 %collective-permute-start.3 = (bf16[384,256]{1,0:T(8,128)(2,1)S(1)}, bf16[384,256]{1,0:T(8,128)(2,1)S(1)}, u32[]{:S(2)}, u32[]{:S(2)}) collective-permute-start(bf16[384,256]{1,0:T(8,128)(2,1)S(1)} %get-tuple-element.115), channel_id=1, source_target_pairs={{0,2},{1,3},{2,4},{3,5},{4,6},{5,7},{6,0},{7,1},{8,14},{9,15},{10,... | collective-permute-start | bytes 589832 | tf_op jit(solution)/shard_map/ppermute | solution.py:499
  41.1 2.5 %collective-permute-start.2 = (bf16[384,256]{1,0:T(8,128)(2,1)S(1)}, bf16[384,256]{1,0:T(8,128)(2,1)S(1)}, u32[]{:S(2)}, u32[]{:S(2)}) collective-permute-start(bf16[384,256]{1,0:T(8,128)(2,1)S(1)} %get-tuple-element.116), channel_id=1, source_target_pairs={{0,1},{1,2},{2,3},{3,4},{4,5},{5,6},{6,7},{7,0},{8,15},{9,8},{10,9... | collective-permute-start | bytes 589832 | tf_op jit(solution)/shard_map/ppermute | solution.py:499
  43.6 0.0 all-to-all-done
  43.6 0.0 copy-start.1
  43.6 1.1 shard_map.103
  44.8 0.0 collective-permute-done.refs_1_.refs_6_
  44.8 0.0 collective-permute-done.6.refs_7_.refs_12_
  44.8 0.0 collective-permute-done.5.refs_5_.refs_10_
  44.8 2.0 %collective-permute-done.3.refs_4_.refs_9_ = bf16[384,256]{1,0:T(8,128)(2,1)S(1)} collective-permute-done((bf16[384,256]{1,0:T(8,128)(2,1)S(1)}, bf16[384,256]{1,0:T(8,128)(2,1)S(1)}, u32[]{:S(2)}, u32[]{:S(2)}) %collective-permute-start.3) | collective-permute-done | bytes 196640 | tf_op jit(solution)/shard_map/ppermute | solution.py:499
  46.8 1.6 %collective-permute-done.2.refs_3_.refs_8_ = bf16[384,256]{1,0:T(8,128)(2,1)S(1)} collective-permute-done((bf16[384,256]{1,0:T(8,128)(2,1)S(1)}, bf16[384,256]{1,0:T(8,128)(2,1)S(1)}, u32[]{:S(2)}, u32[]{:S(2)}) %collective-permute-start.2) | collective-permute-done | bytes 196640 | tf_op jit(solution)/shard_map/ppermute | solution.py:499
  48.4 1.6 %shard_map.104 = (f32[768,128]{1,0:T(8,128)}, f32[2,128,128]{2,1,0:T(8,128)S(1)}, bf16[2,48,128]{2,1,0:T(8,128)(2,1)S(1)}, bf16[2,48,128]{2,1,0:T(8,128)(2,1)S(1)}) custom-call(bf16[256,256]{1,0:T(8,128)(2,1)S(1)} %bitcast.9, bf16[384,256]{1,0:T(8,128)(2,1)S(1)} %collective-permute-done.refs_1_.refs_6_, ...), custom_call_target="tpu_custom_call" | custom-call | flops 100000000 | bytes 2000000 | tf_op jit(solution)/shard_map/pallas_call | solution.py:475
  50.0 13.0 %all-to-all-start.1 = ((f32[64,3,4,128]{3,2,1,0:T(4,128)}), f32[64,3,4,128]{3,2,1,0:T(4,128)S(1)}, u32[]{:S(2)}, u32[]{:S(2)}) async-start(f32[64,3,4,128]{3,2,1,0:T(4,128)} %bitcast.2), calls=%async_computation.1 | async-start | bytes 786432 | tf_op jit(solution)/shard_map/all_to_all | solution.py:491
  62.9 3.5 %collective-permute-start.7 = (bf16[2,48,128]{2,1,0:T(8,128)(2,1)S(1)}, bf16[2,48,128]{2,1,0:T(8,128)(2,1)S(1)}, u32[]{:S(2)}, u32[]{:S(2)}) collective-permute-start(bf16[2,48,128]{2,1,0:T(8,128)(2,1)S(1)} %get-tuple-element.73), channel_id=1, source_target_pairs={{0,8},{8,16},{16,24},{24,32},{32,40},{40,48},{48,56},{56,64},{64,7... | collective-permute-start | bytes 73736 | tf_op jit(solution)/shard_map/ppermute | solution.py:563
  66.5 1.9 %collective-permute-start.8 = (bf16[2,48,128]{2,1,0:T(8,128)(2,1)S(1)}, bf16[2,48,128]{2,1,0:T(8,128)(2,1)S(1)}, u32[]{:S(2)}, u32[]{:S(2)}) collective-permute-start(bf16[2,48,128]{2,1,0:T(8,128)(2,1)S(1)} %get-tuple-element.74), channel_id=1, source_target_pairs={{8,0},{16,8},{24,16},{32,24},{40,32},{48,40},{56,48},{64,56},{72,6... | collective-permute-start | bytes 73736 | tf_op jit(solution)/shard_map/ppermute | solution.py:564
  68.4 2.2 %shard_map.105.inv_far.inv_ref = f32[4,128,128]{2,1,0:T(8,128)S(1)} custom-call(f32[2,128,128]{2,1,0:T(8,128)S(1)} %get-tuple-element.75.qm_ref, f32[2,128,128]{2,1,0:T(8,128)S(1)} %get-tuple-element.76.km_ref), custom_call_target="tpu_custom_call" | custom-call | flops 2000000000 | bytes 2000000 | tf_op jit(solution)/shard_map/pallas_call | solution.py:475
  70.6 0.7 copy-done.6
  71.3 0.0 collective-permute-done.7.above_ref
  71.3 1.0 collective-permute-done.8.below_ref
  72.2 5.8 %all-to-all-done.1 = f32[64,3,4,128]{3,2,1,0:T(4,128)S(1)} async-done(((f32[64,3,4,128]{3,2,1,0:T(4,128)}), f32[64,3,4,128]{3,2,1,0:T(4,128)S(1)}, u32[]{:S(2)}, u32[]{:S(2)}) %all-to-all-start.1) | async-done | bytes 393248 | tf_op jit(solution)/shard_map/all_to_all | solution.py:491
  78.0 0.9 shard_map.106
  78.9 0.6 copy-done.20
  79.5 5.8 %all-to-all-start.2 = ((f32[64,8,128]{2,1,0:T(8,128)}), f32[64,8,128]{2,1,0:T(8,128)S(1)}, u32[]{:S(2)}, u32[]{:S(2)}) async-start(f32[64,8,128]{2,1,0:T(8,128)} %get-tuple-element.79), calls=%async_computation.2 | async-start | bytes 524288 | tf_op jit(solution)/shard_map/all_to_all | solution.py:491
  85.3 0.1 copy.11.taps_ref
  85.4 0.3 shard_map.108.ogt_ref
  85.7 1.0 copy-done.2
  86.7 1.5 %shard_map.107 = (f32[2,128,128]{2,1,0:T(8,128)S(1)}, f32[2,128,128]{2,1,0:T(8,128)S(1)}) custom-call(f32[33,2]{1,0:T(8,128)S(1)} %copy.11.taps_ref, bf16[2,128,128]{2,1,0:T(8,128)(2,1)S(1)} %copy-done.10, f32[2,128,128]{2,1,0:T(8,128)S(1)} %get-tuple-element.80.cg_ref, bf16[2,48,128]{2,1,0:T(8,128)(2,1)S(1)} %collective-permute-done.7.above_ref, ...), custom_call_target="tpu_custom_call" | custom-call | flops 1000000000 | bytes 2000000 | tf_op jit(solution)/shard_map/pallas_call | solution.py:475
  88.2 0.0 copy-start.12
  88.2 0.6 copy-done.12
  88.8 9.6 %all-to-all-done.2 = f32[64,8,128]{2,1,0:T(8,128)S(1)} async-done(((f32[64,8,128]{2,1,0:T(8,128)}), f32[64,8,128]{2,1,0:T(8,128)S(1)}, u32[]{:S(2)}, u32[]{:S(2)}) %all-to-all-start.2) | async-done | bytes 262176 | tf_op jit(solution)/shard_map/all_to_all | solution.py:491
  98.4 0.7 copy-done.22
  99.1 3.2 %shard_map.109 = (bf16[256,128]{1,0:T(8,128)(2,1)}, f32[2,128,128]{2,1,0:T(8,128)}, f32[2,128,128]{2,1,0:T(8,128)}, f32[2,256,128]{2,1,0:T(8,128)}) custom-call(f32[512,128]{1,0:T(8,128)} %bitcast.12, f32[2,128,256]{2,1,0:T(8,128)} %copy-done.3, f32[4,128,128]{2,1,0:T(8,128)} %copy-done.6, f32[2,128,128]{2,1,0:T(8,128)} %copy-done.12), custom_call_target="tpu_custom_call" | custom-call | flops 100000000 | bytes 2000000 | tf_op jit(solution)/shard_map/pallas_call | solution.py:475
  102.4 1.9 %collective-permute-start.10 = (bf16[256,128]{1,0:T(8,128)(2,1)}, bf16[256,128]{1,0:T(8,128)(2,1)S(1)}, u32[]{:S(2)}, u32[]{:S(2)}) collective-permute-start(bf16[256,128]{1,0:T(8,128)(2,1)} %get-tuple-element.96.ctx_ref.refs_0_), channel_id=1, source_target_pairs={{0,7},{1,0},{2,1},{3,2},{4,3},{5,4},{6,5},{7,6},{8,9},{9,10},{10,1... | collective-permute-start | bytes 196616 | tf_op jit(solution)/shard_map/ppermute | solution.py:499
  104.3 4.6 %collective-permute-start.9 = (bf16[256,128]{1,0:T(8,128)(2,1)}, bf16[256,128]{1,0:T(8,128)(2,1)S(1)}, u32[]{:S(2)}, u32[]{:S(2)}) collective-permute-start(bf16[256,128]{1,0:T(8,128)(2,1)} %get-tuple-element.96.ctx_ref.refs_0_), channel_id=1, source_target_pairs={{0,1},{1,2},{2,3},{3,4},{4,5},{5,6},{6,7},{7,0},{8,15},{9,8},{10,9... | collective-permute-start | bytes 196616 | tf_op jit(solution)/shard_map/ppermute | solution.py:499
  108.9 4.6 %shard_map.110 = bf16[64,48,128]{2,1,0:T(8,128)(2,1)} custom-call(f32[8,128]{1,0:T(8,128)} %copy-done.20, f32[2,128,256]{2,1,0:T(8,128)} %copy-done.3, f32[2,128,256]{2,1,0:T(8,128)} %copy-done.14, f32[2,128,128]{2,1,0:T(8,128)} %copy-done.16, f32[4,128,128]{2,1,0:T(8,128)} %copy-done.6, bf16[2,128,128]{2,1,0:T(8,128)(2,1)} %q_ref.5, ...), custom_call_target="tpu_custom_call" | custom-call | flops 1000000000 | bytes 2000000 | tf_op jit(solution)/shard_map/pallas_call | solution.py:475
  113.5 0.0 copy-start.5
  113.5 0.0 collective-permute-done.10.refs_2_
  113.5 0.0 collective-permute-done.9.refs_1_
  113.6 4.4 %all-to-all-start.3 = ((bf16[64,48,128]{2,1,0:T(8,128)(2,1)}), bf16[64,48,128]{2,1,0:T(8,128)(2,1)S(1)}, u32[]{:S(2)}, u32[]{:S(2)}) async-start(bf16[64,48,128]{2,1,0:T(8,128)(2,1)} %shard_map.110), calls=%async_computation.3 | async-start | bytes 1572864 | tf_op jit(solution)/shard_map/all_to_all | solution.py:491
  118.0 5.6 %collective-permute-start.12 = (bf16[512,128]{1,0:T(8,128)(2,1)S(1)}, bf16[512,128]{1,0:T(8,128)(2,1)S(1)}, u32[]{:S(2)}, u32[]{:S(2)}) collective-permute-start(bf16[512,128]{1,0:T(8,128)(2,1)S(1)} %pad_maximum_fusion.1), channel_id=1, source_target_pairs={{0,5},{1,6},{2,7},{3,0},{4,1},{5,2},{6,3},{7,4},{8,11},{9,12},{10,... | collective-permute-start | bytes 393224 | tf_op jit(solution)/shard_map/ppermute | solution.py:499
  123.7 0.0 copy-start.11
  123.7 0.0 copy-start.21
  123.7 3.1 %collective-permute-start.11 = (bf16[768,128]{1,0:T(8,128)(2,1)S(1)}, bf16[768,128]{1,0:T(8,128)(2,1)S(1)}, u32[]{:S(2)}, u32[]{:S(2)}) collective-permute-start(bf16[768,128]{1,0:T(8,128)(2,1)S(1)} %pad_maximum_fusion), channel_id=1, source_target_pairs={{0,3},{1,4},{2,5},{3,6},{4,7},{5,0},{6,1},{7,2},{8,13},{9,14},{10,... | collective-permute-start | bytes 589832 | tf_op jit(solution)/shard_map/ppermute | solution.py:499
  126.9 4.9 %shard_map.112.own_ref = f32[8,128]{1,0:T(8,128)S(1)} custom-call(f32[2,128,128]{2,1,0:T(8,128)S(1)} %get-tuple-element.75.qm_ref, f32[2,128,128]{2,1,0:T(8,128)S(1)} %get-tuple-element.76.km_ref, f32[2,128,128]{2,1,0:T(8,128)S(1)} %copy-done.18, f32[2,128,128]{2,1,0:T(8,128)S(1)} %copy-done.19), custom_call_target="tpu_custom_call" | custom-call | flops 5000000000 | bytes 2000000 | tf_op jit(solution)/shard_map/pallas_call | solution.py:475
  131.8 0.0 copy-start.13
  131.8 3.1 %shard_map.113 = (f32[2,128,128]{2,1,0:T(8,128)S(1)}, f32[2,128,128]{2,1,0:T(8,128)S(1)}, bf16[2,128,128]{2,1,0:T(8,128)(2,1)}) custom-call(f32[8,128]{1,0:T(8,128)S(1)} %copy-done.21, f32[2,128,256]{2,1,0:T(8,128)S(1)} %copy-done.4, f32[2,128,256]{2,1,0:T(8,128)S(1)} %copy-done.15, f32[2,128,128]{2,1,0:T(8,128)S(1)} %copy-done.17, ...), custom_call_target="tpu_custom_call" | custom-call | flops 1000000000 | bytes 2000000 | tf_op jit(solution)/shard_map/pallas_call | solution.py:475
  134.9 0.0 collective-permute-done.12.refs_4_
  134.9 0.3 collective-permute-done.11.refs_3_
  135.2 1.1 shard_map.111
  136.3 4.4 %all-to-all-done.3.got_ref = bf16[64,48,128]{2,1,0:T(8,128)(2,1)S(1)} async-done(((bf16[64,48,128]{2,1,0:T(8,128)(2,1)}), bf16[64,48,128]{2,1,0:T(8,128)(2,1)S(1)}, u32[]{:S(2)}, u32[]{:S(2)}) %all-to-all-start.3) | async-done | bytes 786464 | tf_op jit(solution)/shard_map/all_to_all | solution.py:491
  140.7 0.8 shard_map.114
  (37 shorter events, 0.1 us)
Async XLA Ops:
  4.4 31.5 %collective-permute-start.1 = (bf16[640,256]{1,0:T(8,128)(2,1)}, bf16[640,256]{1,0:T(8,128)(2,1)S(1)}, u32[]{:S(2)}, u32[]{:S(2)}) collective-permute-start(bf16[640,256]{1,0:T(8,128)(2,1)} %get-tuple-element.62), channel_id=1, source_target_pairs={{0,2},{1,3},{2,4},{3,5},{4,6},{5,7},{6,0},{7,1},{8,14},{9,15},{10,... | collective-permute-start | bytes 983048 | tf_op jit(solution)/shard_map/ppermute | solution.py:499
  11.1 22.0 %collective-permute-start.4 = (bf16[512,256]{1,0:T(8,128)(2,1)}, bf16[512,256]{1,0:T(8,128)(2,1)S(1)}, u32[]{:S(2)}, u32[]{:S(2)}) collective-permute-start(bf16[512,256]{1,0:T(8,128)(2,1)} %get-tuple-element.63), channel_id=1, source_target_pairs={{0,6},{1,7},{2,0},{3,1},{4,2},{5,3},{6,4},{7,5},{8,10},{9,11},{10,... | collective-permute-start | bytes 786440 | tf_op jit(solution)/shard_map/ppermute | solution.py:499
  13.0 30.5 %all-to-all-start = ((f32[64,8,128]{2,1,0:T(8,128)}), f32[64,8,128]{2,1,0:T(8,128)S(1)}, u32[]{:S(2)}, u32[]{:S(2)}) async-start(f32[64,8,128]{2,1,0:T(8,128)} %shard_map.101), calls=%async_computation | async-start | bytes 524288 | tf_op jit(solution)/shard_map/all_to_all | solution.py:491
  27.4 17.4 %collective-permute-start = (bf16[384,256]{1,0:T(8,128)(2,1)}, bf16[384,256]{1,0:T(8,128)(2,1)S(1)}, u32[]{:S(2)}, u32[]{:S(2)}) collective-permute-start(bf16[384,256]{1,0:T(8,128)(2,1)} %get-tuple-element.61), channel_id=1, source_target_pairs={{0,1},{1,2},{2,3},{3,4},{4,5},{5,6},{6,7},{7,0},{8,15},{9,8},{10,9... | collective-permute-start | bytes 589832 | tf_op jit(solution)/shard_map/ppermute | solution.py:499
  31.2 13.6 %collective-permute-start.6 = (bf16[384,256]{1,0:T(8,128)(2,1)}, bf16[384,256]{1,0:T(8,128)(2,1)S(1)}, u32[]{:S(2)}, u32[]{:S(2)}) collective-permute-start(bf16[384,256]{1,0:T(8,128)(2,1)} %get-tuple-element.64), channel_id=1, source_target_pairs={{0,7},{1,0},{2,1},{3,2},{4,3},{5,4},{6,5},{7,6},{8,9},{9,10},{10,1... | collective-permute-start | bytes 589832 | tf_op jit(solution)/shard_map/ppermute | solution.py:499
  33.2 10.4 %copy-start.8 = (bf16[2,128,128]{2,1,0:T(8,128)(2,1)S(1)}, bf16[2,128,128]{2,1,0:T(8,128)(2,1)}, u32[]{:S(2)}) copy-start(bf16[2,128,128]{2,1,0:T(8,128)(2,1)} %q_ref.5) | copy-start | bytes 196612
  33.2 10.4 %copy-start.9 = (bf16[2,128,128]{2,1,0:T(8,128)(2,1)S(1)}, bf16[2,128,128]{2,1,0:T(8,128)(2,1)}, u32[]{:S(2)}) copy-start(bf16[2,128,128]{2,1,0:T(8,128)(2,1)} %k_ref.5) | copy-start | bytes 196612
  33.2 10.4 %copy-start.10 = (bf16[2,128,128]{2,1,0:T(8,128)(2,1)S(1)}, bf16[2,128,128]{2,1,0:T(8,128)(2,1)}, u32[]{:S(2)}) copy-start(bf16[2,128,128]{2,1,0:T(8,128)(2,1)} %v_ref.7) | copy-start | bytes 196612
  33.2 15.2 %copy-start = (bf16[128,2048]{1,0:T(8,128)(2,1)S(1)}, bf16[128,2048]{1,0:T(8,128)(2,1)}, u32[]{:S(2)}) copy-start(bf16[128,2048]{1,0:T(8,128)(2,1)} %refs_8_.1) | copy-start | bytes 1572868
  33.2 11.6 %collective-permute-start.5 = (bf16[384,256]{1,0:T(8,128)(2,1)S(1)}, bf16[384,256]{1,0:T(8,128)(2,1)S(1)}, u32[]{:S(2)}, u32[]{:S(2)}) collective-permute-start(bf16[384,256]{1,0:T(8,128)(2,1)S(1)} %slice.14), channel_id=1, source_target_pairs={{0,7},{1,0},{2,1},{3,2},{4,3},{5,4},{6,5},{7,6},{8,9},{9,10},{10,1... | collective-permute-start | bytes 589832 | tf_op jit(solution)/shard_map/ppermute | solution.py:499
  36.0 10.8 %collective-permute-start.3 = (bf16[384,256]{1,0:T(8,128)(2,1)S(1)}, bf16[384,256]{1,0:T(8,128)(2,1)S(1)}, u32[]{:S(2)}, u32[]{:S(2)}) collective-permute-start(bf16[384,256]{1,0:T(8,128)(2,1)S(1)} %get-tuple-element.115), channel_id=1, source_target_pairs={{0,2},{1,3},{2,4},{3,5},{4,6},{5,7},{6,0},{7,1},{8,14},{9,15},{10,... | collective-permute-start | bytes 589832 | tf_op jit(solution)/shard_map/ppermute | solution.py:499
  41.1 7.3 %collective-permute-start.2 = (bf16[384,256]{1,0:T(8,128)(2,1)S(1)}, bf16[384,256]{1,0:T(8,128)(2,1)S(1)}, u32[]{:S(2)}, u32[]{:S(2)}) collective-permute-start(bf16[384,256]{1,0:T(8,128)(2,1)S(1)} %get-tuple-element.116), channel_id=1, source_target_pairs={{0,1},{1,2},{2,3},{3,4},{4,5},{5,6},{6,7},{7,0},{8,15},{9,8},{10,9... | collective-permute-start | bytes 589832 | tf_op jit(solution)/shard_map/ppermute | solution.py:499
  43.6 4.8 %copy-start.1 = (bf16[2,128,256]{2,1,0:T(8,128)(2,1)S(1)}, bf16[2,128,256]{2,1,0:T(8,128)(2,1)}, u32[]{:S(2)}) copy-start(bf16[2,128,256]{2,1,0:T(8,128)(2,1)} %param.11) | copy-start | bytes 393220
  44.7 5.2 %copy-start.3 = (f32[2,128,256]{2,1,0:T(8,128)}, f32[2,128,256]{2,1,0:T(8,128)S(1)}, u32[]{:S(2)}) copy-start(f32[2,128,256]{2,1,0:T(8,128)S(1)} %get-tuple-element.66.refs_10_.t_ref) | copy-start | bytes 786436
  44.8 5.2 %copy-start.14 = (f32[2,128,256]{2,1,0:T(8,128)}, f32[2,128,256]{2,1,0:T(8,128)S(1)}, u32[]{:S(2)}) copy-start(f32[2,128,256]{2,1,0:T(8,128)S(1)} %get-tuple-element.98.s_ref) | copy-start | bytes 786436
  50.0 36.8 %copy-start.16 = (f32[2,128,128]{2,1,0:T(8,128)}, f32[2,128,128]{2,1,0:T(8,128)S(1)}, u32[]{:S(2)}) copy-start(f32[2,128,128]{2,1,0:T(8,128)S(1)} %get-tuple-element.80.cg_ref) | copy-start | bytes 393220
  50.0 28.1 %all-to-all-start.1 = ((f32[64,3,4,128]{3,2,1,0:T(4,128)}), f32[64,3,4,128]{3,2,1,0:T(4,128)S(1)}, u32[]{:S(2)}, u32[]{:S(2)}) async-start(f32[64,3,4,128]{3,2,1,0:T(4,128)} %bitcast.2), calls=%async_computation.1 | async-start | bytes 786432 | tf_op jit(solution)/shard_map/all_to_all | solution.py:491
  62.9 8.3 %collective-permute-start.7 = (bf16[2,48,128]{2,1,0:T(8,128)(2,1)S(1)}, bf16[2,48,128]{2,1,0:T(8,128)(2,1)S(1)}, u32[]{:S(2)}, u32[]{:S(2)}) collective-permute-start(bf16[2,48,128]{2,1,0:T(8,128)(2,1)S(1)} %get-tuple-element.73), channel_id=1, source_target_pairs={{0,8},{8,16},{16,24},{24,32},{32,40},{40,48},{48,56},{56,64},{64,7... | collective-permute-start | bytes 73736 | tf_op jit(solution)/shard_map/ppermute | solution.py:563
  66.5 5.7 %collective-permute-start.8 = (bf16[2,48,128]{2,1,0:T(8,128)(2,1)S(1)}, bf16[2,48,128]{2,1,0:T(8,128)(2,1)S(1)}, u32[]{:S(2)}, u32[]{:S(2)}) collective-permute-start(bf16[2,48,128]{2,1,0:T(8,128)(2,1)S(1)} %get-tuple-element.74), channel_id=1, source_target_pairs={{8,0},{16,8},{24,16},{32,24},{40,32},{48,40},{56,48},{64,56},{72,6... | collective-permute-start | bytes 73736 | tf_op jit(solution)/shard_map/ppermute | solution.py:564
  70.6 0.7 copy-start.6
  78.9 0.6 copy-start.20
  78.9 6.4 %copy-start.23 = (f32[33,2]{0,1:T(2,128)S(1)}, f32[33,2]{0,1:T(2,128)}, u32[]{:S(2)}) copy-start(f32[33,2]{0,1:T(2,128)} %param.9) | copy-start | bytes 796
  79.5 18.9 %all-to-all-start.2 = ((f32[64,8,128]{2,1,0:T(8,128)}), f32[64,8,128]{2,1,0:T(8,128)S(1)}, u32[]{:S(2)}, u32[]{:S(2)}) async-start(f32[64,8,128]{2,1,0:T(8,128)} %get-tuple-element.79), calls=%async_computation.2 | async-start | bytes 524288 | tf_op jit(solution)/shard_map/all_to_all | solution.py:491
  85.7 1.0 copy-start.2
  88.2 0.7 copy-start.12
  98.4 0.7 copy-start.22
  102.4 11.2 %collective-permute-start.10 = (bf16[256,128]{1,0:T(8,128)(2,1)}, bf16[256,128]{1,0:T(8,128)(2,1)S(1)}, u32[]{:S(2)}, u32[]{:S(2)}) collective-permute-start(bf16[256,128]{1,0:T(8,128)(2,1)} %get-tuple-element.96.ctx_ref.refs_0_), channel_id=1, source_target_pairs={{0,7},{1,0},{2,1},{3,2},{4,3},{5,4},{6,5},{7,6},{8,9},{9,10},{10,1... | collective-permute-start | bytes 196616 | tf_op jit(solution)/shard_map/ppermute | solution.py:499
  104.3 9.3 %collective-permute-start.9 = (bf16[256,128]{1,0:T(8,128)(2,1)}, bf16[256,128]{1,0:T(8,128)(2,1)S(1)}, u32[]{:S(2)}, u32[]{:S(2)}) collective-permute-start(bf16[256,128]{1,0:T(8,128)(2,1)} %get-tuple-element.96.ctx_ref.refs_0_), channel_id=1, source_target_pairs={{0,1},{1,2},{2,3},{3,4},{4,5},{5,6},{6,7},{7,0},{8,15},{9,8},{10,9... | collective-permute-start | bytes 196616 | tf_op jit(solution)/shard_map/ppermute | solution.py:499
  113.5 4.4 %copy-start.5 = (bf16[256,128]{1,0:T(8,128)(2,1)S(1)}, bf16[256,128]{1,0:T(8,128)(2,1)}, u32[]{:S(2)}) copy-start(bf16[256,128]{1,0:T(8,128)(2,1)} %get-tuple-element.96.ctx_ref.refs_0_) | copy-start | bytes 196612
  113.6 27.2 %all-to-all-start.3 = ((bf16[64,48,128]{2,1,0:T(8,128)(2,1)}), bf16[64,48,128]{2,1,0:T(8,128)(2,1)S(1)}, u32[]{:S(2)}, u32[]{:S(2)}) async-start(bf16[64,48,128]{2,1,0:T(8,128)(2,1)} %shard_map.110), calls=%async_computation.3 | async-start | bytes 1572864 | tf_op jit(solution)/shard_map/all_to_all | solution.py:491
  118.0 8.9 %copy-start.18 = (f32[2,128,128]{2,1,0:T(8,128)S(1)}, f32[2,128,128]{2,1,0:T(8,128)}, u32[]{:S(2)}) copy-start(f32[2,128,128]{2,1,0:T(8,128)} %get-tuple-element.100.mixed_ref) | copy-start | bytes 393220
  118.0 8.9 %copy-start.19 = (f32[2,128,128]{2,1,0:T(8,128)S(1)}, f32[2,128,128]{2,1,0:T(8,128)}, u32[]{:S(2)}) copy-start(f32[2,128,128]{2,1,0:T(8,128)} %get-tuple-element.107.mix_ref) | copy-start | bytes 393220
  118.0 16.9 %collective-permute-start.12 = (bf16[512,128]{1,0:T(8,128)(2,1)S(1)}, bf16[512,128]{1,0:T(8,128)(2,1)S(1)}, u32[]{:S(2)}, u32[]{:S(2)}) collective-permute-start(bf16[512,128]{1,0:T(8,128)(2,1)S(1)} %pad_maximum_fusion.1), channel_id=1, source_target_pairs={{0,5},{1,6},{2,7},{3,0},{4,1},{5,2},{6,3},{7,4},{8,11},{9,12},{10,... | collective-permute-start | bytes 393224 | tf_op jit(solution)/shard_map/ppermute | solution.py:499
  123.7 8.1 %copy-start.4 = (f32[2,128,256]{2,1,0:T(8,128)S(1)}, f32[2,128,256]{2,1,0:T(8,128)}, u32[]{:S(2)}) copy-start(f32[2,128,256]{2,1,0:T(8,128)} %copy-done.3) | copy-start | bytes 786436
  123.7 8.1 %copy-start.7 = (f32[4,128,128]{2,1,0:T(8,128)S(1)}, f32[4,128,128]{2,1,0:T(8,128)}, u32[]{:S(2)}) copy-start(f32[4,128,128]{2,1,0:T(8,128)} %copy-done.6) | copy-start | bytes 786436
  123.7 8.1 %copy-start.11 = (bf16[2,128,128]{2,1,0:T(8,128)(2,1)S(1)}, bf16[2,128,128]{2,1,0:T(8,128)(2,1)}, u32[]{:S(2)}) copy-start(bf16[2,128,128]{2,1,0:T(8,128)(2,1)} %v_ref.7) | copy-start | bytes 196612
  123.7 8.1 %copy-start.15 = (f32[2,128,256]{2,1,0:T(8,128)S(1)}, f32[2,128,256]{2,1,0:T(8,128)}, u32[]{:S(2)}) copy-start(f32[2,128,256]{2,1,0:T(8,128)} %copy-done.14) | copy-start | bytes 786436
  123.7 8.1 %copy-start.17 = (f32[2,128,128]{2,1,0:T(8,128)S(1)}, f32[2,128,128]{2,1,0:T(8,128)}, u32[]{:S(2)}) copy-start(f32[2,128,128]{2,1,0:T(8,128)} %copy-done.16) | copy-start | bytes 393220
  123.7 8.1 %copy-start.21 = (f32[8,128]{1,0:T(8,128)S(1)}, f32[8,128]{1,0:T(8,128)}, u32[]{:S(2)}) copy-start(f32[8,128]{1,0:T(8,128)} %copy-done.20) | copy-start | bytes 12292
  123.7 11.5 %collective-permute-start.11 = (bf16[768,128]{1,0:T(8,128)(2,1)S(1)}, bf16[768,128]{1,0:T(8,128)(2,1)S(1)}, u32[]{:S(2)}, u32[]{:S(2)}) collective-permute-start(bf16[768,128]{1,0:T(8,128)(2,1)S(1)} %pad_maximum_fusion), channel_id=1, source_target_pairs={{0,3},{1,4},{2,5},{3,6},{4,7},{5,0},{6,1},{7,2},{8,13},{9,14},{10,... | collective-permute-start | bytes 589832 | tf_op jit(solution)/shard_map/ppermute | solution.py:499
  131.8 3.4 %copy-start.13 = (bf16[128,256]{1,0:T(8,128)(2,1)S(1)}, bf16[128,256]{1,0:T(8,128)(2,1)}, u32[]{:S(2)}) copy-start(bf16[128,256]{1,0:T(8,128)(2,1)} %get-tuple-element.105.refs_5_) | copy-start | bytes 196612

commit v6 on v5

--- a/solution.py
+++ b/solution.py
@@ -599,7 +599,6 @@
             pltpu.SemaphoreType.DMA((2,)),
         ],
         far=(2, 3),
-        grant=60,
     )
     near = [shift_by(context_b, 1, parts), shift_by(context_b, parts - 1, parts)]
     sent_shape = (groups, 16 + column_rows, channels)
@@ -614,7 +613,6 @@
             pltpu.SemaphoreType.DMA((2,)),
         ],
         far_out=True,
-        grant=60,
         flops=1e9,
     )
     sent, near, mix = lax.optimization_barrier((sent, near, mix))

time: 142 us -> 141 us (level)
  Pallas kernels: 29 us -> 24.8 us
  local copies, waits for them, and re-layouts: 3.85 us -> 6.07 us
    pallas_call x14, Pallas kernels: 29 us -> 24.8 us  [call(): pl.pallas_call(kernel, out_shape=[jax.ShapeDtypeStruct(shape, kind) for s...]
    unnamed x49 -> x69, local copies, waits for them, and re-layouts: 3.81 us -> 5.35 us
  transfers between devices with their start and end apart: 17 -> 17, of which waited for: 7 -> 7; matrix products, arithmetic and copies ran while one was open for 0% -> 1% of each run, Pallas kernels for 13% -> 12%
where the time goes in v6:
time: 141 us; the launch traced here: 140 us
  starting transfers between devices  83.3 us (59%)
  Pallas kernels  24.8 us (18%)
  waiting for transfers between devices  24.6 us (17%)
  local copies, waits for them, and re-layouts  6.07 us (4%)
    ppermute x11, starting transfers between devices, shift_by(): return lax.ppermute(block, ('seq', 'head'), pairs)  39.9 us
    all_to_all x4, starting transfers between devices, exchange(): return lax.all_to_all(blocks, axis, 0, 0, tiled=True)  37.9 us
    pallas_call x14, Pallas kernels, call(): pl.pallas_call(kernel, out_shape=[jax.ShapeDtypeStruct(shape, kind) for s...  24.8 us
    all_to_all x4, waiting for transfers between devices, exchange(): return lax.all_to_all(blocks, axis, 0, 0, tiled=True)  20 us
    unnamed x69, local copies, waits for them, and re-layouts  5.35 us
    ppermute x11, waiting for transfers between devices, shift_by(): return lax.ppermute(block, ('seq', 'head'), pairs)  3.64 us
    ppermute x1, starting transfers between devices, shards(): above = lax.ppermute(last_rows, 'seq', [(i, i + 1) for i in range(ends)])  3.54 us
  transfers between devices with their start and end apart: 17, of which 7 were waited for; matrix products, arithmetic and copies ran while one was open for 1% of the time, Pallas kernels for 12%

profile of v6, /device:TPU:1, one launch (start us, length us, event | category | flops | bytes accessed | tf_op | source)
XLA Modules:
  0.0 140.0 jit_solution(5302094681904277110)
XLA Ops:
  0.6 1.6 %shard_map.101 = f32[64,8,128]{2,1,0:T(8,128)} custom-call(bf16[2,128,128]{2,1,0:T(8,128)(2,1)} %q_ref.5, bf16[2,128,128]{2,1,0:T(8,128)(2,1)} %k_ref.5), custom_call_target="tpu_custom_call" | custom-call | flops 100000000 | bytes 2000000 | tf_op jit(solution)/shard_map/pallas_call | solution.py:475
  2.3 2.2 %shard_map.102 = (bf16[384,256]{1,0:T(8,128)(2,1)}, bf16[384,256]{1,0:T(8,128)(2,1)}, bf16[640,256]{1,0:T(8,128)(2,1)}, bf16[512,256]{1,0:T(8,128)(2,1)}, bf16[128,256]{1,0:T(8,128)(2,1)}) custom-call(bf16[256,256]{1,0:T(8,128)(2,1)} %bitcast.8, bf16[128,2048]{1,0:T(8,128)(2,1)} %refs_8_.1), custom_call_target="tpu_custom_call" | custom-call | flops 100000000 | bytes 2000000 | tf_op jit(solution)/shard_map/pallas_call | solution.py:475
  4.5 6.7 %collective-permute-start.1 = (bf16[640,256]{1,0:T(8,128)(2,1)}, bf16[640,256]{1,0:T(8,128)(2,1)S(1)}, u32[]{:S(2)}, u32[]{:S(2)}) collective-permute-start(bf16[640,256]{1,0:T(8,128)(2,1)} %get-tuple-element.62), channel_id=1, source_target_pairs={{0,2},{1,3},{2,4},{3,5},{4,6},{5,7},{6,0},{7,1},{8,14},{9,15},{10,... | collective-permute-start | bytes 983048 | tf_op jit(solution)/shard_map/ppermute | solution.py:499
  11.2 1.9 %collective-permute-start.4 = (bf16[512,256]{1,0:T(8,128)(2,1)}, bf16[512,256]{1,0:T(8,128)(2,1)S(1)}, u32[]{:S(2)}, u32[]{:S(2)}) collective-permute-start(bf16[512,256]{1,0:T(8,128)(2,1)} %get-tuple-element.63), channel_id=1, source_target_pairs={{0,6},{1,7},{2,0},{3,1},{4,2},{5,3},{6,4},{7,5},{8,10},{9,11},{10,... | collective-permute-start | bytes 786440 | tf_op jit(solution)/shard_map/ppermute | solution.py:499
  13.1 14.3 %all-to-all-start = ((f32[64,8,128]{2,1,0:T(8,128)}), f32[64,8,128]{2,1,0:T(8,128)S(1)}, u32[]{:S(2)}, u32[]{:S(2)}) async-start(f32[64,8,128]{2,1,0:T(8,128)} %shard_map.101), calls=%async_computation | async-start | bytes 524288 | tf_op jit(solution)/shard_map/all_to_all | solution.py:491
  27.4 3.8 %collective-permute-start = (bf16[384,256]{1,0:T(8,128)(2,1)}, bf16[384,256]{1,0:T(8,128)(2,1)S(1)}, u32[]{:S(2)}, u32[]{:S(2)}) collective-permute-start(bf16[384,256]{1,0:T(8,128)(2,1)} %get-tuple-element.61), channel_id=1, source_target_pairs={{0,1},{1,2},{2,3},{3,4},{4,5},{5,6},{6,7},{7,0},{8,15},{9,8},{10,9... | collective-permute-start | bytes 589832 | tf_op jit(solution)/shard_map/ppermute | solution.py:499
  31.3 1.9 %collective-permute-start.6 = (bf16[384,256]{1,0:T(8,128)(2,1)}, bf16[384,256]{1,0:T(8,128)(2,1)S(1)}, u32[]{:S(2)}, u32[]{:S(2)}) collective-permute-start(bf16[384,256]{1,0:T(8,128)(2,1)} %get-tuple-element.64), channel_id=1, source_target_pairs={{0,7},{1,0},{2,1},{3,2},{4,3},{5,4},{6,5},{7,6},{8,9},{9,10},{10,1... | collective-permute-start | bytes 589832 | tf_op jit(solution)/shard_map/ppermute | solution.py:499
  33.2 0.0 collective-permute-done.4.refs_6_.refs_11_
  33.2 0.0 copy-start.10
  33.2 0.0 copy-start.11
  33.2 0.0 copy-start.12
  33.2 0.0 copy-start
  33.3 2.7 %collective-permute-start.5 = (bf16[384,256]{1,0:T(8,128)(2,1)S(1)}, bf16[384,256]{1,0:T(8,128)(2,1)S(1)}, u32[]{:S(2)}, u32[]{:S(2)}) collective-permute-start(bf16[384,256]{1,0:T(8,128)(2,1)S(1)} %slice.14), channel_id=1, source_target_pairs={{0,7},{1,0},{2,1},{3,2},{4,3},{5,4},{6,5},{7,6},{8,9},{9,10},{10,1... | collective-permute-start | bytes 589832 | tf_op jit(solution)/shard_map/ppermute | solution.py:499
  36.0 0.0 collective-permute-done.1.refs_2_.refs_7_
  36.0 0.7 fusion
  36.7 5.1 %collective-permute-start.3 = (bf16[384,256]{1,0:T(8,128)(2,1)}, bf16[384,256]{1,0:T(8,128)(2,1)S(1)}, u32[]{:S(2)}, u32[]{:S(2)}) collective-permute-start(bf16[384,256]{1,0:T(8,128)(2,1)} %get-tuple-element.115), channel_id=1, source_target_pairs={{0,2},{1,3},{2,4},{3,5},{4,6},{5,7},{6,0},{7,1},{8,14},{9,15},{10,... | collective-permute-start | bytes 589832 | tf_op jit(solution)/shard_map/ppermute | solution.py:499
  41.8 2.5 %collective-permute-start.2 = (bf16[384,256]{1,0:T(8,128)(2,1)S(1)}, bf16[384,256]{1,0:T(8,128)(2,1)S(1)}, u32[]{:S(2)}, u32[]{:S(2)}) collective-permute-start(bf16[384,256]{1,0:T(8,128)(2,1)S(1)} %get-tuple-element.116), channel_id=1, source_target_pairs={{0,1},{1,2},{2,3},{3,4},{4,5},{5,6},{6,7},{7,0},{8,15},{9,8},{10,9... | collective-permute-start | bytes 589832 | tf_op jit(solution)/shard_map/ppermute | solution.py:499
  44.3 0.0 all-to-all-done
  44.3 0.0 copy-start.1
  44.3 1.1 shard_map.103
  45.5 0.7 copy-done.14
  46.2 0.0 collective-permute-done.refs_1_.refs_6_
  46.2 0.0 collective-permute-done.6.refs_7_.refs_12_
  46.2 0.0 collective-permute-done.5.refs_5_.refs_10_
  46.2 1.5 %collective-permute-done.3.refs_4_.refs_9_ = bf16[384,256]{1,0:T(8,128)(2,1)S(1)} collective-permute-done((bf16[384,256]{1,0:T(8,128)(2,1)}, bf16[384,256]{1,0:T(8,128)(2,1)S(1)}, u32[]{:S(2)}, u32[]{:S(2)}) %collective-permute-start.3) | collective-permute-done | bytes 196640 | tf_op jit(solution)/shard_map/ppermute | solution.py:499
  47.7 1.6 %collective-permute-done.2.refs_3_.refs_8_ = bf16[384,256]{1,0:T(8,128)(2,1)S(1)} collective-permute-done((bf16[384,256]{1,0:T(8,128)(2,1)S(1)}, bf16[384,256]{1,0:T(8,128)(2,1)S(1)}, u32[]{:S(2)}, u32[]{:S(2)}) %collective-permute-start.2) | collective-permute-done | bytes 196640 | tf_op jit(solution)/shard_map/ppermute | solution.py:499
  49.3 1.6 %shard_map.104 = (f32[768,128]{1,0:T(8,128)}, f32[2,128,128]{2,1,0:T(8,128)S(1)}, bf16[2,48,128]{2,1,0:T(8,128)(2,1)S(1)}, bf16[2,48,128]{2,1,0:T(8,128)(2,1)S(1)}) custom-call(bf16[256,256]{1,0:T(8,128)(2,1)S(1)} %bitcast.9, bf16[384,256]{1,0:T(8,128)(2,1)S(1)} %collective-permute-done.refs_1_.refs_6_, ...), custom_call_target="tpu_custom_call" | custom-call | flops 100000000 | bytes 2000000 | tf_op jit(solution)/shard_map/pallas_call | solution.py:475
  50.9 0.7 copy-done.21
  51.5 13.0 %all-to-all-start.1 = ((f32[64,3,4,128]{3,2,1,0:T(4,128)}), f32[64,3,4,128]{3,2,1,0:T(4,128)S(1)}, u32[]{:S(2)}, u32[]{:S(2)}) async-start(f32[64,3,4,128]{3,2,1,0:T(4,128)} %bitcast.2), calls=%async_computation.1 | async-start | bytes 786432 | tf_op jit(solution)/shard_map/all_to_all | solution.py:491
  64.5 3.5 %collective-permute-start.7 = (bf16[2,48,128]{2,1,0:T(8,128)(2,1)S(1)}, bf16[2,48,128]{2,1,0:T(8,128)(2,1)S(1)}, u32[]{:S(2)}, u32[]{:S(2)}) collective-permute-start(bf16[2,48,128]{2,1,0:T(8,128)(2,1)S(1)} %get-tuple-element.73), channel_id=1, source_target_pairs={{0,8},{8,16},{16,24},{24,32},{32,40},{40,48},{48,56},{56,64},{64,7... | collective-permute-start | bytes 73736 | tf_op jit(solution)/shard_map/ppermute | solution.py:563
  68.0 1.9 %collective-permute-start.8 = (bf16[2,48,128]{2,1,0:T(8,128)(2,1)S(1)}, bf16[2,48,128]{2,1,0:T(8,128)(2,1)S(1)}, u32[]{:S(2)}, u32[]{:S(2)}) collective-permute-start(bf16[2,48,128]{2,1,0:T(8,128)(2,1)S(1)} %get-tuple-element.74), channel_id=1, source_target_pairs={{8,0},{16,8},{24,16},{32,24},{40,32},{48,40},{56,48},{64,56},{72,6... | collective-permute-start | bytes 73736 | tf_op jit(solution)/shard_map/ppermute | solution.py:564
  70.0 2.2 %shard_map.105.inv_far.inv_ref = f32[4,128,128]{2,1,0:T(8,128)S(1)} custom-call(f32[2,128,128]{2,1,0:T(8,128)S(1)} %get-tuple-element.75.qm_ref, f32[2,128,128]{2,1,0:T(8,128)S(1)} %get-tuple-element.76.km_ref), custom_call_target="tpu_custom_call" | custom-call | flops 2000000000 | bytes 2000000 | tf_op jit(solution)/shard_map/pallas_call | solution.py:475
  72.2 0.7 copy-done.6
  72.8 0.0 collective-permute-done.7.above_ref
  72.9 0.9 collective-permute-done.8.below_ref
  73.8 5.8 %all-to-all-done.1 = f32[64,3,4,128]{3,2,1,0:T(4,128)S(1)} async-done(((f32[64,3,4,128]{3,2,1,0:T(4,128)}), f32[64,3,4,128]{3,2,1,0:T(4,128)S(1)}, u32[]{:S(2)}, u32[]{:S(2)}) %all-to-all-start.1) | async-done | bytes 393248 | tf_op jit(solution)/shard_map/all_to_all | solution.py:491
  79.6 0.9 shard_map.106
  80.5 5.9 %all-to-all-start.2 = ((f32[64,8,128]{2,1,0:T(8,128)}), f32[64,8,128]{2,1,0:T(8,128)S(1)}, u32[]{:S(2)}, u32[]{:S(2)}) async-start(f32[64,8,128]{2,1,0:T(8,128)} %get-tuple-element.79), calls=%async_computation.2 | async-start | bytes 524288 | tf_op jit(solution)/shard_map/all_to_all | solution.py:491
  86.4 0.1 copy.11.taps_ref
  86.5 0.3 shard_map.108.ogt_ref
  86.8 0.6 copy-done.22
  87.4 1.5 %shard_map.107 = (f32[2,128,128]{2,1,0:T(8,128)S(1)}, f32[2,128,128]{2,1,0:T(8,128)S(1)}) custom-call(f32[33,2]{1,0:T(8,128)S(1)} %copy.11.taps_ref, bf16[2,128,128]{2,1,0:T(8,128)(2,1)S(1)} %copy-done.12, f32[2,128,128]{2,1,0:T(8,128)S(1)} %copy-done.22, bf16[2,48,128]{2,1,0:T(8,128)(2,1)S(1)} %collective-permute-done.7.above_ref, ...), custom_call_target="tpu_custom_call" | custom-call | flops 1000000000 | bytes 2000000 | tf_op jit(solution)/shard_map/pallas_call | solution.py:475
  88.9 0.6 copy-done.31
  89.5 10.0 %all-to-all-done.2 = f32[64,8,128]{2,1,0:T(8,128)S(1)} async-done(((f32[64,8,128]{2,1,0:T(8,128)}), f32[64,8,128]{2,1,0:T(8,128)S(1)}, u32[]{:S(2)}, u32[]{:S(2)}) %all-to-all-start.2) | async-done | bytes 262176 | tf_op jit(solution)/shard_map/all_to_all | solution.py:491
  99.6 0.9 copy-done.7
  100.5 0.8 shard_map.109
  101.3 1.9 %collective-permute-start.10 = (bf16[256,128]{1,0:T(8,128)(2,1)S(1)}, bf16[256,128]{1,0:T(8,128)(2,1)S(1)}, u32[]{:S(2)}, u32[]{:S(2)}) collective-permute-start(bf16[256,128]{1,0:T(8,128)(2,1)S(1)} %get-tuple-element.96.ctx_ref.refs_0_), channel_id=1, source_target_pairs={{0,7},{1,0},{2,1},{3,2},{4,3},{5,4},{6,5},{7,6},{8,9},{9,10},{10,1... | collective-permute-start | bytes 196616 | tf_op jit(solution)/shard_map/ppermute | solution.py:499
  103.3 4.6 %collective-permute-start.9 = (bf16[256,128]{1,0:T(8,128)(2,1)S(1)}, bf16[256,128]{1,0:T(8,128)(2,1)S(1)}, u32[]{:S(2)}, u32[]{:S(2)}) collective-permute-start(bf16[256,128]{1,0:T(8,128)(2,1)S(1)} %get-tuple-element.96.ctx_ref.refs_0_), channel_id=1, source_target_pairs={{0,1},{1,2},{2,3},{3,4},{4,5},{5,6},{6,7},{7,0},{8,15},{9,8},{10,9... | collective-permute-start | bytes 196616 | tf_op jit(solution)/shard_map/ppermute | solution.py:499
  107.9 2.9 %shard_map.110 = bf16[64,48,128]{2,1,0:T(8,128)(2,1)S(1)} custom-call(f32[8,128]{1,0:T(8,128)S(1)} %get-tuple-element.97.log_ref, f32[2,128,256]{2,1,0:T(8,128)S(1)} %copy-done.3, f32[2,128,256]{2,1,0:T(8,128)S(1)} %copy-done.15, f32[2,128,128]{2,1,0:T(8,128)S(1)} %copy-done.23, f32[4,128,128]{2,1,0:T(8,128)S(1)} %copy-done.8, ...), custom_call_target="tpu_custom_call" | custom-call | flops 1000000000 | bytes 2000000 | tf_op jit(solution)/shard_map/pallas_call | solution.py:475
  110.8 0.9 copy-done.5
  111.7 0.0 collective-permute-done.10.refs_2_
  111.7 0.0 collective-permute-done.9.refs_1_
  111.7 4.8 %all-to-all-start.3 = ((bf16[64,48,128]{2,1,0:T(8,128)(2,1)}), bf16[64,48,128]{2,1,0:T(8,128)(2,1)S(1)}, u32[]{:S(2)}, u32[]{:S(2)}) async-start(bf16[64,48,128]{2,1,0:T(8,128)(2,1)} %copy-done.5), calls=%async_computation.3 | async-start | bytes 1572864 | tf_op jit(solution)/shard_map/all_to_all | solution.py:491
  116.6 5.2 %collective-permute-start.12 = (bf16[512,128]{1,0:T(8,128)(2,1)S(1)}, bf16[512,128]{1,0:T(8,128)(2,1)S(1)}, u32[]{:S(2)}, u32[]{:S(2)}) collective-permute-start(bf16[512,128]{1,0:T(8,128)(2,1)S(1)} %pad_maximum_fusion.1), channel_id=1, source_target_pairs={{0,5},{1,6},{2,7},{3,0},{4,1},{5,2},{6,3},{7,4},{8,11},{9,12},{10,... | collective-permute-start | bytes 393224 | tf_op jit(solution)/shard_map/ppermute | solution.py:499
  121.9 0.0 copy-start.24
  121.9 3.5 %collective-permute-start.11 = (bf16[768,128]{1,0:T(8,128)(2,1)S(1)}, bf16[768,128]{1,0:T(8,128)(2,1)S(1)}, u32[]{:S(2)}, u32[]{:S(2)}) collective-permute-start(bf16[768,128]{1,0:T(8,128)(2,1)S(1)} %pad_maximum_fusion), channel_id=1, source_target_pairs={{0,3},{1,4},{2,5},{3,6},{4,7},{5,0},{6,1},{7,2},{8,13},{9,14},{10,... | collective-permute-start | bytes 589832 | tf_op jit(solution)/shard_map/ppermute | solution.py:499
  125.5 4.9 %shard_map.112.own_ref = f32[8,128]{1,0:T(8,128)S(1)} custom-call(f32[2,128,128]{2,1,0:T(8,128)S(1)} %copy-done.18, f32[2,128,128]{2,1,0:T(8,128)S(1)} %copy-done.20, f32[2,128,128]{2,1,0:T(8,128)S(1)} %copy-done.26, f32[2,128,128]{2,1,0:T(8,128)S(1)} %copy-done.28), custom_call_target="tpu_custom_call" | custom-call | flops 5000000000 | bytes 2000000 | tf_op jit(solution)/shard_map/pallas_call | solution.py:475
  130.4 0.0 copy-start.13
  130.4 3.1 %shard_map.113 = (f32[2,128,128]{2,1,0:T(8,128)S(1)}, f32[2,128,128]{2,1,0:T(8,128)S(1)}, bf16[2,128,128]{2,1,0:T(8,128)(2,1)}) custom-call(f32[8,128]{1,0:T(8,128)S(1)} %get-tuple-element.97.log_ref, f32[2,128,256]{2,1,0:T(8,128)S(1)} %copy-done.4, f32[2,128,256]{2,1,0:T(8,128)S(1)} %copy-done.16, f32[2,128,128]{2,1,0:T(8,128)S(1)} %copy-done.24, ...), custom_call_target="tpu_custom_call" | custom-call | flops 1000000000 | bytes 2000000 | tf_op jit(solution)/shard_map/pallas_call | solution.py:475
  133.5 0.0 collective-permute-done.12.refs_4_
  133.5 0.5 collective-permute-done.11.refs_3_
  134.0 1.1 shard_map.111
  135.1 4.2 %all-to-all-done.3.got_ref = bf16[64,48,128]{2,1,0:T(8,128)(2,1)S(1)} async-done(((bf16[64,48,128]{2,1,0:T(8,128)(2,1)}), bf16[64,48,128]{2,1,0:T(8,128)(2,1)S(1)}, u32[]{:S(2)}, u32[]{:S(2)}) %all-to-all-start.3) | async-done | bytes 786464 | tf_op jit(solution)/shard_map/all_to_all | solution.py:491
  139.3 0.8 shard_map.114
  (57 shorter events, 0.1 us)
Async XLA Ops:
  4.5 31.5 %collective-permute-start.1 = (bf16[640,256]{1,0:T(8,128)(2,1)}, bf16[640,256]{1,0:T(8,128)(2,1)S(1)}, u32[]{:S(2)}, u32[]{:S(2)}) collective-permute-start(bf16[640,256]{1,0:T(8,128)(2,1)} %get-tuple-element.62), channel_id=1, source_target_pairs={{0,2},{1,3},{2,4},{3,5},{4,6},{5,7},{6,0},{7,1},{8,14},{9,15},{10,... | collective-permute-start | bytes 983048 | tf_op jit(solution)/shard_map/ppermute | solution.py:499
  11.2 22.0 %collective-permute-start.4 = (bf16[512,256]{1,0:T(8,128)(2,1)}, bf16[512,256]{1,0:T(8,128)(2,1)S(1)}, u32[]{:S(2)}, u32[]{:S(2)}) collective-permute-start(bf16[512,256]{1,0:T(8,128)(2,1)} %get-tuple-element.63), channel_id=1, source_target_pairs={{0,6},{1,7},{2,0},{3,1},{4,2},{5,3},{6,4},{7,5},{8,10},{9,11},{10,... | collective-permute-start | bytes 786440 | tf_op jit(solution)/shard_map/ppermute | solution.py:499
  13.1 31.2 %all-to-all-start = ((f32[64,8,128]{2,1,0:T(8,128)}), f32[64,8,128]{2,1,0:T(8,128)S(1)}, u32[]{:S(2)}, u32[]{:S(2)}) async-start(f32[64,8,128]{2,1,0:T(8,128)} %shard_map.101), calls=%async_computation | async-start | bytes 524288 | tf_op jit(solution)/shard_map/all_to_all | solution.py:491
  27.4 18.8 %collective-permute-start = (bf16[384,256]{1,0:T(8,128)(2,1)}, bf16[384,256]{1,0:T(8,128)(2,1)S(1)}, u32[]{:S(2)}, u32[]{:S(2)}) collective-permute-start(bf16[384,256]{1,0:T(8,128)(2,1)} %get-tuple-element.61), channel_id=1, source_target_pairs={{0,1},{1,2},{2,3},{3,4},{4,5},{5,6},{6,7},{7,0},{8,15},{9,8},{10,9... | collective-permute-start | bytes 589832 | tf_op jit(solution)/shard_map/ppermute | solution.py:499
  31.3 14.9 %collective-permute-start.6 = (bf16[384,256]{1,0:T(8,128)(2,1)}, bf16[384,256]{1,0:T(8,128)(2,1)S(1)}, u32[]{:S(2)}, u32[]{:S(2)}) collective-permute-start(bf16[384,256]{1,0:T(8,128)(2,1)} %get-tuple-element.64), channel_id=1, source_target_pairs={{0,7},{1,0},{2,1},{3,2},{4,3},{5,4},{6,5},{7,6},{8,9},{9,10},{10,1... | collective-permute-start | bytes 589832 | tf_op jit(solution)/shard_map/ppermute | solution.py:499
  33.2 11.1 %copy-start.10 = (bf16[2,128,128]{2,1,0:T(8,128)(2,1)S(1)}, bf16[2,128,128]{2,1,0:T(8,128)(2,1)}, u32[]{:S(2)}) copy-start(bf16[2,128,128]{2,1,0:T(8,128)(2,1)} %q_ref.5) | copy-start | bytes 196612
  33.2 11.1 %copy-start.11 = (bf16[2,128,128]{2,1,0:T(8,128)(2,1)S(1)}, bf16[2,128,128]{2,1,0:T(8,128)(2,1)}, u32[]{:S(2)}) copy-start(bf16[2,128,128]{2,1,0:T(8,128)(2,1)} %k_ref.5) | copy-start | bytes 196612
  33.2 11.1 %copy-start.12 = (bf16[2,128,128]{2,1,0:T(8,128)(2,1)S(1)}, bf16[2,128,128]{2,1,0:T(8,128)(2,1)}, u32[]{:S(2)}) copy-start(bf16[2,128,128]{2,1,0:T(8,128)(2,1)} %v_ref.7) | copy-start | bytes 196612
  33.2 16.0 %copy-start = (bf16[128,2048]{1,0:T(8,128)(2,1)S(1)}, bf16[128,2048]{1,0:T(8,128)(2,1)}, u32[]{:S(2)}) copy-start(bf16[128,2048]{1,0:T(8,128)(2,1)} %refs_8_.1) | copy-start | bytes 1572868
  33.3 12.9 %collective-permute-start.5 = (bf16[384,256]{1,0:T(8,128)(2,1)S(1)}, bf16[384,256]{1,0:T(8,128)(2,1)S(1)}, u32[]{:S(2)}, u32[]{:S(2)}) collective-permute-start(bf16[384,256]{1,0:T(8,128)(2,1)S(1)} %slice.14), channel_id=1, source_target_pairs={{0,7},{1,0},{2,1},{3,2},{4,3},{5,4},{6,5},{7,6},{8,9},{9,10},{10,1... | collective-permute-start | bytes 589832 | tf_op jit(solution)/shard_map/ppermute | solution.py:499
  36.7 11.0 %collective-permute-start.3 = (bf16[384,256]{1,0:T(8,128)(2,1)}, bf16[384,256]{1,0:T(8,128)(2,1)S(1)}, u32[]{:S(2)}, u32[]{:S(2)}) collective-permute-start(bf16[384,256]{1,0:T(8,128)(2,1)} %get-tuple-element.115), channel_id=1, source_target_pairs={{0,2},{1,3},{2,4},{3,5},{4,6},{5,7},{6,0},{7,1},{8,14},{9,15},{10,... | collective-permute-start | bytes 589832 | tf_op jit(solution)/shard_map/ppermute | solution.py:499
  41.8 7.5 %collective-permute-start.2 = (bf16[384,256]{1,0:T(8,128)(2,1)S(1)}, bf16[384,256]{1,0:T(8,128)(2,1)S(1)}, u32[]{:S(2)}, u32[]{:S(2)}) collective-permute-start(bf16[384,256]{1,0:T(8,128)(2,1)S(1)} %get-tuple-element.116), channel_id=1, source_target_pairs={{0,1},{1,2},{2,3},{3,4},{4,5},{5,6},{6,7},{7,0},{8,15},{9,8},{10,9... | collective-permute-start | bytes 589832 | tf_op jit(solution)/shard_map/ppermute | solution.py:499
  44.3 5.0 %copy-start.1 = (bf16[2,128,256]{2,1,0:T(8,128)(2,1)S(1)}, bf16[2,128,256]{2,1,0:T(8,128)(2,1)}, u32[]{:S(2)}) copy-start(bf16[2,128,256]{2,1,0:T(8,128)(2,1)} %param.11) | copy-start | bytes 393220
  45.4 0.7 copy-start.14
  46.2 4.7 %copy-start.2 = (f32[2,128,256]{2,1,0:T(8,128)}, f32[2,128,256]{2,1,0:T(8,128)S(1)}, u32[]{:S(2)}) copy-start(f32[2,128,256]{2,1,0:T(8,128)S(1)} %get-tuple-element.66.refs_10_.t_ref) | copy-start | bytes 786436
  46.2 23.8 %copy-start.17 = (f32[2,128,128]{2,1,0:T(8,128)}, f32[2,128,128]{2,1,0:T(8,128)S(1)}, u32[]{:S(2)}) copy-start(f32[2,128,128]{2,1,0:T(8,128)S(1)} %get-tuple-element.75.qm_ref) | copy-start | bytes 393220
  46.2 23.8 %copy-start.19 = (f32[2,128,128]{2,1,0:T(8,128)}, f32[2,128,128]{2,1,0:T(8,128)S(1)}, u32[]{:S(2)}) copy-start(f32[2,128,128]{2,1,0:T(8,128)S(1)} %get-tuple-element.76.km_ref) | copy-start | bytes 393220
  50.9 0.7 copy-start.21
  51.5 28.1 %all-to-all-start.1 = ((f32[64,3,4,128]{3,2,1,0:T(4,128)}), f32[64,3,4,128]{3,2,1,0:T(4,128)S(1)}, u32[]{:S(2)}, u32[]{:S(2)}) async-start(f32[64,3,4,128]{3,2,1,0:T(4,128)} %bitcast.2), calls=%async_computation.1 | async-start | bytes 786432 | tf_op jit(solution)/shard_map/all_to_all | solution.py:491
  64.5 8.4 %collective-permute-start.7 = (bf16[2,48,128]{2,1,0:T(8,128)(2,1)S(1)}, bf16[2,48,128]{2,1,0:T(8,128)(2,1)S(1)}, u32[]{:S(2)}, u32[]{:S(2)}) collective-permute-start(bf16[2,48,128]{2,1,0:T(8,128)(2,1)S(1)} %get-tuple-element.73), channel_id=1, source_target_pairs={{0,8},{8,16},{16,24},{24,32},{32,40},{40,48},{48,56},{56,64},{64,7... | collective-permute-start | bytes 73736 | tf_op jit(solution)/shard_map/ppermute | solution.py:563
  68.0 5.7 %collective-permute-start.8 = (bf16[2,48,128]{2,1,0:T(8,128)(2,1)S(1)}, bf16[2,48,128]{2,1,0:T(8,128)(2,1)S(1)}, u32[]{:S(2)}, u32[]{:S(2)}) collective-permute-start(bf16[2,48,128]{2,1,0:T(8,128)(2,1)S(1)} %get-tuple-element.74), channel_id=1, source_target_pairs={{8,0},{16,8},{24,16},{32,24},{40,32},{48,40},{56,48},{64,56},{72,6... | collective-permute-start | bytes 73736 | tf_op jit(solution)/shard_map/ppermute | solution.py:564
  72.1 0.7 copy-start.6
  73.8 6.7 %copy-start.29 = (bf16[2,48,128]{2,1,0:T(8,128)(2,1)}, bf16[2,48,128]{2,1,0:T(8,128)(2,1)S(1)}, u32[]{:S(2)}) copy-start(bf16[2,48,128]{2,1,0:T(8,128)(2,1)S(1)} %collective-permute-done.8.below_ref) | copy-start | bytes 73732
  80.5 5.9 %copy-start.33 = (f32[33,2]{0,1:T(2,128)S(1)}, f32[33,2]{0,1:T(2,128)}, u32[]{:S(2)}) copy-start(f32[33,2]{0,1:T(2,128)} %param.9) | copy-start | bytes 796
  80.5 19.1 %all-to-all-start.2 = ((f32[64,8,128]{2,1,0:T(8,128)}), f32[64,8,128]{2,1,0:T(8,128)S(1)}, u32[]{:S(2)}, u32[]{:S(2)}) async-start(f32[64,8,128]{2,1,0:T(8,128)} %get-tuple-element.79), calls=%async_computation.2 | async-start | bytes 524288 | tf_op jit(solution)/shard_map/all_to_all | solution.py:491
  86.5 0.9 copy-start.22
  86.5 0.9 copy-start.30
  87.4 12.1 %copy-start.3 = (f32[2,128,256]{2,1,0:T(8,128)S(1)}, f32[2,128,256]{2,1,0:T(8,128)}, u32[]{:S(2)}) copy-start(f32[2,128,256]{2,1,0:T(8,128)} %copy-done.2) | copy-start | bytes 786436
  88.9 0.6 copy-start.31
  99.6 1.0 copy-start.7
  100.5 7.3 %copy-start.8 = (f32[4,128,128]{2,1,0:T(8,128)S(1)}, f32[4,128,128]{2,1,0:T(8,128)}, u32[]{:S(2)}) copy-start(f32[4,128,128]{2,1,0:T(8,128)} %copy-done.6) | copy-start | bytes 786436
  100.5 7.3 %copy-start.15 = (f32[2,128,256]{2,1,0:T(8,128)S(1)}, f32[2,128,256]{2,1,0:T(8,128)}, u32[]{:S(2)}) copy-start(f32[2,128,256]{2,1,0:T(8,128)} %copy-done.14) | copy-start | bytes 786436
  100.5 7.4 %copy-start.23 = (f32[2,128,128]{2,1,0:T(8,128)S(1)}, f32[2,128,128]{2,1,0:T(8,128)}, u32[]{:S(2)}) copy-start(f32[2,128,128]{2,1,0:T(8,128)} %copy-done.21) | copy-start | bytes 393220
  101.3 9.4 %copy-start.25 = (f32[2,128,128]{2,1,0:T(8,128)}, f32[2,128,128]{2,1,0:T(8,128)S(1)}, u32[]{:S(2)}) copy-start(f32[2,128,128]{2,1,0:T(8,128)S(1)} %get-tuple-element.100.mixed_ref) | copy-start | bytes 393220
  101.3 9.4 %copy-start.27 = (f32[2,128,128]{2,1,0:T(8,128)}, f32[2,128,128]{2,1,0:T(8,128)S(1)}, u32[]{:S(2)}) copy-start(f32[2,128,128]{2,1,0:T(8,128)S(1)} %get-tuple-element.107.mix_ref) | copy-start | bytes 393220
  101.3 10.4 %collective-permute-start.10 = (bf16[256,128]{1,0:T(8,128)(2,1)S(1)}, bf16[256,128]{1,0:T(8,128)(2,1)S(1)}, u32[]{:S(2)}, u32[]{:S(2)}) collective-permute-start(bf16[256,128]{1,0:T(8,128)(2,1)S(1)} %get-tuple-element.96.ctx_ref.refs_0_), channel_id=1, source_target_pairs={{0,7},{1,0},{2,1},{3,2},{4,3},{5,4},{6,5},{7,6},{8,9},{9,10},{10,1... | collective-permute-start | bytes 196616 | tf_op jit(solution)/shard_map/ppermute | solution.py:499
  103.3 8.4 %collective-permute-start.9 = (bf16[256,128]{1,0:T(8,128)(2,1)S(1)}, bf16[256,128]{1,0:T(8,128)(2,1)S(1)}, u32[]{:S(2)}, u32[]{:S(2)}) collective-permute-start(bf16[256,128]{1,0:T(8,128)(2,1)S(1)} %get-tuple-element.96.ctx_ref.refs_0_), channel_id=1, source_target_pairs={{0,1},{1,2},{2,3},{3,4},{4,5},{5,6},{6,7},{7,0},{8,15},{9,8},{10,9... | collective-permute-start | bytes 196616 | tf_op jit(solution)/shard_map/ppermute | solution.py:499
  110.8 0.9 copy-start.5
  111.7 27.6 %all-to-all-start.3 = ((bf16[64,48,128]{2,1,0:T(8,128)(2,1)}), bf16[64,48,128]{2,1,0:T(8,128)(2,1)S(1)}, u32[]{:S(2)}, u32[]{:S(2)}) async-start(bf16[64,48,128]{2,1,0:T(8,128)(2,1)} %copy-done.5), calls=%async_computation.3 | async-start | bytes 1572864 | tf_op jit(solution)/shard_map/all_to_all | solution.py:491
  116.5 8.9 %copy-start.28 = (f32[2,128,128]{2,1,0:T(8,128)S(1)}, f32[2,128,128]{2,1,0:T(8,128)}, u32[]{:S(2)}) copy-start(f32[2,128,128]{2,1,0:T(8,128)} %copy-done.27) | copy-start | bytes 393220
  116.6 8.9 %copy-start.18 = (f32[2,128,128]{2,1,0:T(8,128)S(1)}, f32[2,128,128]{2,1,0:T(8,128)}, u32[]{:S(2)}) copy-start(f32[2,128,128]{2,1,0:T(8,128)} %copy-done.17) | copy-start | bytes 393220
  116.6 8.9 %copy-start.20 = (f32[2,128,128]{2,1,0:T(8,128)S(1)}, f32[2,128,128]{2,1,0:T(8,128)}, u32[]{:S(2)}) copy-start(f32[2,128,128]{2,1,0:T(8,128)} %copy-done.19) | copy-start | bytes 393220
  116.6 8.9 %copy-start.26 = (f32[2,128,128]{2,1,0:T(8,128)S(1)}, f32[2,128,128]{2,1,0:T(8,128)}, u32[]{:S(2)}) copy-start(f32[2,128,128]{2,1,0:T(8,128)} %copy-done.25) | copy-start | bytes 393220
  116.6 16.9 %collective-permute-start.12 = (bf16[512,128]{1,0:T(8,128)(2,1)S(1)}, bf16[512,128]{1,0:T(8,128)(2,1)S(1)}, u32[]{:S(2)}, u32[]{:S(2)}) collective-permute-start(bf16[512,128]{1,0:T(8,128)(2,1)S(1)} %pad_maximum_fusion.1), channel_id=1, source_target_pairs={{0,5},{1,6},{2,7},{3,0},{4,1},{5,2},{6,3},{7,4},{8,11},{9,12},{10,... | collective-permute-start | bytes 393224 | tf_op jit(solution)/shard_map/ppermute | solution.py:499
  121.8 8.5 %copy-start.4 = (f32[2,128,256]{2,1,0:T(8,128)S(1)}, f32[2,128,256]{2,1,0:T(8,128)}, u32[]{:S(2)}) copy-start(f32[2,128,256]{2,1,0:T(8,128)} %copy-done.2) | copy-start | bytes 786436
  121.8 8.5 %copy-start.9 = (f32[4,128,128]{2,1,0:T(8,128)S(1)}, f32[4,128,128]{2,1,0:T(8,128)}, u32[]{:S(2)}) copy-start(f32[4,128,128]{2,1,0:T(8,128)} %copy-done.6) | copy-start | bytes 786436
  121.9 8.5 %copy-start.16 = (f32[2,128,256]{2,1,0:T(8,128)S(1)}, f32[2,128,256]{2,1,0:T(8,128)}, u32[]{:S(2)}) copy-start(f32[2,128,256]{2,1,0:T(8,128)} %copy-done.14) | copy-start | bytes 786436
  121.9 8.5 %copy-start.24 = (f32[2,128,128]{2,1,0:T(8,128)S(1)}, f32[2,128,128]{2,1,0:T(8,128)}, u32[]{:S(2)}) copy-start(f32[2,128,128]{2,1,0:T(8,128)} %copy-done.21) | copy-start | bytes 393220
  121.9 8.5 %copy-start.32 = (f32[2,128,128]{2,1,0:T(8,128)S(1)}, f32[2,128,128]{2,1,0:T(8,128)}, u32[]{:S(2)}) copy-start(f32[2,128,128]{2,1,0:T(8,128)} %copy-done.31) | copy-start | bytes 393220
  121.9 12.1 %collective-permute-start.11 = (bf16[768,128]{1,0:T(8,128)(2,1)S(1)}, bf16[768,128]{1,0:T(8,128)(2,1)S(1)}, u32[]{:S(2)}, u32[]{:S(2)}) collective-permute-start(bf16[768,128]{1,0:T(8,128)(2,1)S(1)} %pad_maximum_fusion), channel_id=1, source_target_pairs={{0,3},{1,4},{2,5},{3,6},{4,7},{5,0},{6,1},{7,2},{8,13},{9,14},{10,... | collective-permute-start | bytes 589832 | tf_op jit(solution)/shard_map/ppermute | solution.py:499
  130.4 3.7 %copy-start.13 = (bf16[128,256]{1,0:T(8,128)(2,1)S(1)}, bf16[128,256]{1,0:T(8,128)(2,1)}, u32[]{:S(2)}) copy-start(bf16[128,256]{1,0:T(8,128)(2,1)} %get-tuple-element.105.refs_5_) | copy-start | bytes 196612
